TPU v7x, 256 devices: a whole 4x4x8 slice. The times are simulated.
256 devices in a mesh: ctx: 16 (over z, core), ch: 4 (over x), dp: 4 (over y).
Axes of the slice: x: 4, y: 4, z: 8, core: 2. Of those that a mesh axis runs over, the one named last changes fastest.
Arguments:
- query_rows: bfloat16 [4, 2048, 8192], P('dp', 'ctx', 'ch'), may hold values from -6 to 6
- key_rows: bfloat16 [4, 2048, 8192], P('dp', 'ctx', 'ch'), may hold values from -6 to 6
- value_rows: bfloat16 [4, 2048, 8192], P('dp', 'ctx', 'ch'), may hold values from -6 to 6
- cotangent: bfloat16 [4, 2048, 8192], P('dp', 'ctx', 'ch'), may hold values from -6 to 6
- lengths: int32 [4, 8], P('dp'), may hold values from 1 to 1024, 2048 in all within a row
- short_filter: float32 [3, 7, 8192], P(None, None, 'ch'), may hold values from -2.5 to 2.5
- residue: float32 [8192, 16], P('ch'), may hold values from -1.5 to 1.5
- decay_rate: float32 [8192, 16], P('ch'), may hold values from 0.00024414062 to 0.0625
- skip_gain: float32 [8192], P('ch'), may hold values from 0.5 to 1.5
Outputs:
- block_out: bfloat16 [4, 2048, 8192], P('dp', 'ctx', 'ch')
- grad_query: bfloat16 [4, 2048, 8192], P('dp', 'ctx', 'ch')
- grad_key: bfloat16 [4, 2048, 8192], P('dp', 'ctx', 'ch')
- grad_value: bfloat16 [4, 2048, 8192], P('dp', 'ctx', 'ch')
- grad_short: float32 [3, 7, 8192], P(None, None, 'ch')
- grad_residue: float32 [8192, 16], P('ch')
- grad_skip: float32 [8192], P('ch')
Inputs may be any that keep to these rules, and one draw needn't show every extreme that they name: Each row of lengths sums to 2048, and its longest document holds exactly 1024 positions.
All inputs are finite; a program needn't handle non-finite values.
Results may differ from a plain program's by a relative error of at most 0.0011.
Values may be sent and summed in bfloat16 or wider, within the bound.
No kernel may reach another device: no remote copies, remote signals or barrier semaphores. Data moves between devices by JAX's collectives and lax.ppermute only.
A program may use at most 128 MiB of HBM per device.

v0:
```python
import math

import jax
import jax.numpy as jnp
from jax import lax
from jax.sharding import PartitionSpec as P


def shifted(value, axis, steps):
    count = lax.axis_size(axis)
    leading, last = (max(0, -steps), min(count, count - steps))
    return lax.ppermute(value, axis, [(source, source + steps) for source in range(leading, last)])


def doc_index(positions, starts):
    return jnp.sum((positions[:, None] >= starts[None, :]).astype(jnp.int32), axis=1)


def decayed_total(values, kept_rows, offsets, decay_rate, block_rows):
    block_count = values.shape[0] // block_rows
    pieces = (
        values.reshape(block_count, block_rows, -1),
        kept_rows.reshape(block_count, block_rows),
        offsets.reshape(block_count, block_rows),
    )

    def absorb(running, block_piece):
        value_blk, kept_blk, offset_blk = block_piece
        factor = jnp.exp(-decay_rate[None] * offset_blk[:, None, None])
        return (
            running + jnp.sum(factor * (value_blk * kept_blk[:, None])[:, :, None], axis=0),
            None,
        )

    summed, unused = lax.scan(absorb, jnp.zeros(decay_rate.shape, jnp.float32), pieces)
    return summed


def per_device(
    query_rows,
    key_rows,
    value_rows,
    cotangent,
    lengths,
    short_filter,
    residue,
    decay_rate,
    skip_gain,
):
    row_count = query_rows.shape[1]
    channels = query_rows.shape[2]
    tap_count = short_filter.shape[1]
    halo_rows = tap_count - 1
    block_rows = math.gcd(row_count, 32)
    block_count = row_count // block_rows
    anchor = lax.axis_index("ctx") * row_count
    doc_lengths = lengths[0]
    starts = jnp.cumsum(doc_lengths) - doc_lengths
    local_index = jnp.arange(row_count, dtype=jnp.int32)
    doc_rows = doc_index(anchor + local_index, starts)
    doc_before = doc_index(jnp.reshape(anchor - 1, (1,)), starts)[0]
    doc_last = doc_rows[row_count - 1]
    stacked = jnp.stack([query_rows[0], key_rows[0], value_rows[0]])
    earlier_rows = shifted(stacked[:, row_count - halo_rows :, :], "ctx", 1)
    extended = jnp.concatenate([earlier_rows, stacked], axis=1).astype(jnp.float32)
    extended_docs = doc_index(
        anchor - halo_rows + jnp.arange(row_count + halo_rows, dtype=jnp.int32), starts
    )
    featured = jnp.zeros((3, row_count, channels), jnp.float32)
    tap_masks = []
    for tap_step in range(tap_count):
        window = extended[:, halo_rows - tap_step : halo_rows - tap_step + row_count]
        same_doc = (
            extended_docs[halo_rows - tap_step : halo_rows - tap_step + row_count] == doc_rows
        ).astype(jnp.float32)
        tap_masks.append(same_doc)
        featured = (
            featured + short_filter[:, tap_step, :][:, None, :] * window * same_doc[None, :, None]
        )
    query_feat, key_feat, value_feat = (featured[0], featured[1], featured[2])
    product = key_feat * value_feat
    mode_weight = residue * jnp.sqrt(decay_rate)
    upstream = cotangent[0].astype(jnp.float32)
    grad_filtered = upstream * query_feat
    reverse_offsets = (row_count - 1 - local_index).astype(jnp.float32)
    forward_offsets = local_index.astype(jnp.float32)
    local_end = decayed_total(
        product, (doc_rows == doc_last).astype(jnp.float32), reverse_offsets, decay_rate, block_rows
    )
    local_begin = decayed_total(
        grad_filtered,
        (doc_rows == doc_before).astype(jnp.float32),
        forward_offsets,
        decay_rate,
        block_rows,
    )
    passing = (doc_before == doc_last).astype(jnp.float32)
    through = passing * jnp.exp(-decay_rate * row_count)
    zero_state = jnp.zeros_like(decay_rate)

    def pass_down(step_index, incoming):
        return shifted(local_end + through * incoming, "ctx", 1)

    def pass_up(step_index, incoming):
        return shifted(local_begin + through * incoming, "ctx", -1)

    entering = lax.fori_loop(0, lax.axis_size("ctx") - 1, pass_down, zero_state)
    returning = lax.fori_loop(0, lax.axis_size("ctx") - 1, pass_up, zero_state)
    offsets = jnp.arange(block_rows, dtype=jnp.float32)
    growth = jnp.exp(decay_rate[None] * offsets[:, None, None])
    shrink = jnp.exp(-decay_rate[None] * offsets[:, None, None])
    step_decay = jnp.exp(-decay_rate)
    edge_decay = jnp.exp(-decay_rate[None] * (block_rows - offsets)[:, None, None])
    row_ids = jnp.arange(block_rows, dtype=jnp.int32)
    lower_tri = row_ids[None, :] <= row_ids[:, None]
    upper_tri = row_ids[None, :] >= row_ids[:, None]
    doc_blocks = doc_rows.reshape(block_count, block_rows)
    previous_docs = jnp.concatenate(
        [jnp.reshape(doc_before, (1,)), doc_blocks[:-1, block_rows - 1]]
    )
    upstream_blocks = grad_filtered.reshape(block_count, block_rows, channels)

    def forward_block(running, block_piece):
        state_in, weight_sum = running
        source_blk, upstream_blk, doc_blk, previous = block_piece
        same_doc = doc_blk[:, None] == doc_blk[None, :]
        lower_mask = (lower_tri & same_doc).astype(jnp.float32)
        lifted = (growth * source_blk[:, :, None]).reshape(block_rows, -1)
        summed = jnp.dot(lower_mask, lifted, precision=lax.Precision.HIGHEST).reshape(
            block_rows, channels, -1
        )
        open_rows = (doc_blk == previous).astype(jnp.float32)
        states = (
            shrink * summed + open_rows[:, None, None] * shrink * step_decay[None] * state_in[None]
        )
        result = jnp.sum(states * mode_weight[None], axis=2)
        weight_sum = weight_sum + jnp.sum(states * upstream_blk[:, :, None], axis=0)
        return ((states[block_rows - 1], weight_sum), result)

    (unused_state, weight_grad), conv_blocks = lax.scan(
        forward_block,
        (entering, zero_state),
        (
            product.reshape(block_count, block_rows, channels),
            upstream_blocks,
            doc_blocks,
            previous_docs,
        ),
    )
    filtered = conv_blocks.reshape(row_count, channels) + skip_gain[None, :] * product
    block_out = (query_feat * filtered).astype(jnp.bfloat16)
    grad_query_feat = upstream * filtered

    def backward_block(state_in, block_piece):
        upstream_blk, doc_blk, previous = block_piece
        same_doc = doc_blk[:, None] == doc_blk[None, :]
        upper_mask = (upper_tri & same_doc).astype(jnp.float32)
        lowered = (shrink * upstream_blk[:, :, None]).reshape(block_rows, -1)
        summed = jnp.dot(upper_mask, lowered, precision=lax.Precision.HIGHEST).reshape(
            block_rows, channels, -1
        )
        tail_rows = (doc_blk == doc_blk[block_rows - 1]).astype(jnp.float32)
        states = growth * summed + tail_rows[:, None, None] * edge_decay * state_in[None]
        result = jnp.sum(states * mode_weight[None], axis=2)
        state_out = states[0] * (doc_blk[0] == previous).astype(jnp.float32)
        return (state_out, result)

    unused_begin, back_blocks = lax.scan(
        backward_block, returning, (upstream_blocks, doc_blocks, previous_docs), reverse=True
    )
    grad_product = back_blocks.reshape(row_count, channels) + skip_gain[None, :] * grad_filtered
    grad_skip_part = jnp.sum(grad_filtered * product, axis=0)
    grad_features = jnp.stack([grad_query_feat, grad_product * value_feat, grad_product * key_feat])
    later_rows = shifted(grad_features[:, :halo_rows, :], "ctx", -1)
    reaching = jnp.concatenate([grad_features, later_rows], axis=1)
    reaching_docs = doc_index(anchor + jnp.arange(row_count + halo_rows, dtype=jnp.int32), starts)
    grad_inputs = jnp.zeros((3, row_count, channels), jnp.float32)
    tap_grads = []
    for tap_step in range(tap_count):
        ahead_rows = reaching[:, tap_step : tap_step + row_count]
        ahead_same = (reaching_docs[tap_step : tap_step + row_count] == doc_rows).astype(
            jnp.float32
        )
        grad_inputs = (
            grad_inputs
            + short_filter[:, tap_step, :][:, None, :] * ahead_rows * ahead_same[None, :, None]
        )
        window = extended[:, halo_rows - tap_step : halo_rows - tap_step + row_count]
        tap_grads.append(
            jnp.sum(grad_features * window * tap_masks[tap_step][None, :, None], axis=1)
        )
    grad_short_part = jnp.stack(tap_grads, axis=1)
    grad_short, grad_residue, grad_skip = lax.psum(
        (grad_short_part, weight_grad * jnp.sqrt(decay_rate), grad_skip_part), ("ctx", "dp")
    )
    rounded = grad_inputs.astype(jnp.bfloat16)
    return (
        block_out[None],
        rounded[0][None],
        rounded[1][None],
        rounded[2][None],
        grad_short,
        grad_residue,
        grad_skip,
    )


def solution(mesh):
    in_specs = (
        P("dp", "ctx", "ch"),
        P("dp", "ctx", "ch"),
        P("dp", "ctx", "ch"),
        P("dp", "ctx", "ch"),
        P("dp", None),
        P(None, None, "ch"),
        P("ch", None),
        P("ch", None),
        P("ch"),
    )
    out_specs = (
        P("dp", "ctx", "ch"),
        P("dp", "ctx", "ch"),
        P("dp", "ctx", "ch"),
        P("dp", "ctx", "ch"),
        P(None, None, "ch"),
        P("ch", None),
        P("ch"),
    )
    return jax.shard_map(
        per_device, mesh=mesh, in_specs=in_specs, out_specs=out_specs, check_vma=False
    )
```

profile of v0, /device:TPU:1, one launch (start us, length us, event | category | flops | bytes accessed | tf_op | source)
XLA Modules:
  0.0 890.3 jit_solution(12812909244574324545)
XLA Ops:
  10.7 4.9 collective-permute-start.2
  26.4 3.5 multiply_add_fusion.2
  33.3 20.1 %while.81 = (s32[]{:T(128)}, f32[2048,16]{0,1:T(8,128)}, f32[1,2048,16]{1,2,0:T(8,128)}, f32[4,32]{1,0:T(4,128)S(1)}, f32[4,32,2048]{2,1,0:T(8,128)}, /*index=5*/f32[4,32]{1,0:T(4,128)S(1)}, s32[]{:T(128)}, s32[]{:T(128)}) while((s32[]{:T(128)}, f32[2048,16]{0,1:T(8,128)}, f32[1,2048,16]{1,2,0:T(8,128)}, f32[4,32]{1,0:T(4,128)S(1)}, ...), condition=%wide.region_6.7_spmd.clone, body=%wide.region_4.6_spmd.clone.sunk | while | flops 3244035 | bytes 1442663 | solution.py:35
  34.4 2.3 multiply_reduce_fusion.17
  39.3 2.3 multiply_reduce_fusion.17
  44.3 2.3 multiply_reduce_fusion.17
  49.4 2.3 multiply_reduce_fusion.17
  54.0 122.3 %while.79 = (s32[]{:T(128)}, f32[2048,16]{0,1:T(8,128)}, f32[2048,16]{0,1:T(8,128)}, f32[2048,16]{0,1:T(8,128)}, s32[]{:T(128)}) while((s32[]{:T(128)}, f32[2048,16]{0,1:T(8,128)}, f32[2048,16]{0,1:T(8,128)}, f32[2048,16]{0,1:T(8,128)}, s32[]{:T(128)}) %tuple.223), condition=%wide.region_8.9_spmd, body=%wide.region_7.8_spmd.sunk | while | flops 65538 | bytes 1048677 | solution.py:107
  61.6 4.3 collective-permute-start
  70.0 4.3 collective-permute-start
  78.3 4.3 collective-permute-start
  86.6 4.3 collective-permute-start
  94.9 4.3 collective-permute-start
  103.2 4.3 collective-permute-start
  111.5 4.3 collective-permute-start
  119.8 4.3 collective-permute-start
  128.2 4.3 collective-permute-start
  136.5 4.3 collective-permute-start
  144.8 4.3 collective-permute-start
  153.1 4.3 collective-permute-start
  161.4 4.3 collective-permute-start
  169.7 4.3 collective-permute-start
  177.4 163.2 %while.82 = (s32[]{:T(128)}, f32[2048,16]{0,1:T(8,128)}, f32[2048,16]{0,1:T(8,128)}, f32[4,32,2048]{2,1,0:T(8,128)}, s32[4,32]{1,0:T(4,128)S(1)}, /*index=5*/f32...) while((s32[]{:T(128)}, f32[2048,16]{0,1:T(8,128)}, ...), condition=%wide.region_12.13_spmd.clone, body=%wide.region_9.12_spmd.clone.sunk | while | flops 415206464 | bytes 18220384 | solution.py:140
  182.6 11.3 %fusion.76 = f32[2048,16,32]{2,1,0:T(8,128)S(1)} fusion(f32[2048,16]{1,0:T(8,128)} %get-tuple-element.1295, f32[32,2048]{0,1:T(8,128)} %bitcast.157), kind=kLoop, calls=%fused_computation.19.clone.1 | loop fusion | flops 2097152 | bytes 4587520 | tf_op jit(solution)/shard_map/while/body/eval_jaxpr/dot_general | solution.py:129
  194.9 18.9 %multiply_reduce_fusion.18 = (f32[32,2048]{1,0:T(8,128)S(1)}, f32[2048,16]{0,1:T(8,128)}, f32[32,2048,16]{1,0,2:T(8,128)}) fusion(f32[2048,16]{0,1:T(8,128)S(1)} %copy-done.7, f32[32,2048]{1,0:T(8,128)S(1)} %dynamic-slice_bitcast_fusion.2, f32[2048,16]{0,1:T(8,128)} %get-tuple-element.1272, f32[2048,16]{0,1:T(8,128)S(1)} %copy-done.12, ...), kind=kOutput, calls=%fused_computation.26.clone.1 | convolution fusion | flops 413043712 | bytes 9568512 | tf_op jit(solution)/shard_map/while/body/eval_jaxpr/dot_general | solution.py:129
  223.4 11.3 %fusion.76 = f32[2048,16,32]{2,1,0:T(8,128)S(1)} fusion(f32[2048,16]{1,0:T(8,128)} %get-tuple-element.1295, f32[32,2048]{0,1:T(8,128)} %bitcast.157), kind=kLoop, calls=%fused_computation.19.clone.1 | loop fusion | flops 2097152 | bytes 4587520 | tf_op jit(solution)/shard_map/while/body/eval_jaxpr/dot_general | solution.py:129
  235.7 18.9 %multiply_reduce_fusion.18 = (f32[32,2048]{1,0:T(8,128)S(1)}, f32[2048,16]{0,1:T(8,128)}, f32[32,2048,16]{1,0,2:T(8,128)}) fusion(f32[2048,16]{0,1:T(8,128)S(1)} %copy-done.7, f32[32,2048]{1,0:T(8,128)S(1)} %dynamic-slice_bitcast_fusion.2, f32[2048,16]{0,1:T(8,128)} %get-tuple-element.1272, f32[2048,16]{0,1:T(8,128)S(1)} %copy-done.12, ...), kind=kOutput, calls=%fused_computation.26.clone.1 | convolution fusion | flops 413043712 | bytes 9568512 | tf_op jit(solution)/shard_map/while/body/eval_jaxpr/dot_general | solution.py:129
  264.2 11.3 %fusion.76 = f32[2048,16,32]{2,1,0:T(8,128)S(1)} fusion(f32[2048,16]{1,0:T(8,128)} %get-tuple-element.1295, f32[32,2048]{0,1:T(8,128)} %bitcast.157), kind=kLoop, calls=%fused_computation.19.clone.1 | loop fusion | flops 2097152 | bytes 4587520 | tf_op jit(solution)/shard_map/while/body/eval_jaxpr/dot_general | solution.py:129
  276.5 18.9 %multiply_reduce_fusion.18 = (f32[32,2048]{1,0:T(8,128)S(1)}, f32[2048,16]{0,1:T(8,128)}, f32[32,2048,16]{1,0,2:T(8,128)}) fusion(f32[2048,16]{0,1:T(8,128)S(1)} %copy-done.7, f32[32,2048]{1,0:T(8,128)S(1)} %dynamic-slice_bitcast_fusion.2, f32[2048,16]{0,1:T(8,128)} %get-tuple-element.1272, f32[2048,16]{0,1:T(8,128)S(1)} %copy-done.12, ...), kind=kOutput, calls=%fused_computation.26.clone.1 | convolution fusion | flops 413043712 | bytes 9568512 | tf_op jit(solution)/shard_map/while/body/eval_jaxpr/dot_general | solution.py:129
  305.0 11.3 %fusion.76 = f32[2048,16,32]{2,1,0:T(8,128)S(1)} fusion(f32[2048,16]{1,0:T(8,128)} %get-tuple-element.1295, f32[32,2048]{0,1:T(8,128)} %bitcast.157), kind=kLoop, calls=%fused_computation.19.clone.1 | loop fusion | flops 2097152 | bytes 4587520 | tf_op jit(solution)/shard_map/while/body/eval_jaxpr/dot_general | solution.py:129
  317.3 18.9 %multiply_reduce_fusion.18 = (f32[32,2048]{1,0:T(8,128)S(1)}, f32[2048,16]{0,1:T(8,128)}, f32[32,2048,16]{1,0,2:T(8,128)}) fusion(f32[2048,16]{0,1:T(8,128)S(1)} %copy-done.7, f32[32,2048]{1,0:T(8,128)S(1)} %dynamic-slice_bitcast_fusion.2, f32[2048,16]{0,1:T(8,128)} %get-tuple-element.1272, f32[2048,16]{0,1:T(8,128)S(1)} %copy-done.12, ...), kind=kOutput, calls=%fused_computation.26.clone.1 | convolution fusion | flops 413043712 | bytes 9568512 | tf_op jit(solution)/shard_map/while/body/eval_jaxpr/dot_general | solution.py:129
  340.6 20.0 %while.83 = (s32[]{:T(128)}, f32[2048,16]{0,1:T(8,128)}, f32[1,2048,16]{1,2,0:T(8,128)}, f32[4,32]{1,0:T(4,128)S(1)}, f32[4,32,2048]{2,1,0:T(8,128)}, /*index=5*/f32[4,32]{1,0:T(4,128)S(1)}, s32[]{:T(128)}, s32[]{:T(128)}) while((s32[]{:T(128)}, f32[2048,16]{0,1:T(8,128)}, f32[1,2048,16]{1,2,0:T(8,128)}, ...), condition=%wide.region_15.16_spmd.clone, body=%wide.region_13.15_spmd.clone.sunk | while | flops 3244035 | bytes 1442663 | solution.py:35
  341.7 2.3 multiply_reduce_fusion.19
  361.3 144.6 %while.80 = (s32[]{:T(128)}, f32[2048,16]{0,1:T(8,128)}, f32[2048,16]{0,1:T(8,128)}, f32[2048,16]{0,1:T(8,128)}, s32[]{:T(128)}) while((s32[]{:T(128)}, f32[2048,16]{0,1:T(8,128)}, f32[2048,16]{0,1:T(8,128)}, f32[2048,16]{0,1:T(8,128)}, s32[]{:T(128)}) %tuple.240), condition=%wide.region_17.18_spmd, body=%wide.region_16.17_spmd.sunk | while | flops 65538 | bytes 1048677 | solution.py:108
  364.9 6.1 collective-permute-done.1
  374.6 5.7 collective-permute-done.1
  384.0 6.6 collective-permute-done.1
  394.2 5.7 collective-permute-done.1
  403.6 6.6 collective-permute-done.1
  413.8 5.7 collective-permute-done.1
  423.2 6.6 collective-permute-done.1
  433.4 5.9 collective-permute-done.1
  442.9 5.9 collective-permute-done.1
  452.4 5.9 collective-permute-done.1
  462.0 5.9 collective-permute-done.1
  471.5 5.9 collective-permute-done.1
  481.0 5.9 collective-permute-done.1
  490.5 5.9 collective-permute-done.1
  500.0 5.9 collective-permute-done.1
  507.0 161.1 %while.84 = (s32[]{:T(128)}, f32[2048,16]{0,1:T(8,128)}, f32[4,32,2048]{2,1,0:T(8,128)}, s32[4,32]{1,0:T(4,128)S(1)}, f32[4,32,2048]{2,1,0:T(8,128)}, /*index=5*...) while((s32[]{:T(128)}, f32[2048,16]{0,1:T(8,128)}, ...), condition=%wide.region_20.21_spmd.clone.clone, body=%wide.region_18.20_spmd.clone.clone.sunk | while | flops 413109312 | bytes 17171840 | solution.py:168
  513.5 11.3 %fusion.79 = f32[2048,16,32]{2,1,0:T(8,128)S(1)} fusion(f32[2048,16]{1,0:T(8,128)} %copy.82, f32[32,2048]{0,1:T(8,128)} %bitcast.156), kind=kLoop, calls=%fused_computation.52.clone.1 | loop fusion | flops 2097152 | bytes 4587520 | tf_op jit(solution)/shard_map/while/body/eval_jaxpr/dot_general | solution.py:159
  524.9 17.8 %multiply_reduce_fusion.20 = (f32[32,2048]{1,0:T(8,128)S(1)}, f32[32,2048,16]{1,0,2:T(8,128)}) fusion(f32[2048,16]{0,1:T(8,128)S(1)} %copy-done.8, f32[2048,16]{0,1:T(8,128)} %get-tuple-element.1195, f32[32]{0:T(128)S(1)} %get-tuple-element.1215, f32[2048,16]{0,1:T(8,128)S(1)} %get-tuple-element.1213, f32[32]{0:T(128)S(1)} %compare_convert_fusion.22, ...), kind=kOutput, calls=%fused_computation.57.clone.1 | convolution fusion | flops 410979328 | bytes 9175424 | tf_op jit(solution)/shard_map/while/body/eval_jaxpr/dot_general | solution.py:159
  553.8 11.3 %fusion.79 = f32[2048,16,32]{2,1,0:T(8,128)S(1)} fusion(f32[2048,16]{1,0:T(8,128)} %copy.82, f32[32,2048]{0,1:T(8,128)} %bitcast.156), kind=kLoop, calls=%fused_computation.52.clone.1 | loop fusion | flops 2097152 | bytes 4587520 | tf_op jit(solution)/shard_map/while/body/eval_jaxpr/dot_general | solution.py:159
  565.1 17.8 %multiply_reduce_fusion.20 = (f32[32,2048]{1,0:T(8,128)S(1)}, f32[32,2048,16]{1,0,2:T(8,128)}) fusion(f32[2048,16]{0,1:T(8,128)S(1)} %copy-done.8, f32[2048,16]{0,1:T(8,128)} %get-tuple-element.1195, f32[32]{0:T(128)S(1)} %get-tuple-element.1215, f32[2048,16]{0,1:T(8,128)S(1)} %get-tuple-element.1213, f32[32]{0:T(128)S(1)} %compare_convert_fusion.22, ...), kind=kOutput, calls=%fused_computation.57.clone.1 | convolution fusion | flops 410979328 | bytes 9175424 | tf_op jit(solution)/shard_map/while/body/eval_jaxpr/dot_general | solution.py:159
  594.1 11.3 %fusion.79 = f32[2048,16,32]{2,1,0:T(8,128)S(1)} fusion(f32[2048,16]{1,0:T(8,128)} %copy.82, f32[32,2048]{0,1:T(8,128)} %bitcast.156), kind=kLoop, calls=%fused_computation.52.clone.1 | loop fusion | flops 2097152 | bytes 4587520 | tf_op jit(solution)/shard_map/while/body/eval_jaxpr/dot_general | solution.py:159
  605.4 17.8 %multiply_reduce_fusion.20 = (f32[32,2048]{1,0:T(8,128)S(1)}, f32[32,2048,16]{1,0,2:T(8,128)}) fusion(f32[2048,16]{0,1:T(8,128)S(1)} %copy-done.8, f32[2048,16]{0,1:T(8,128)} %get-tuple-element.1195, f32[32]{0:T(128)S(1)} %get-tuple-element.1215, f32[2048,16]{0,1:T(8,128)S(1)} %get-tuple-element.1213, f32[32]{0:T(128)S(1)} %compare_convert_fusion.22, ...), kind=kOutput, calls=%fused_computation.57.clone.1 | convolution fusion | flops 410979328 | bytes 9175424 | tf_op jit(solution)/shard_map/while/body/eval_jaxpr/dot_general | solution.py:159
  634.4 11.3 %fusion.79 = f32[2048,16,32]{2,1,0:T(8,128)S(1)} fusion(f32[2048,16]{1,0:T(8,128)} %copy.82, f32[32,2048]{0,1:T(8,128)} %bitcast.156), kind=kLoop, calls=%fused_computation.52.clone.1 | loop fusion | flops 2097152 | bytes 4587520 | tf_op jit(solution)/shard_map/while/body/eval_jaxpr/dot_general | solution.py:159
  645.7 17.8 %multiply_reduce_fusion.20 = (f32[32,2048]{1,0:T(8,128)S(1)}, f32[32,2048,16]{1,0,2:T(8,128)}) fusion(f32[2048,16]{0,1:T(8,128)S(1)} %copy-done.8, f32[2048,16]{0,1:T(8,128)} %get-tuple-element.1195, f32[32]{0:T(128)S(1)} %get-tuple-element.1215, f32[2048,16]{0,1:T(8,128)S(1)} %get-tuple-element.1213, f32[32]{0:T(128)S(1)} %compare_convert_fusion.22, ...), kind=kOutput, calls=%fused_computation.57.clone.1 | convolution fusion | flops 410979328 | bytes 9175424 | tf_op jit(solution)/shard_map/while/body/eval_jaxpr/dot_general | solution.py:159
  668.1 4.9 slice_multiply_fusion.7
  673.1 3.8 multiply_reduce_fusion.5
  681.4 124.5 %psum.23 = f32[2048]{0:T(1024)} all-reduce(f32[2048]{0:T(1024)S(1)} %get-tuple-element.790), channel_id=1, replica_groups=mesh['ctx'=16,'ch'=4,'dp'=4] {'ctx','dp'}, use_global_device_ids=true, to_apply=%region_32.33 | all-reduce | flops 2048 | bytes 16384 | tf_op jit(solution)/shard_map/psum | solution.py:193
  806.1 2.4 pad_maximum_fusion
  808.9 3.6 fusion.50
  813.7 66.5 %all-reduce.3.cloned.1.call-done = (f32[3,7,2048]{2,0,1:T(4,128)}, f32[2048,16]{0,1:T(8,128)}) async-done(((f32[3,7,2048]{2,0,1:T(4,128)}, f32[2048,16]{0,1:T(8,128)}), (f32[3,7,2048]{2,0,1:T(4,128)}, f32[2048,16]{0,1:T(8,128)})) %all-reduce.3.cloned.1.call-update) | async-done | bytes 303120 | tf_op jit(solution)/shard_map/psum | solution.py:193
  (347 shorter events, 254.1 us)
Async XLA Ops:
  7.2 8.5 copy-start.49
  7.2 12.7 %copy-start.31 = (f32[3,7,2048]{2,1,0:T(8,128)S(1)}, f32[3,7,2048]{2,1,0:T(8,128)}, u32[]{:S(2)}) copy-start(f32[3,7,2048]{2,1,0:T(8,128)} %param.26) | copy-start | bytes 516100
  7.2 12.9 %copy-start.9 = (f32[2048,16]{0,1:T(8,128)S(1)}, f32[2048,16]{0,1:T(8,128)}, u32[]{:S(2)}) copy-start(f32[2048,16]{0,1:T(8,128)} %param.28) | copy-start | bytes 393220
  7.2 15.1 %copy-start.32 = (f32[2048,16]{0,1:T(8,128)S(1)}, f32[2048,16]{0,1:T(8,128)}, u32[]{:S(2)}) copy-start(f32[2048,16]{0,1:T(8,128)} %param.27) | copy-start | bytes 393220
  7.2 873.0 %all-reduce.3.cloned.1.call-start = ((), (), s32[]{:S(2)}) async-start(), calls=%async_computation | async-start | bytes 720896 | tf_op jit(solution)/shard_map/psum | solution.py:193
  10.6 13.7 %copy-start.14 = (bf16[3,128,2048]{2,1,0:T(8,128)(2,1)}, bf16[3,128,2048]{2,1,0:T(8,128)(2,1)S(1)}, u32[]{:S(2)}) copy-start(bf16[3,128,2048]{2,1,0:T(8,128)(2,1)S(1)} %constant_dynamic-update-slice_fusion) | copy-start | bytes 4718596
  10.7 13.7 %collective-permute-start.2 = (bf16[3,6,2048]{2,1,0:T(8,128)(2,1)S(1)}, bf16[3,6,2048]{2,1,0:T(8,128)(2,1)}, u32[]{:S(2)}, u32[]{:S(2)}) collective-permute-start(bf16[3,6,2048]{2,1,0:T(8,128)(2,1)S(1)} %slice.231), channel_id=1, source_target_pairs={{0,16},{16,32},{32,48},{48,64},{64,80},{80,96},{96,112},{112,128},... | collective-permute-start | bytes 221192 | tf_op jit(solution)/shard_map/ppermute | solution.py:12
  20.1 6.2 copy-start.17
  22.2 7.7 copy-start.19
  22.2 7.7 copy-start.21
  22.2 7.7 copy-start.23
  22.2 7.7 copy-start.25
  22.3 7.7 copy-start.27
  22.3 7.7 copy-start.29
  26.3 5.3 copy-start.15
  53.4 124.1 %copy-start.50 = (s32[4]{0:T(128)S(1)}, s32[4]{0:T(128)}, u32[]{:S(2)}) copy-start(s32[4]{0:T(128)} %pad_add_fusion) | copy-start | bytes 52
  55.8 4.2 collective-permute-start
  61.6 6.6 collective-permute-start
  70.0 6.6 collective-permute-start
  78.3 6.6 collective-permute-start
  86.6 6.6 collective-permute-start
  94.9 6.6 collective-permute-start
  103.2 6.6 collective-permute-start
  111.5 6.6 collective-permute-start
  119.8 6.6 collective-permute-start
  128.2 6.6 collective-permute-start
  136.5 6.6 collective-permute-start
  144.8 6.6 collective-permute-start
  153.1 6.6 collective-permute-start
  161.4 6.6 collective-permute-start
  169.7 6.6 collective-permute-start
  182.6 12.3 %copy-start.7 = (f32[2048,16]{0,1:T(8,128)S(1)}, f32[2048,16]{0,1:T(8,128)}, u32[]{:S(2)}) copy-start(f32[2048,16]{0,1:T(8,128)} %get-tuple-element.1294) | copy-start | bytes 393220 | tf_op jit(solution)/shard_map/while
  182.6 12.3 %copy-start.12 = (f32[2048,16]{0,1:T(8,128)S(1)}, f32[2048,16]{0,1:T(8,128)}, u32[]{:S(2)}) copy-start(f32[2048,16]{0,1:T(8,128)} %get-tuple-element.1292) | copy-start | bytes 393220 | tf_op jit(solution)/shard_map/while
  223.4 12.3 %copy-start.7 = (f32[2048,16]{0,1:T(8,128)S(1)}, f32[2048,16]{0,1:T(8,128)}, u32[]{:S(2)}) copy-start(f32[2048,16]{0,1:T(8,128)} %get-tuple-element.1294) | copy-start | bytes 393220 | tf_op jit(solution)/shard_map/while
  223.4 12.3 %copy-start.12 = (f32[2048,16]{0,1:T(8,128)S(1)}, f32[2048,16]{0,1:T(8,128)}, u32[]{:S(2)}) copy-start(f32[2048,16]{0,1:T(8,128)} %get-tuple-element.1292) | copy-start | bytes 393220 | tf_op jit(solution)/shard_map/while
  264.2 12.3 %copy-start.7 = (f32[2048,16]{0,1:T(8,128)S(1)}, f32[2048,16]{0,1:T(8,128)}, u32[]{:S(2)}) copy-start(f32[2048,16]{0,1:T(8,128)} %get-tuple-element.1294) | copy-start | bytes 393220 | tf_op jit(solution)/shard_map/while
  264.2 12.3 %copy-start.12 = (f32[2048,16]{0,1:T(8,128)S(1)}, f32[2048,16]{0,1:T(8,128)}, u32[]{:S(2)}) copy-start(f32[2048,16]{0,1:T(8,128)} %get-tuple-element.1292) | copy-start | bytes 393220 | tf_op jit(solution)/shard_map/while
  305.0 12.3 %copy-start.7 = (f32[2048,16]{0,1:T(8,128)S(1)}, f32[2048,16]{0,1:T(8,128)}, u32[]{:S(2)}) copy-start(f32[2048,16]{0,1:T(8,128)} %get-tuple-element.1294) | copy-start | bytes 393220 | tf_op jit(solution)/shard_map/while
  305.0 12.3 %copy-start.12 = (f32[2048,16]{0,1:T(8,128)S(1)}, f32[2048,16]{0,1:T(8,128)}, u32[]{:S(2)}) copy-start(f32[2048,16]{0,1:T(8,128)} %get-tuple-element.1292) | copy-start | bytes 393220 | tf_op jit(solution)/shard_map/while
  363.0 8.0 collective-permute-start.1
  372.7 7.7 collective-permute-start.1
  382.1 8.5 collective-permute-start.1
  392.3 7.7 collective-permute-start.1
  401.7 8.5 collective-permute-start.1
  411.9 7.7 collective-permute-start.1
  421.3 8.5 collective-permute-start.1
  431.5 7.8 collective-permute-start.1
  441.0 7.8 collective-permute-start.1
  450.5 7.8 collective-permute-start.1
  460.0 7.8 collective-permute-start.1
  469.5 7.8 collective-permute-start.1
  479.1 7.8 collective-permute-start.1
  488.6 7.8 collective-permute-start.1
  498.1 7.8 collective-permute-start.1
  507.0 161.1 %copy-start.33 = (f32[2048]{0:T(1024)S(1)}, f32[2048]{0:T(1024)}, u32[]{:S(2)}) copy-start(f32[2048]{0:T(1024)} %param.29) | copy-start | bytes 24580
  513.5 11.3 %copy-start.8 = (f32[2048,16]{0,1:T(8,128)S(1)}, f32[2048,16]{0,1:T(8,128)}, u32[]{:S(2)}) copy-start(f32[2048,16]{0,1:T(8,128)} %get-tuple-element.1212) | copy-start | bytes 393220 | tf_op jit(solution)/shard_map/while
  513.5 11.3 %copy-start.10 = (f32[2048,16]{0,1:T(8,128)S(1)}, f32[2048,16]{0,1:T(8,128)}, u32[]{:S(2)}) copy-start(f32[2048,16]{0,1:T(8,128)} %get-tuple-element.1214) | copy-start | bytes 393220 | tf_op jit(solution)/shard_map/while
  553.8 11.3 %copy-start.8 = (f32[2048,16]{0,1:T(8,128)S(1)}, f32[2048,16]{0,1:T(8,128)}, u32[]{:S(2)}) copy-start(f32[2048,16]{0,1:T(8,128)} %get-tuple-element.1212) | copy-start | bytes 393220 | tf_op jit(solution)/shard_map/while
  553.8 11.3 %copy-start.10 = (f32[2048,16]{0,1:T(8,128)S(1)}, f32[2048,16]{0,1:T(8,128)}, u32[]{:S(2)}) copy-start(f32[2048,16]{0,1:T(8,128)} %get-tuple-element.1214) | copy-start | bytes 393220 | tf_op jit(solution)/shard_map/while
  594.1 11.3 %copy-start.8 = (f32[2048,16]{0,1:T(8,128)S(1)}, f32[2048,16]{0,1:T(8,128)}, u32[]{:S(2)}) copy-start(f32[2048,16]{0,1:T(8,128)} %get-tuple-element.1212) | copy-start | bytes 393220 | tf_op jit(solution)/shard_map/while
  594.1 11.3 %copy-start.10 = (f32[2048,16]{0,1:T(8,128)S(1)}, f32[2048,16]{0,1:T(8,128)}, u32[]{:S(2)}) copy-start(f32[2048,16]{0,1:T(8,128)} %get-tuple-element.1214) | copy-start | bytes 393220 | tf_op jit(solution)/shard_map/while
  634.3 11.3 %copy-start.8 = (f32[2048,16]{0,1:T(8,128)S(1)}, f32[2048,16]{0,1:T(8,128)}, u32[]{:S(2)}) copy-start(f32[2048,16]{0,1:T(8,128)} %get-tuple-element.1212) | copy-start | bytes 393220 | tf_op jit(solution)/shard_map/while
  634.4 11.3 %copy-start.10 = (f32[2048,16]{0,1:T(8,128)S(1)}, f32[2048,16]{0,1:T(8,128)}, u32[]{:S(2)}) copy-start(f32[2048,16]{0,1:T(8,128)} %get-tuple-element.1214) | copy-start | bytes 393220 | tf_op jit(solution)/shard_map/while
  678.7 127.4 %collective-permute-start.3 = (f32[3,6,2048]{2,1,0:T(8,128)S(1)}, f32[3,6,2048]{2,1,0:T(8,128)S(1)}, u32[]{:S(2)}, u32[]{:S(2)}) collective-permute-start(f32[3,6,2048]{2,1,0:T(8,128)S(1)} %slice.242), channel_id=1, source_target_pairs={{16,0},{32,16},{48,32},{64,48},{80,64},{96,80},{112,96},{128,112},... | collective-permute-start | bytes 442376 | tf_op jit(solution)/shard_map/ppermute | solution.py:12
  (32 other events, 99.6 us)
Sparse Core Ops, SparseCore 0:
  681.5 198.5 all-reduce.2
where the time goes:
time: 896 us; the launch traced here: 890 us
  other arithmetic  227 us (25%)
  waiting for transfers between devices  190 us (21%)
  matrix products  147 us (16%)
  blocking collectives  125 us (14%)
  starting transfers between devices  98.3 us (11%)
  local copies, waits for them, and re-layouts  81.3 us (9%)
  between operations  16 us (2%)
    psum x1, blocking collectives, per_device(): lax.psum((grad_short_part, weight_grad * jnp.sqrt(decay_rate), grad_skip_...  125 us
    ppermute x32, waiting for transfers between devices, shifted(): lax.ppermute(value, axis, [(source, source + steps) for source in range(l...  124 us
    ppermute x32, starting transfers between devices, shifted(): lax.ppermute(value, axis, [(source, source + steps) for source in range(l...  98.2 us
    dot_general x4, matrix products, forward_block(): jnp.dot(lower_mask, lifted, precision=lax.Precision.HIGHEST)  75.6 us
    dot_general x4, matrix products, backward_block(): jnp.dot(upper_mask, lowered, precision=lax.Precision.HIGHEST)  71.2 us
    psum x1, waiting for transfers between devices, per_device(): lax.psum((grad_short_part, weight_grad * jnp.sqrt(decay_rate), grad_skip_...  66.5 us
    dot_general x4, other arithmetic, backward_block(): jnp.dot(upper_mask, lowered, precision=lax.Precision.HIGHEST)  45.2 us
    dot_general x4, other arithmetic, forward_block(): jnp.dot(lower_mask, lifted, precision=lax.Precision.HIGHEST)  45.2 us
  transfers between devices with their start and end apart: 33, of which 31 were waited for; matrix products, arithmetic and copies ran while one was open for 2% of the time, Pallas kernels for 0%

commit v1 on v0

v1 whole, which is shorter than its diff:
```python
import jax
import jax.numpy as jnp
from jax import lax
from jax.experimental import pallas as pl
from jax.experimental.pallas import tpu as pltpu
from jax.sharding import PartitionSpec as P

SEGS = 8
STEPS = 16
ROWS = SEGS * STEPS
TAPS = 7
HALO = TAPS - 1
MODES = 16
LANES = 128
REDUCED = 40
F32 = jnp.float32
VMEM_BYTES = 56 << 20


def lanes_of(tile):
    return pl.ds(pl.multiple_of(tile * LANES, LANES), LANES)


def row(ref, index, lanes):
    return jnp.broadcast_to(ref[index : index + 1, lanes], (SEGS, LANES))


def slab(index):
    return slice(index * SEGS, (index + 1) * SEGS)


def store_masks(dist_ref, mask_ref, steps, gaps):
    for gap in range(1, gaps + 1):
        for t in range(steps):
            mask_ref[gap - 1, t] = (dist_ref[t] >= gap).astype(F32)


def fetch_columns(ref, stage, lanes):
    stage[...] = ref[:, lanes].astype(F32)
    return [stage[pl.ds(t, SEGS, stride=STEPS), :] for t in range(STEPS)]


def feature_kernel(
    q_ref, k_ref, v_ref, cot_ref, halo_ref, taps_ref, decay_ref, dist_ref, end_ref, chain_ref,
    raw_ref, feat_ref, cot_out, source_ref, grad_ref, gseg_ref, sloc_ref, rloc_ref, end_out, begin_out,
    stage, masks, open_mask, end_mask,
):
    store_masks(dist_ref, masks, STEPS, HALO)
    for t in range(STEPS):
        open_mask[t] = (dist_ref[t] >= t + 1).astype(F32)
        end_mask[t] = (end_ref[...] >= STEPS - 1 - t).astype(F32)

    def tile_body(tile, carry):
        lanes = lanes_of(tile)
        segment = lax.broadcasted_iota(jnp.int32, (SEGS, LANES), 0)
        first, last = segment == 0, segment == SEGS - 1
        for branch, ref in enumerate((q_ref, k_ref, v_ref)):
            rows = fetch_columns(ref, stage.at[branch], lanes)
            before = {}
            for back in range(1, HALO + 1):
                edge = row(halo_ref, branch * 8 + 8 - back, lanes)
                before[-back] = jnp.where(first, edge, pltpu.roll(rows[STEPS - back], 1, 0))
            taps = [row(taps_ref, branch * TAPS + j, lanes) for j in range(TAPS)]
            for t in range(STEPS):
                raw_ref[branch, slab(t), lanes] = rows[t]
                total = taps[0] * rows[t]
                for j in range(1, TAPS):
                    earlier = rows[t - j] if t >= j else before[t - j]
                    total = total + taps[j] * (earlier * masks[j - 1, t])
                feat_ref[branch, slab(t), lanes] = total
        upstream = fetch_columns(cot_ref, stage.at[3], lanes)
        for t in range(STEPS):
            cot_out[slab(t), lanes] = upstream[t]
            source_ref[slab(t), lanes] = feat_ref[1, slab(t), lanes] * feat_ref[2, slab(t), lanes]
            grad_ref[slab(t), lanes] = upstream[t] * feat_ref[0, slab(t), lanes]
        for low in range(0, MODES, 8):
            modes = range(low, low + 8)
            decay = [row(decay_ref, m, lanes) for m in modes]
            ends = [source_ref[slab(0), lanes] * end_mask[0]] * 8
            for t in range(1, STEPS):
                value = source_ref[slab(t), lanes] * end_mask[t]
                ends = [d * e + value for d, e in zip(decay, ends)]
            begins = [grad_ref[slab(STEPS - 1), lanes] * open_mask[STEPS - 1]] * 8
            for t in range(STEPS - 2, -1, -1):
                value = grad_ref[slab(t), lanes] * open_mask[t]
                begins = [d * b + value for d, b in zip(decay, begins)]
            for m, d, e, b in zip(modes, decay, ends, begins):
                gseg_ref[slab(m), lanes] = b
                for _ in range(4):
                    d = d * d
                for k in range(3):
                    e = e + (d * chain_ref[k]) * pltpu.roll(e, 1 << k, 0)
                    b = b + (d * chain_ref[3 + k]) * pltpu.roll(b, SEGS - (1 << k), 0)
                    d = d * d
                sloc_ref[slab(m), lanes] = jnp.where(first, 0.0, pltpu.roll(e, 1, 0))
                rloc_ref[slab(m), lanes] = jnp.where(last, 0.0, pltpu.roll(b, SEGS - 1, 0))
                end_out[m : m + 1, lanes] = e[SEGS - 1 :]
                begin_out[m : m + 1, lanes] = b[:1]
        return carry

    lax.fori_loop(0, q_ref.shape[1] // LANES, tile_body, 0)


def local_kernel(
    source_ref, grad_ref, gseg_ref, sloc_ref, rloc_ref, decay_ref, rate_ref, weight_ref, skip_ref, dist_ref, reach_ref,
    conv_ref, back_ref, swt_ref, rwt_ref, scoef_ref, rcoef_ref, local_ref,
    masks, stage,
):
    store_masks(dist_ref, masks, STEPS, STEPS - 1)

    def tile_body(tile, carry):
        lanes = lanes_of(tile)
        segment = lax.broadcasted_iota(jnp.int32, (SEGS, LANES), 0).astype(F32)
        decay = decay_ref[:, lanes]
        power = weight_ref[:, lanes]
        kernel = []
        for gap in range(STEPS):
            kernel.append(jnp.sum(power, axis=0, keepdims=True))
            power = power * decay
        kernel[0] = kernel[0] + skip_ref[:, lanes]
        source = [source_ref[slab(t), lanes] for t in range(STEPS)]
        grads = [grad_ref[slab(t), lanes] for t in range(STEPS)]
        conv, back, paired = [None] * STEPS, [None] * STEPS, []
        for gap in range(STEPS):
            weight = jnp.broadcast_to(kernel[gap], (SEGS, LANES))
            pair = jnp.zeros((SEGS, LANES), F32)
            for t in range(gap, STEPS):
                value, grad = source[t - gap], grads[t]
                if gap:
                    value, grad = value * masks[gap - 1, t], grad * masks[gap - 1, t]
                conv[t] = weight * value if gap == 0 else conv[t] + weight * value
                back[t - gap] = weight * grad if gap == 0 else back[t - gap] + weight * grad
                pair = pair + grads[t] * value
            paired.append(jnp.sum(pair, axis=0, keepdims=True))
        for t in range(STEPS):
            conv_ref[slab(t), lanes] = conv[t]
            back_ref[slab(t), lanes] = back[t]
        total = jnp.broadcast_to(paired[STEPS - 1], (MODES, LANES))
        for gap in range(STEPS - 2, -1, -1):
            total = total * decay + paired[gap]
        for m in range(MODES):
            arriving = sloc_ref[slab(m), lanes]
            stage[m : m + 1, :] = jnp.sum(arriving * gseg_ref[slab(m), lanes], axis=0, keepdims=True)
            scale = row(weight_ref, m, lanes) * row(decay_ref, m, lanes)
            rate = row(rate_ref, m, lanes) * (-float(STEPS))
            swt_ref[slab(m), lanes] = scale * arriving
            rwt_ref[slab(m), lanes] = scale * rloc_ref[slab(m), lanes]
            scoef_ref[slab(m), lanes] = scale * reach_ref[0] * jnp.exp(rate * segment)
            rcoef_ref[slab(m), lanes] = scale * reach_ref[1] * jnp.exp(rate * (SEGS - 1 - segment))
        local_ref[tile, 0:MODES] = total + stage[...] * decay
        local_ref[tile, MODES : MODES + 8] = jnp.broadcast_to(paired[0], (8, LANES))
        return carry

    lax.fori_loop(0, decay_ref.shape[1] // LANES, tile_body, 0)


def gradient_kernel(
    raw_ref, feat_ref, cot_ref, conv_ref, back_ref, swt_ref, rwt_ref, scoef_ref, rcoef_ref, local_ref,
    enter_ref, return_ref, begin_ref, decay_ref, root_ref, halo_ref, dist_ref, end_ref,
    out_ref, gfeat_ref, edge_ref, reduced_ref,
    stage, masks, open_mask, end_mask,
):
    store_masks(dist_ref, masks, STEPS, HALO)
    for t in range(STEPS):
        open_mask[t] = (dist_ref[t] >= t + 1).astype(F32)
        end_mask[t] = (end_ref[...] >= STEPS - 1 - t).astype(F32)

    def tile_body(tile, carry):
        lanes = lanes_of(tile)
        segment = lax.broadcasted_iota(jnp.int32, (SEGS, LANES), 0)
        first = segment == 0
        decay = [row(decay_ref, m, lanes) for m in range(MODES)]
        state = [
            swt_ref[slab(m), lanes] + scoef_ref[slab(m), lanes] * row(enter_ref, m, lanes)
            for m in range(MODES)
        ]
        for t in range(STEPS):
            filtered = conv_ref[slab(t), lanes] + open_mask[t] * tree_sum(state)
            stage[pl.ds(t, SEGS, stride=STEPS), :] = feat_ref[0, slab(t), lanes] * filtered
            gfeat_ref[0, slab(t), lanes] = cot_ref[slab(t), lanes] * filtered
            if t < STEPS - 1:
                state = [d * s for d, s in zip(decay, state)]
        out_ref[:, lanes] = stage[...].astype(out_ref.dtype)
        state = [
            rwt_ref[slab(m), lanes] + rcoef_ref[slab(m), lanes] * row(return_ref, m, lanes)
            for m in range(MODES)
        ]
        for t in range(STEPS - 1, -1, -1):
            grad = back_ref[slab(t), lanes] + end_mask[t] * tree_sum(state)
            gfeat_ref[1, slab(t), lanes] = grad * feat_ref[2, slab(t), lanes]
            gfeat_ref[2, slab(t), lanes] = grad * feat_ref[1, slab(t), lanes]
            if t:
                state = [d * s for d, s in zip(decay, state)]
        reduced_ref[tile, 0:MODES] = root_ref[:, lanes] * (
            local_ref[tile, 0:MODES] + enter_ref[:, lanes] * decay_ref[:, lanes] * begin_ref[:, lanes]
        )
        for branch in range(3):
            totals = [jnp.zeros((SEGS, LANES), F32)] * TAPS
            rows = [raw_ref[branch, slab(t), lanes] for t in range(STEPS)]
            before = {}
            for back in range(1, HALO + 1):
                edge = row(halo_ref, branch * 8 + 8 - back, lanes)
                before[-back] = jnp.where(first, edge, pltpu.roll(rows[STEPS - back], 1, 0))
            for t in range(STEPS):
                grad = gfeat_ref[branch, slab(t), lanes]
                if t < HALO:
                    edge_ref[branch * 8 + t : branch * 8 + t + 1, lanes] = grad[:1]
                totals[0] = totals[0] + grad * rows[t]
                for j in range(1, TAPS):
                    earlier = rows[t - j] if t >= j else before[t - j]
                    totals[j] = totals[j] + (grad * masks[j - 1, t]) * earlier
            edge_ref[branch * 8 + HALO : branch * 8 + 8, lanes] = jnp.zeros((8 - HALO, LANES), F32)
            for j in range(TAPS):
                at = MODES + branch * TAPS + j
                reduced_ref[tile, at : at + 1] = jnp.sum(totals[j], axis=0, keepdims=True)
        at = MODES + 3 * TAPS
        reduced_ref[tile, at:REDUCED] = local_ref[tile, MODES : MODES + REDUCED - at]
        return carry

    lax.fori_loop(0, decay_ref.shape[1] // LANES, tile_body, 0)


def tree_sum(values):
    while len(values) > 1:
        values = [a + b for a, b in zip(values[::2], values[1::2])]
    return values[0]


def input_kernel(gfeat_ref, edge_ref, taps_ref, dist_ref, gq_ref, gk_ref, gv_ref, stage, masks):
    store_masks(dist_ref, masks, STEPS + HALO, HALO)

    def tile_body(tile, carry):
        lanes = lanes_of(tile)
        segment = lax.broadcasted_iota(jnp.int32, (SEGS, LANES), 0)
        last = segment == SEGS - 1
        for branch, out_ref in enumerate((gq_ref, gk_ref, gv_ref)):
            rows = [gfeat_ref[branch, slab(t), lanes] for t in range(STEPS)]
            for t in range(HALO):
                edge = row(edge_ref, branch * 8 + t, lanes)
                rows.append(jnp.where(last, edge, pltpu.roll(rows[t], SEGS - 1, 0)))
            taps = [row(taps_ref, branch * TAPS + j, lanes) for j in range(TAPS)]
            for t in range(STEPS):
                total = taps[0] * rows[t]
                for j in range(1, TAPS):
                    total = total + taps[j] * (rows[t + j] * masks[j - 1, t + j])
                stage[branch, pl.ds(t, SEGS, stride=STEPS), :] = total
            out_ref[:, lanes] = stage[branch].astype(out_ref.dtype)
        return carry

    lax.fori_loop(0, gq_ref.shape[1] // LANES, tile_body, 0)


def call(body, name, outs, scratch, flops, *args):
    return pl.pallas_call(
        body,
        name=name,
        out_shape=[jax.ShapeDtypeStruct(shape, dtype) for shape, dtype in outs],
        in_specs=[pl.BlockSpec(memory_space=pltpu.VMEM)] * len(args),
        out_specs=[pl.BlockSpec(memory_space=pltpu.VMEM)] * len(outs),
        scratch_shapes=[pltpu.VMEM(shape, F32) for shape in scratch],
        compiler_params=pltpu.CompilerParams(vmem_limit_bytes=VMEM_BYTES),
        cost_estimate=pl.CostEstimate(flops=flops, bytes_accessed=8 << 20, transcendentals=0),
    )(*args)


def per_device(query_rows, key_rows, value_rows, cotangent, lengths, short_filter, residue, decay_rate, skip_gain):
    channels = query_rows.shape[2]
    tiles = channels // LANES
    count = lax.axis_size("ctx")
    here = lax.axis_index("ctx")
    chip, core = here // 2, here % 2
    anchor = here * ROWS

    order = jnp.arange(lengths.shape[1])
    starts = jnp.sum(jnp.where(order[None, :] < order[:, None], lengths[0][None, :], 0), axis=1)

    def since_start(positions):
        begun = jnp.where(starts <= positions[..., None], starts, -1)
        return (positions - jnp.max(begun, axis=-1)).astype(F32)

    def spread(values):
        return jnp.broadcast_to(values[..., None], (*values.shape, LANES))

    stacked = jnp.concatenate([x[0, ROWS - 8 :] for x in (query_rows, key_rows, value_rows)], axis=0)
    halo = lax.ppermute(stacked, "ctx", [(i, i + 1) for i in range(count - 1)]).astype(F32)

    segs, steps = jnp.arange(SEGS, dtype=jnp.int32), jnp.arange(STEPS + HALO, dtype=jnp.int32)
    dist = spread(since_start(anchor + segs[None, :] * STEPS + steps[:, None]))
    seg_end = since_start(anchor + segs * STEPS + STEPS - 1)
    chain = []
    for k in range(3):
        chain.append((seg_end >= (STEPS << k)) & (segs >= (1 << k)))
    for k in range(3):
        ahead = jnp.minimum(segs + (1 << k) - 1, SEGS - 1)
        through = since_start(anchor + ahead * STEPS + STEPS - 1) >= (STEPS << k)
        chain.append(through & (segs + (1 << k) < SEGS))
    chain = spread(jnp.stack(chain).astype(F32))
    from_left = (since_start(anchor + segs * STEPS - 1) >= segs * STEPS) | (segs == 0)
    to_right = seg_end[SEGS - 1] >= (SEGS - 1 - segs) * STEPS
    reach = spread(jnp.stack([from_left, to_right]).astype(F32))
    seg_end = spread(seg_end)

    rate = decay_rate.T
    root = jnp.sqrt(rate)
    weight = residue.T * root
    decay = jnp.exp(-rate)
    taps = short_filter.reshape(3 * TAPS, channels)

    def passes(position, span):
        return (since_start(position) >= span).astype(F32) * jnp.exp(-rate * float(span))

    full = (ROWS, channels)
    states = (MODES * SEGS, channels)
    raw, feat, upstream, source, grad, gseg, sloc, rloc, end_state, begin_state = call(
        feature_kernel, "features",
        [((3, *full), F32), ((3, *full), F32), (full, F32), (full, F32), (full, F32),
         (states, F32), (states, F32), (states, F32), ((MODES, channels), F32), ((MODES, channels), F32)],
        [(4, ROWS, LANES), (HALO, STEPS, SEGS, LANES), (STEPS, SEGS, LANES), (STEPS, SEGS, LANES)],
        1 << 26,
        query_rows[0], key_rows[0], value_rows[0], cotangent[0], halo, taps, decay, dist, seg_end, chain,
    )

    pairs = [(i, i ^ 1) for i in range(count)]

    def onward(value, chips):
        moves = [(i, i + 2 * chips * (1 - 2 * (i % 2))) for i in range(count)]
        return lax.ppermute(value, "ctx", [(i, j) for i, j in moves if 0 <= j < count])

    lower = core == 0
    own = jnp.where(lower, end_state, begin_state)
    other = lax.ppermute(jnp.where(lower, begin_state, end_state), "ctx", pairs)
    partner_end = (here ^ 1) * ROWS + ROWS - 1
    own_pass = passes(anchor + ROWS - 1, ROWS)
    partner_pass = passes(partner_end, ROWS)
    chip_pass = passes(chip * 2 * ROWS + 2 * ROWS - 1, 2 * ROWS)
    far_pass = passes(jnp.where(lower, chip * 2 * ROWS - 1, (chip + 3) * 2 * ROWS - 1), 4 * ROWS)
    chip_state = other + partner_pass * own
    chip_state = chip_state + chip_pass * onward(chip_state, 1)
    near, far = onward(chip_state, 1), onward(chip_state, 3)
    arrived = near + far_pass * far
    handed = lax.ppermute(own + own_pass * arrived, "ctx", pairs)
    entering = jnp.where(lower, arrived, handed)
    returning = jnp.where(lower, handed, arrived)

    conv, back, swt, rwt, scoef, rcoef, local = call(
        local_kernel, "local_filter",
        [(full, F32), (full, F32), (states, F32), (states, F32), (states, F32), (states, F32),
         ((tiles, MODES + 8, LANES), F32)],
        [(STEPS - 1, STEPS, SEGS, LANES), (MODES, LANES)],
        1 << 26,
        source, grad, gseg, sloc, rloc, decay, rate, weight, skip_gain[None], dist, reach,
    )
    block_out, gfeat, edge, reduced = call(
        gradient_kernel, "filter_gradients",
        [(full, jnp.bfloat16), ((3, *full), F32), ((24, channels), F32), ((tiles, REDUCED, LANES), F32)],
        [(ROWS, LANES), (HALO, STEPS, SEGS, LANES), (STEPS, SEGS, LANES), (STEPS, SEGS, LANES)],
        1 << 26,
        raw, feat, upstream, conv, back, swt, rwt, scoef, rcoef, local,
        entering, returning, begin_state, decay, root, halo, dist, seg_end,
    )
    next_edge = lax.ppermute(edge, "ctx", [(i, i - 1) for i in range(1, count)])
    grad_query, grad_key, grad_value = call(
        input_kernel, "input_gradients",
        [(full, jnp.bfloat16)] * 3,
        [(3, ROWS, LANES), (HALO, STEPS + HALO, SEGS, LANES)],
        1 << 26,
        gfeat, next_edge, taps, dist,
    )

    place = lax.axis_index("dp")
    cuts = [("ctx", 1, core), ("dp", 2, place // 2), ("dp", 1, place % 2)]
    total = reduced

    def exchange(value, axis, flip):
        return lax.ppermute(value, axis, [(i, i ^ flip) for i in range(lax.axis_size(axis))])

    for axis, flip, bit in cuts:
        half = total.shape[0] // 2
        low, high = total[:half], total[half:]
        sent = exchange(jnp.where(bit == 0, high, low), axis, flip)
        total = jnp.where(bit == 0, low, high) + sent
    flip = 2
    while flip < count:
        total = total + exchange(total, "ctx", flip)
        flip *= 2
    for axis, flip, bit in reversed(cuts):
        other_half = exchange(total, axis, flip)
        total = jnp.where(
            bit == 0, jnp.concatenate([total, other_half]), jnp.concatenate([other_half, total])
        )
    total = total.transpose(1, 0, 2).reshape(REDUCED, channels)
    return (
        block_out[None],
        grad_query[None],
        grad_key[None],
        grad_value[None],
        total[MODES : MODES + 3 * TAPS].reshape(3, TAPS, channels),
        total[:MODES].T,
        total[MODES + 3 * TAPS],
    )


def solution(mesh):
    rows = P("dp", "ctx", "ch")
    return jax.shard_map(
        per_device,
        mesh=mesh,
        in_specs=(rows, rows, rows, rows, P("dp", None), P(None, None, "ch"), P("ch", None), P("ch", None), P("ch")),
        out_specs=(rows, rows, rows, rows, P(None, None, "ch"), P("ch", None), P("ch")),
        check_vma=False,
    )
```

time: 896 us -> 134 us (0.15)
  other arithmetic: 227 us -> 11 us
  waiting for transfers between devices: 190 us -> 27.6 us
  matrix products: 147 us -> 0 us
  blocking collectives: 125 us -> 0 us
  local copies, waits for them, and re-layouts: 81.3 us -> 9.34 us
  starting transfers between devices: 98.3 us -> 40.5 us
  Pallas kernels: 0 us -> 41.2 us
  between operations: 16 us -> 3.58 us
    dot_general x8 -> x0, matrix products: 147 us -> none  [the longest x4 75.6 us: forward_block(): jnp.dot(lower_mask, lifted, precision=lax.Precision.HIGHEST)]
    psum x1 -> x0, blocking collectives: 125 us -> none  [per_device(): lax.psum((grad_short_part, weight_grad * jnp.sqrt(decay_rate), grad_skip_...]
    ppermute x32 -> x16, waiting for transfers between devices: 124 us -> 27.6 us  [the longest x3 12.2 us: onward(): lax.ppermute(value, 'ctx', [(i, j) for i, j in moves if 0 <= j < count])]
    dot_general x8 -> x0, other arithmetic: 90.4 us -> none  [the longest x4 45.2 us: backward_block(): jnp.dot(upper_mask, lowered, precision=lax.Precision.HIGHEST)]
    add x45 -> x11, other arithmetic: 74.4 us -> 3.11 us  [the longest x3 1.05 us: per_device(): total = jnp.where(bit == 0, low, high) + sent]
    psum x1 -> x0, waiting for transfers between devices: 66.5 us -> none  [per_device(): lax.psum((grad_short_part, weight_grad * jnp.sqrt(decay_rate), grad_skip_...]
    ppermute x32 -> x16, starting transfers between devices: 98.2 us -> 40.5 us  [the longest x9 20.6 us: exchange(): lax.ppermute(value, axis, [(i, i ^ flip) for i in range(lax.axis_size(axi...]
    pallas_call x0 -> x4, Pallas kernels: none -> 41.2 us  [call(): pl.pallas_call(body, name=name, out_shape=[jax.ShapeDtypeStruct(shape, dt...]
  transfers between devices with their start and end apart: 33 -> 16, of which waited for: 31 -> 11; matrix products, arithmetic and copies ran while one was open for 2% -> 6% of each run, Pallas kernels for 0% -> 11%
where the time goes in v1:
time: 134 us; the launch traced here: 133 us
  Pallas kernels  41.2 us (31%)
  starting transfers between devices  40.5 us (30%)
  waiting for transfers between devices  27.6 us (21%)
  other arithmetic  11 us (8%)
  local copies, waits for them, and re-layouts  9.34 us (7%)
  between operations  3.58 us (3%)
    pallas_call x4, Pallas kernels, call(): pl.pallas_call(body, name=name, out_shape=[jax.ShapeDtypeStruct(shape, dt...  41.2 us
    ppermute x9, starting transfers between devices, exchange(): lax.ppermute(value, axis, [(i, i ^ flip) for i in range(lax.axis_size(axi...  20.6 us
    ppermute x3, waiting for transfers between devices, onward(): lax.ppermute(value, 'ctx', [(i, j) for i, j in moves if 0 <= j < count])  12.2 us
    ppermute x9, waiting for transfers between devices, exchange(): lax.ppermute(value, axis, [(i, i ^ flip) for i in range(lax.axis_size(axi...  11.6 us
    ppermute x1, starting transfers between devices, per_device(): next_edge = lax.ppermute(edge, 'ctx', [(i, i - 1) for i in range(1, count)])  7.84 us
    ppermute x1, starting transfers between devices, per_device(): lax.ppermute(stacked, 'ctx', [(i, i + 1) for i in range(count - 1)])  4.94 us
    ppermute x3, starting transfers between devices, onward(): lax.ppermute(value, 'ctx', [(i, j) for i, j in moves if 0 <= j < count])  3.88 us
    ppermute x1, waiting for transfers between devices, per_device(): next_edge = lax.ppermute(edge, 'ctx', [(i, i - 1) for i in range(1, count)])  3.77 us
  transfers between devices with their start and end apart: 16, of which 11 were waited for; matrix products, arithmetic and copies ran while one was open for 6% of the time, Pallas kernels for 11%

profile of v1, /device:TPU:1, one launch (start us, length us, event | category | flops | bytes accessed | tf_op | source)
XLA Modules:
  0.0 133.2 jit_solution(7509443897570912341)
XLA Ops:
  0.6 0.0 copy-start
  0.6 0.8 slice_bitcast_fusion.3
  1.4 0.8 slice_bitcast_fusion.1
  2.2 4.9 %collective-permute-start = (bf16[24,2048]{1,0:T(8,128)(2,1)S(1)}, bf16[24,2048]{1,0:T(8,128)(2,1)S(1)}, u32[]{:S(2)}, u32[]{:S(2)}) collective-permute-start(bf16[24,2048]{1,0:T(8,128)(2,1)S(1)} %pad_maximum_fusion), channel_id=1, source_target_pairs={{0,16},{16,32},{32,48},{48,64},{64,80},{80,96},{96,112},{112,128},... | collective-permute-start | bytes 294920 | tf_op jit(solution)/shard_map/ppermute | solution.py:285
  7.3 0.1 iota_add_fusion
  7.3 0.8 select_reduce_fusion.6
  8.1 0.1 select_reduce_fusion
  8.2 0.1 subtract_convert_fusion
  8.3 0.3 select_reduce_fusion.1
  8.5 1.7 %bitcast_sqrt_fusion = (f32[16,2048]{1,0:T(8,128)}, f32[16,2048]{1,0:T(8,128)}, f32[16,2048]{1,0:T(8,128)}) fusion(f32[2048,16]{0,1:T(8,128)} %param.16, f32[2048,16]{0,1:T(8,128)} %param.15), kind=kLoop, calls=%fused_computation.74 | loop fusion | flops 65536 | bytes 655360 | tf_op jit(solution)/shard_map/sqrt | solution.py:304
  10.3 1.6 %reshape.423.taps_ref = f32[21,2048]{1,0:T(8,128)} reshape(f32[3,7,2048]{2,1,0:T(8,128)} %param.14) | data formatting | bytes 344064 | tf_op jit(solution)/shard_map/reshape | solution.py:307
  12.0 0.1 copy.18
  12.1 0.0 collective-permute-done
  12.1 0.7 convert_element_type.150.halo_ref
  12.8 0.7 broadcast_in_dim.102.dist_ref
  13.5 0.7 broadcast_in_dim.104.end_ref
  14.2 0.7 broadcast_in_dim.105.chain_ref
  14.9 13.4 %features.1 = (f32[3,128,2048]{2,1,0:T(8,128)}, f32[3,128,2048]{2,1,0:T(8,128)}, f32[128,2048]{1,0:T(8,128)}, f32[128,2048]{1,0:T(8,128)}, f32[128,2048]{1,0:T(8...) custom-call(bf16[128,2048]{1,0:T(8,128)(2,1)} %bitcast.74, ...), custom_call_target="tpu_custom_call" | custom-call | flops 67108864 | bytes 8388608 | tf_op jit(solution)/shard_map/features/pallas_call | solution.py:254
  28.3 0.9 broadcast_select_fusion.3
  29.2 0.1 collective-permute-start.1
  29.3 0.7 fusion.4
  30.8 0.0 collective-permute-done.1
  30.8 1.0 multiply_add_fusion.3
  31.7 1.3 collective-permute-start.2
  33.7 3.9 %collective-permute-done.2 = f32[16,2048]{1,0:T(8,128)S(1)} collective-permute-done((f32[16,2048]{1,0:T(8,128)S(1)}, f32[16,2048]{1,0:T(8,128)S(1)}, u32[]{:S(2)}, u32[]{:S(2)}) %collective-permute-start.2) | collective-permute-done | bytes 131104 | tf_op jit(solution)/shard_map/ppermute | solution.py:327
  37.7 1.3 collective-permute-start.3
  39.0 1.3 collective-permute-start.4
  40.3 0.6 slice.47
  42.2 1.7 %collective-permute-done.3 = f32[16,2048]{1,0:T(8,128)S(1)} collective-permute-done((f32[16,2048]{1,0:T(8,128)S(1)}, f32[16,2048]{1,0:T(8,128)S(1)}, u32[]{:S(2)}, u32[]{:S(2)}) %collective-permute-start.3) | collective-permute-done | bytes 131104 | tf_op jit(solution)/shard_map/ppermute | solution.py:327
  43.9 6.6 %collective-permute-done.4 = f32[16,2048]{1,0:T(8,128)S(1)} collective-permute-done((f32[16,2048]{1,0:T(8,128)S(1)}, f32[16,2048]{1,0:T(8,128)S(1)}, u32[]{:S(2)}, u32[]{:S(2)}) %collective-permute-start.4) | collective-permute-done | bytes 131104 | tf_op jit(solution)/shard_map/ppermute | solution.py:327
  50.4 1.0 multiply_add_fusion
  51.4 3.1 %collective-permute-start.5 = (f32[16,2048]{1,0:T(8,128)S(1)}, f32[16,2048]{1,0:T(8,128)S(1)}, u32[]{:S(2)}, u32[]{:S(2)}) collective-permute-start(f32[16,2048]{1,0:T(8,128)S(1)} %get-tuple-element.64), channel_id=1, source_target_pairs={{0,16},{16,0},{32,48},{48,32},{64,80},{80,64},{96,112},{112,96},{1... | collective-permute-start | bytes 393224 | tf_op jit(solution)/shard_map/ppermute | solution.py:341
  54.6 0.7 convert_compare_fusion
  55.2 0.7 broadcast_in_dim.107.reach_ref
  55.9 9.1 %local_filter.1 = (f32[128,2048]{1,0:T(8,128)}, f32[128,2048]{1,0:T(8,128)}, f32[128,2048]{1,0:T(8,128)}, f32[128,2048]{1,0:T(8,128)}, f32[128,2048]{1,0:T(8,128...) custom-call(f32[128,2048]{1,0:T(8,128)} %get-tuple-element.34.source_ref, f32[128,2048]{1,0:T(8,128)} %get-tuple-element.35.grad_ref, ...), custom_call_target="tpu_custom_call" | custom-call | flops 67108864 | bytes 8388608 | tf_op jit(solution)/shard_map/local_filter/pallas_call | solution.py:254
  65.0 0.0 collective-permute-done.5
  65.0 0.7 broadcast_select_fusion
  65.7 12.8 %filter_gradients.1 = (bf16[128,2048]{1,0:T(8,128)(2,1)}, f32[3,128,2048]{2,1,0:T(8,128)}, f32[24,2048]{1,0:T(8,128)}, f32[16,40,128]{2,1,0:T(8,128)}) custom-call(f32[3,128,2048]{2,1,0:T(8,128)} %get-tuple-element.31.raw_ref, f32[3,128,2048]{2,1,0:T(8,128)} %get-tuple-element.32.feat_ref, f32[128,2048]{1,0:T(8,128)} %get-tuple-element.33.cot_ref, ...), custom_call_target="tpu_custom_call" | custom-call | flops 67108864 | bytes 8388608 | tf_op jit(solution)/shard_map/filter_gradients/pallas_call | solution.py:254
  78.5 1.0 slice_select_fusion
  79.5 0.1 collective-permute-start.7
  79.7 1.4 %collective-permute-done.7 = f32[8,40,128]{2,1,0:T(8,128)S(1)} collective-permute-done((f32[8,40,128]{2,1,0:T(8,128)S(1)}, f32[8,40,128]{2,1,0:T(8,128)S(1)}, u32[]{:S(2)}, u32[]{:S(2)}) %collective-permute-start.7) | collective-permute-done | bytes 163872 | tf_op jit(solution)/shard_map/ppermute | solution.py:375
  81.0 1.0 select_add_fusion
  82.1 3.0 %collective-permute-start.8 = (f32[4,40,128]{2,1,0:T(8,128)S(1)}, f32[4,40,128]{2,1,0:T(8,128)S(1)}, u32[]{:S(2)}, u32[]{:S(2)}) collective-permute-start(f32[4,40,128]{2,1,0:T(8,128)S(1)} %slice_select_fusion.1), channel_id=1, source_target_pairs={{0,2},{1,3},{2,0},{3,1},{4,6},{5,7},{6,4},{7,5},{8,10},{9,11},{10,... | collective-permute-start | bytes 245768 | tf_op jit(solution)/shard_map/ppermute | solution.py:375
  85.1 2.5 %collective-permute-done.8 = f32[4,40,128]{2,1,0:T(8,128)S(1)} collective-permute-done((f32[4,40,128]{2,1,0:T(8,128)S(1)}, f32[4,40,128]{2,1,0:T(8,128)S(1)}, u32[]{:S(2)}, u32[]{:S(2)}) %collective-permute-start.8) | collective-permute-done | bytes 81952 | tf_op jit(solution)/shard_map/ppermute | solution.py:375
  87.6 1.4 %collective-permute-start.9 = (f32[2,40,128]{2,1,0:T(8,128)S(1)}, f32[2,40,128]{2,1,0:T(8,128)S(1)}, u32[]{:S(2)}, u32[]{:S(2)}) collective-permute-start(f32[2,40,128]{2,1,0:T(8,128)S(1)} %slice_select_fusion.2), channel_id=1, source_target_pairs={{0,1},{1,0},{2,3},{3,2},{4,5},{5,4},{6,7},{7,6},{8,9},{9,8},{10,11... | collective-permute-start | bytes 122888 | tf_op jit(solution)/shard_map/ppermute | solution.py:375
  89.0 1.6 %collective-permute-done.9 = f32[2,40,128]{2,1,0:T(8,128)S(1)} collective-permute-done((f32[2,40,128]{2,1,0:T(8,128)S(1)}, f32[2,40,128]{2,1,0:T(8,128)S(1)}, u32[]{:S(2)}, u32[]{:S(2)}) %collective-permute-start.9) | collective-permute-done | bytes 40992 | tf_op jit(solution)/shard_map/ppermute | solution.py:375
  90.5 1.8 %collective-permute-start.10 = (f32[2,40,128]{2,1,0:T(8,128)S(1)}, f32[2,40,128]{2,1,0:T(8,128)S(1)}, u32[]{:S(2)}, u32[]{:S(2)}) collective-permute-start(f32[2,40,128]{2,1,0:T(8,128)S(1)} %select_add_fusion.2), channel_id=1, source_target_pairs={{0,32},{16,48},{32,0},{48,16},{64,96},{80,112},{96,64},{112,80},{1... | collective-permute-start | bytes 122888 | tf_op jit(solution)/shard_map/ppermute | solution.py:375
  92.3 1.4 %collective-permute-done.10 = f32[2,40,128]{2,1,0:T(8,128)S(1)} collective-permute-done((f32[2,40,128]{2,1,0:T(8,128)S(1)}, f32[2,40,128]{2,1,0:T(8,128)S(1)}, u32[]{:S(2)}, u32[]{:S(2)}) %collective-permute-start.10) | collective-permute-done | bytes 40992 | tf_op jit(solution)/shard_map/ppermute | solution.py:375
  93.7 2.7 %collective-permute-start.11 = (f32[2,40,128]{2,1,0:T(8,128)S(1)}, f32[2,40,128]{2,1,0:T(8,128)S(1)}, u32[]{:S(2)}, u32[]{:S(2)}) collective-permute-start(f32[2,40,128]{2,1,0:T(8,128)S(1)} %add.424), channel_id=1, source_target_pairs={{0,64},{16,80},{32,96},{48,112},{64,0},{80,16},{96,32},{112,48},{1... | collective-permute-start | bytes 122888 | tf_op jit(solution)/shard_map/ppermute | solution.py:375
  96.4 1.4 %collective-permute-done.11 = f32[2,40,128]{2,1,0:T(8,128)S(1)} collective-permute-done((f32[2,40,128]{2,1,0:T(8,128)S(1)}, f32[2,40,128]{2,1,0:T(8,128)S(1)}, u32[]{:S(2)}, u32[]{:S(2)}) %collective-permute-start.11) | collective-permute-done | bytes 40992 | tf_op jit(solution)/shard_map/ppermute | solution.py:375
  97.8 6.0 %collective-permute-start.12 = (f32[2,40,128]{2,1,0:T(8,128)S(1)}, f32[2,40,128]{2,1,0:T(8,128)S(1)}, u32[]{:S(2)}, u32[]{:S(2)}) collective-permute-start(f32[2,40,128]{2,1,0:T(8,128)S(1)} %add.425), channel_id=1, source_target_pairs={{0,128},{16,144},{32,160},{48,176},{64,192},{80,208},{96,224},{112... | collective-permute-start | bytes 122888 | tf_op jit(solution)/shard_map/ppermute | solution.py:375
  103.8 1.6 %collective-permute-done.12 = f32[2,40,128]{2,1,0:T(8,128)S(1)} collective-permute-done((f32[2,40,128]{2,1,0:T(8,128)S(1)}, f32[2,40,128]{2,1,0:T(8,128)S(1)}, u32[]{:S(2)}, u32[]{:S(2)}) %collective-permute-start.12) | collective-permute-done | bytes 40992 | tf_op jit(solution)/shard_map/ppermute | solution.py:375
  105.4 1.3 collective-permute-start.13
  106.7 1.9 %collective-permute-done.13 = f32[2,40,128]{2,1,0:T(8,128)S(1)} collective-permute-done((f32[2,40,128]{2,1,0:T(8,128)S(1)}, f32[2,40,128]{2,1,0:T(8,128)S(1)}, u32[]{:S(2)}, u32[]{:S(2)}) %collective-permute-start.13) | collective-permute-done | bytes 40992 | tf_op jit(solution)/shard_map/ppermute | solution.py:375
  108.6 3.0 %collective-permute-start.14 = (f32[4,40,128]{2,1,0:T(8,128)S(1)}, f32[4,40,128]{2,1,0:T(8,128)S(1)}, u32[]{:S(2)}, u32[]{:S(2)}) collective-permute-start(f32[4,40,128]{2,1,0:T(8,128)S(1)} %maximum_select_fusion.2), channel_id=1, source_target_pairs={{0,2},{1,3},{2,0},{3,1},{4,6},{5,7},{6,4},{7,5},{8,10},{9,11},{10,... | collective-permute-start | bytes 245768 | tf_op jit(solution)/shard_map/ppermute | solution.py:375
  111.6 7.8 %collective-permute-start.6 = (f32[24,2048]{1,0:T(8,128)}, f32[24,2048]{1,0:T(8,128)S(1)}, u32[]{:S(2)}, u32[]{:S(2)}) collective-permute-start(f32[24,2048]{1,0:T(8,128)} %get-tuple-element.50), channel_id=1, source_target_pairs={{16,0},{32,16},{48,32},{64,48},{80,64},{96,80},{112,96},{128,112},... | collective-permute-start | bytes 589832 | tf_op jit(solution)/shard_map/ppermute | solution.py:361
  119.4 0.0 collective-permute-done.14
  119.4 1.4 %collective-permute-start.15 = (f32[8,40,128]{2,1,0:T(8,128)S(1)}, f32[8,40,128]{2,1,0:T(8,128)S(1)}, u32[]{:S(2)}, u32[]{:S(2)}) collective-permute-start(f32[8,40,128]{2,1,0:T(8,128)S(1)} %maximum_select_fusion.1), channel_id=1, source_target_pairs={{0,16},{16,0},{32,48},{48,32},{64,80},{80,64},{96,112},{112,96},{1... | collective-permute-start | bytes 491528 | tf_op jit(solution)/shard_map/ppermute | solution.py:375
  120.8 3.8 %collective-permute-done.6.edge_ref = f32[24,2048]{1,0:T(8,128)S(1)} collective-permute-done((f32[24,2048]{1,0:T(8,128)}, f32[24,2048]{1,0:T(8,128)S(1)}, u32[]{:S(2)}, u32[]{:S(2)}) %collective-permute-start.6) | collective-permute-done | bytes 196640 | tf_op jit(solution)/shard_map/ppermute | solution.py:361
  124.6 0.7 copy-done.1
  125.2 5.9 %input_gradients.1 = (bf16[128,2048]{1,0:T(8,128)(2,1)}, bf16[128,2048]{1,0:T(8,128)(2,1)}, bf16[128,2048]{1,0:T(8,128)(2,1)}) custom-call(f32[3,128,2048]{2,1,0:T(8,128)} %get-tuple-element.49.gfeat_ref, f32[24,2048]{1,0:T(8,128)} %copy-done.1, f32[21,2048]{1,0:T(8,128)} %reshape.423.taps_ref, f32[22,8,128]{2,1,0:T(8,128)} %broadcast_in_dim.102.dist_ref), custom_call_target="tpu_custom_call" | custom-call | flops 67108864 | bytes 8388608 | tf_op jit(solution)/shard_map/input_gradients/pallas_call | solution.py:254
  131.2 0.7 bitcast_bitcast_fusion
  131.8 0.6 slice.64
  132.5 0.7 reshape.424
  (30 shorter events, 0.3 us)
Async XLA Ops:
  0.6 30.1 %copy-start = (f32[2048,16]{0,1:T(8,128)S(1)}, f32[2048,16]{0,1:T(8,128)}, u32[]{:S(2)}) copy-start(f32[2048,16]{0,1:T(8,128)} %param.16) | copy-start | bytes 393220
  2.2 9.9 %collective-permute-start = (bf16[24,2048]{1,0:T(8,128)(2,1)S(1)}, bf16[24,2048]{1,0:T(8,128)(2,1)S(1)}, u32[]{:S(2)}, u32[]{:S(2)}) collective-permute-start(bf16[24,2048]{1,0:T(8,128)(2,1)S(1)} %pad_maximum_fusion), channel_id=1, source_target_pairs={{0,16},{16,32},{32,48},{48,64},{64,80},{80,96},{96,112},{112,128},... | collective-permute-start | bytes 294920 | tf_op jit(solution)/shard_map/ppermute | solution.py:285
  29.2 1.5 %collective-permute-start.1 = (f32[16,2048]{1,0:T(8,128)S(1)}, f32[16,2048]{1,0:T(8,128)S(1)}, u32[]{:S(2)}, u32[]{:S(2)}) collective-permute-start(f32[16,2048]{1,0:T(8,128)S(1)} %broadcast_select_fusion.3), channel_id=1, source_target_pairs={{0,16},{16,0},{32,48},{48,32},{64,80},{80,64},{96,112},{112,96},{1... | collective-permute-start | bytes 393224 | tf_op jit(solution)/shard_map/ppermute | solution.py:331
  31.7 5.9 %collective-permute-start.2 = (f32[16,2048]{1,0:T(8,128)S(1)}, f32[16,2048]{1,0:T(8,128)S(1)}, u32[]{:S(2)}, u32[]{:S(2)}) collective-permute-start(f32[16,2048]{1,0:T(8,128)S(1)} %multiply_add_fusion.3), channel_id=1, source_target_pairs={{0,32},{32,64},{48,16},{64,96},{80,48},{96,128},{112,80},{128,160}... | collective-permute-start | bytes 393224 | tf_op jit(solution)/shard_map/ppermute | solution.py:327
  37.7 6.2 %collective-permute-start.3 = (f32[16,2048]{1,0:T(8,128)S(1)}, f32[16,2048]{1,0:T(8,128)S(1)}, u32[]{:S(2)}, u32[]{:S(2)}) collective-permute-start(f32[16,2048]{1,0:T(8,128)S(1)} %multiply_add_fusion.2), channel_id=1, source_target_pairs={{0,32},{32,64},{48,16},{64,96},{80,48},{96,128},{112,80},{128,160}... | collective-permute-start | bytes 393224 | tf_op jit(solution)/shard_map/ppermute | solution.py:327
  39.0 11.5 %collective-permute-start.4 = (f32[16,2048]{1,0:T(8,128)S(1)}, f32[16,2048]{1,0:T(8,128)S(1)}, u32[]{:S(2)}, u32[]{:S(2)}) collective-permute-start(f32[16,2048]{1,0:T(8,128)S(1)} %multiply_add_fusion.2), channel_id=1, source_target_pairs={{0,96},{32,128},{64,160},{96,192},{112,16},{128,224},{144,48},{176... | collective-permute-start | bytes 393224 | tf_op jit(solution)/shard_map/ppermute | solution.py:327
  51.4 13.6 %collective-permute-start.5 = (f32[16,2048]{1,0:T(8,128)S(1)}, f32[16,2048]{1,0:T(8,128)S(1)}, u32[]{:S(2)}, u32[]{:S(2)}) collective-permute-start(f32[16,2048]{1,0:T(8,128)S(1)} %get-tuple-element.64), channel_id=1, source_target_pairs={{0,16},{16,0},{32,48},{48,32},{64,80},{80,64},{96,112},{112,96},{1... | collective-permute-start | bytes 393224 | tf_op jit(solution)/shard_map/ppermute | solution.py:341
  79.5 1.5 %collective-permute-start.7 = (f32[8,40,128]{2,1,0:T(8,128)S(1)}, f32[8,40,128]{2,1,0:T(8,128)S(1)}, u32[]{:S(2)}, u32[]{:S(2)}) collective-permute-start(f32[8,40,128]{2,1,0:T(8,128)S(1)} %slice_select_fusion), channel_id=1, source_target_pairs={{0,16},{16,0},{32,48},{48,32},{64,80},{80,64},{96,112},{112,96},{1... | collective-permute-start | bytes 491528 | tf_op jit(solution)/shard_map/ppermute | solution.py:375
  82.1 5.5 %collective-permute-start.8 = (f32[4,40,128]{2,1,0:T(8,128)S(1)}, f32[4,40,128]{2,1,0:T(8,128)S(1)}, u32[]{:S(2)}, u32[]{:S(2)}) collective-permute-start(f32[4,40,128]{2,1,0:T(8,128)S(1)} %slice_select_fusion.1), channel_id=1, source_target_pairs={{0,2},{1,3},{2,0},{3,1},{4,6},{5,7},{6,4},{7,5},{8,10},{9,11},{10,... | collective-permute-start | bytes 245768 | tf_op jit(solution)/shard_map/ppermute | solution.py:375
  87.6 2.9 %collective-permute-start.9 = (f32[2,40,128]{2,1,0:T(8,128)S(1)}, f32[2,40,128]{2,1,0:T(8,128)S(1)}, u32[]{:S(2)}, u32[]{:S(2)}) collective-permute-start(f32[2,40,128]{2,1,0:T(8,128)S(1)} %slice_select_fusion.2), channel_id=1, source_target_pairs={{0,1},{1,0},{2,3},{3,2},{4,5},{5,4},{6,7},{7,6},{8,9},{9,8},{10,11... | collective-permute-start | bytes 122888 | tf_op jit(solution)/shard_map/ppermute | solution.py:375
  90.5 3.1 %collective-permute-start.10 = (f32[2,40,128]{2,1,0:T(8,128)S(1)}, f32[2,40,128]{2,1,0:T(8,128)S(1)}, u32[]{:S(2)}, u32[]{:S(2)}) collective-permute-start(f32[2,40,128]{2,1,0:T(8,128)S(1)} %select_add_fusion.2), channel_id=1, source_target_pairs={{0,32},{16,48},{32,0},{48,16},{64,96},{80,112},{96,64},{112,80},{1... | collective-permute-start | bytes 122888 | tf_op jit(solution)/shard_map/ppermute | solution.py:375
  93.7 4.1 %collective-permute-start.11 = (f32[2,40,128]{2,1,0:T(8,128)S(1)}, f32[2,40,128]{2,1,0:T(8,128)S(1)}, u32[]{:S(2)}, u32[]{:S(2)}) collective-permute-start(f32[2,40,128]{2,1,0:T(8,128)S(1)} %add.424), channel_id=1, source_target_pairs={{0,64},{16,80},{32,96},{48,112},{64,0},{80,16},{96,32},{112,48},{1... | collective-permute-start | bytes 122888 | tf_op jit(solution)/shard_map/ppermute | solution.py:375
  97.8 7.6 %collective-permute-start.12 = (f32[2,40,128]{2,1,0:T(8,128)S(1)}, f32[2,40,128]{2,1,0:T(8,128)S(1)}, u32[]{:S(2)}, u32[]{:S(2)}) collective-permute-start(f32[2,40,128]{2,1,0:T(8,128)S(1)} %add.425), channel_id=1, source_target_pairs={{0,128},{16,144},{32,160},{48,176},{64,192},{80,208},{96,224},{112... | collective-permute-start | bytes 122888 | tf_op jit(solution)/shard_map/ppermute | solution.py:375
  105.4 3.1 %collective-permute-start.13 = (f32[2,40,128]{2,1,0:T(8,128)S(1)}, f32[2,40,128]{2,1,0:T(8,128)S(1)}, u32[]{:S(2)}, u32[]{:S(2)}) collective-permute-start(f32[2,40,128]{2,1,0:T(8,128)S(1)} %add.426), channel_id=1, source_target_pairs={{0,1},{1,0},{2,3},{3,2},{4,5},{5,4},{6,7},{7,6},{8,9},{9,8},{10,11... | collective-permute-start | bytes 122888 | tf_op jit(solution)/shard_map/ppermute | solution.py:375
  108.6 10.9 %collective-permute-start.14 = (f32[4,40,128]{2,1,0:T(8,128)S(1)}, f32[4,40,128]{2,1,0:T(8,128)S(1)}, u32[]{:S(2)}, u32[]{:S(2)}) collective-permute-start(f32[4,40,128]{2,1,0:T(8,128)S(1)} %maximum_select_fusion.2), channel_id=1, source_target_pairs={{0,2},{1,3},{2,0},{3,1},{4,6},{5,7},{6,4},{7,5},{8,10},{9,11},{10,... | collective-permute-start | bytes 245768 | tf_op jit(solution)/shard_map/ppermute | solution.py:375
  111.6 13.0 %collective-permute-start.6 = (f32[24,2048]{1,0:T(8,128)}, f32[24,2048]{1,0:T(8,128)S(1)}, u32[]{:S(2)}, u32[]{:S(2)}) collective-permute-start(f32[24,2048]{1,0:T(8,128)} %get-tuple-element.50), channel_id=1, source_target_pairs={{16,0},{32,16},{48,32},{64,48},{80,64},{96,80},{112,96},{128,112},... | collective-permute-start | bytes 589832 | tf_op jit(solution)/shard_map/ppermute | solution.py:361
  119.4 11.7 %collective-permute-start.15 = (f32[8,40,128]{2,1,0:T(8,128)S(1)}, f32[8,40,128]{2,1,0:T(8,128)S(1)}, u32[]{:S(2)}, u32[]{:S(2)}) collective-permute-start(f32[8,40,128]{2,1,0:T(8,128)S(1)} %maximum_select_fusion.1), channel_id=1, source_target_pairs={{0,16},{16,0},{32,48},{48,32},{64,80},{80,64},{96,112},{112,96},{1... | collective-permute-start | bytes 491528 | tf_op jit(solution)/shard_map/ppermute | solution.py:375
  124.6 0.7 copy-start.1

commit v2 on v1

v2 whole, which is shorter than its diff:
```python
from functools import partial

import jax
import jax.numpy as jnp
from jax import lax
from jax.experimental import pallas as pl
from jax.experimental.pallas import tpu as pltpu
from jax.sharding import PartitionSpec as P

SEGS = 8
STEPS = 16
ROWS = SEGS * STEPS
TAPS = 7
HALO = TAPS - 1
MODES = 16
LANES = 128
REDUCED = 40
F32 = jnp.float32
BF16 = jnp.bfloat16
VMEM_BYTES = 12 << 20
CHUNKS = 4
RAW, FEAT, COT = 0, 3, 6
SOURCE, GRAD, GSEG, SLOC, RLOC = range(5)
CONV, BACK, SWT, RWT, SCOEF, RCOEF = range(6)


def slab(block, index):
    at = block * ROWS + index * SEGS
    return slice(at, at + SEGS)


def row(ref, index, lanes):
    return jnp.broadcast_to(ref[index : index + 1, lanes], (SEGS, LANES))


def starts_of(spot_ref):
    found, begun = [], jnp.int32(0)
    for j in range(2, spot_ref.shape[0]):
        found.append(begun)
        begun = begun + spot_ref[j]
    return found


def since_start(starts, positions):
    begun = jnp.zeros_like(positions)
    for start in starts:
        begun = jnp.where(positions >= start, start, begun)
    return positions - begun


def segments():
    return lax.broadcasted_iota(jnp.int32, (SEGS, LANES), 0)


def flag(condition):
    return jnp.where(condition, 1.0, 0.0)


def store_masks(starts, anchor, mask_ref, steps, gaps):
    for t in range(steps):
        dist = since_start(starts, anchor + segments() * STEPS + t)
        for gap in range(1, gaps + 1):
            mask_ref[gap - 1, t] = flag(dist >= gap)


def store_edge_masks(starts, anchor, open_mask, end_mask):
    at_end = since_start(starts, anchor + segments() * STEPS + STEPS - 1)
    for t in range(STEPS):
        dist = since_start(starts, anchor + segments() * STEPS + t)
        open_mask[t] = flag(dist >= t + 1)
        end_mask[t] = flag(at_end >= STEPS - 1 - t)


def each_tile(count, body):
    def step(index, carry):
        body(index, pl.ds(pl.multiple_of(index * LANES, LANES), LANES))
        return carry

    lax.fori_loop(0, count, step, 0)


def fetch_columns(ref, stage, lanes):
    stage[...] = ref[:, lanes].astype(F32)
    return [stage[pl.ds(t, SEGS, stride=STEPS), :] for t in range(STEPS)]


def rows_before(rows, halo_ref, branch, lanes):
    first = segments() == 0
    return {
        -back: jnp.where(first, row(halo_ref, branch * 8 + 8 - back, lanes), pltpu.roll(rows[STEPS - back], 1, 0))
        for back in range(1, HALO + 1)
    }


def feature_kernel(
    spot_ref, q_ref, k_ref, v_ref, cot_ref, taps_in, rate_in, residue_in, skip_in, halo_ref,
    save_ref, pre_ref, own_ref, sent_ref, pass_ref, taps_ref, rate_ref, residue_ref, skip_ref,
    stage, masks, open_mask, end_mask, chain, columns, arrived, loaded,
):
    starts, here = starts_of(spot_ref), spot_ref[0]
    anchor, core, chip = here * ROWS, here % 2, here // 2

    inputs = (q_ref, k_ref, v_ref, cot_ref)
    chunk = columns.shape[2] // CHUNKS

    def fetch(which, part):
        cols = pl.ds(pl.multiple_of(part * chunk, LANES), chunk)
        return pltpu.make_async_copy(inputs[which].at[:, cols], columns.at[which, :, cols], arrived.at[which, part])

    parameters = [
        pltpu.make_async_copy(source, target, loaded.at[which])
        for which, (source, target) in enumerate(
            ((taps_in, taps_ref), (rate_in, rate_ref), (residue_in, residue_ref), (skip_in, skip_ref))
        )
    ]
    for which in range(4):
        fetch(which, 0).start()
    for copy in parameters:
        copy.start()
    for part in range(1, CHUNKS):
        for which in range(4):
            fetch(which, part).start()
    store_masks(starts, anchor, masks, STEPS, HALO)
    store_edge_masks(starts, anchor, open_mask, end_mask)
    for k in range(3):
        span = STEPS << k
        at_end = since_start(starts, anchor + segments() * STEPS + STEPS - 1)
        chain[k] = flag((at_end >= span) & (segments() >= (1 << k)))
        ahead = jnp.minimum(segments() + (1 << k), SEGS)
        at_end = since_start(starts, anchor + ahead * STEPS - 1)
        chain[3 + k] = flag((at_end >= span) & (segments() + (1 << k) < SEGS))

    for copy in parameters:
        copy.wait()

    def passes(position, span):
        return flag(since_start(starts, position) >= span)

    far_end = jnp.where(core == 0, chip, chip + 3) * 2 * ROWS - 1
    own_pass = passes(anchor + ROWS - 1, ROWS)
    partner_pass = passes((here + 1 - 2 * core) * ROWS + ROWS - 1, ROWS)
    chip_pass = passes(chip * 2 * ROWS + 2 * ROWS - 1, 2 * ROWS)
    far_pass = passes(far_end, 4 * ROWS)
    lower = core == 0

    def tile_body(tile, lanes):
        segment = segments()
        first, last = segment == 0, segment == SEGS - 1

        @pl.when(tile % (chunk // LANES) == 0)
        def _():
            for which in range(4):
                fetch(which, tile // (chunk // LANES)).wait()

        for branch in range(3):
            rows = fetch_columns(columns.at[branch], stage.at[branch], lanes)
            before = rows_before(rows, halo_ref, branch, lanes)
            taps = [jnp.broadcast_to(taps_ref[branch, j : j + 1, lanes], (SEGS, LANES)) for j in range(TAPS)]
            for t in range(STEPS):
                save_ref[tile, slab(RAW + branch, t)] = rows[t]
                total = taps[0] * rows[t]
                for j in range(1, TAPS):
                    earlier = rows[t - j] if t >= j else before[t - j]
                    total = total + taps[j] * (earlier * masks[j - 1, t])
                save_ref[tile, slab(FEAT + branch, t)] = total
        upstream = fetch_columns(columns.at[3], stage.at[3], lanes)
        for t in range(STEPS):
            save_ref[tile, slab(COT, t)] = upstream[t]
            pre_ref[tile, slab(SOURCE, t)] = save_ref[tile, slab(FEAT + 1, t)] * save_ref[tile, slab(FEAT + 2, t)]
            pre_ref[tile, slab(GRAD, t)] = upstream[t] * save_ref[tile, slab(FEAT, t)]
        for low in range(0, MODES, 8):
            modes = range(low, low + 8)
            decay = [jnp.exp(-row(rate_ref, m, lanes)) for m in modes]
            ends = [pre_ref[tile, slab(SOURCE, 0)] * end_mask[0]] * 8
            for t in range(1, STEPS):
                value = pre_ref[tile, slab(SOURCE, t)] * end_mask[t]
                ends = [d * e + value for d, e in zip(decay, ends)]
            begins = [pre_ref[tile, slab(GRAD, STEPS - 1)] * open_mask[STEPS - 1]] * 8
            for t in range(STEPS - 2, -1, -1):
                value = pre_ref[tile, slab(GRAD, t)] * open_mask[t]
                begins = [d * b + value for d, b in zip(decay, begins)]
            for m, d, e, b in zip(modes, decay, ends, begins):
                pre_ref[tile, slab(GSEG, m)] = b
                for _ in range(4):
                    d = d * d
                for k in range(3):
                    e = e + (d * chain[k]) * pltpu.roll(e, 1 << k, 0)
                    b = b + (d * chain[3 + k]) * pltpu.roll(b, SEGS - (1 << k), 0)
                    d = d * d
                pre_ref[tile, slab(SLOC, m)] = jnp.where(first, 0.0, pltpu.roll(e, 1, 0))
                pre_ref[tile, slab(RLOC, m)] = jnp.where(last, 0.0, pltpu.roll(b, SEGS - 1, 0))
                own_ref[m : m + 1, lanes] = jnp.where(lower, e[SEGS - 1 :], b[:1])
                sent_ref[m : m + 1, lanes] = jnp.where(lower, b[:1], e[SEGS - 1 :])
        power = jnp.exp(rate_ref[:, lanes] * -float(ROWS))
        pass_ref[0, :, lanes] = own_pass * power
        pass_ref[1, :, lanes] = partner_pass * power
        power = power * power
        pass_ref[2, :, lanes] = chip_pass * power
        pass_ref[3, :, lanes] = far_pass * (power * power)

    each_tile(save_ref.shape[0], tile_body)


def local_kernel(
    spot_ref, pre_ref, rate_ref, residue_ref, skip_ref,
    post_ref, local_ref,
    masks, reach, stage, weight_stage,
):
    starts, anchor = starts_of(spot_ref), spot_ref[0] * ROWS

    store_masks(starts, anchor, masks, STEPS, STEPS - 1)
    before = since_start(starts, anchor + segments() * STEPS - 1)
    reach[0] = flag((before >= segments() * STEPS) | (segments() == 0))
    at_end = since_start(starts, anchor + segments() * 0 + ROWS - 1)
    reach[1] = flag(at_end >= (SEGS - 1 - segments()) * STEPS)

    def tile_body(tile, lanes):
        segment = segments().astype(F32)
        rates = rate_ref[:, lanes]
        decay = jnp.exp(-rates)
        power = residue_ref[:, lanes] * jnp.sqrt(rates)
        weight_stage[...] = power * decay
        kernel = []
        for gap in range(STEPS):
            kernel.append(jnp.sum(power, axis=0, keepdims=True))
            power = power * decay
        kernel[0] = kernel[0] + skip_ref[:, lanes]
        source = [pre_ref[tile, slab(SOURCE, t)] for t in range(STEPS)]
        grads = [pre_ref[tile, slab(GRAD, t)] for t in range(STEPS)]
        conv, back, paired = [None] * STEPS, [None] * STEPS, []
        for gap in range(STEPS):
            weight = jnp.broadcast_to(kernel[gap], (SEGS, LANES))
            pair = jnp.zeros((SEGS, LANES), F32)
            for t in range(gap, STEPS):
                value, grad = source[t - gap], grads[t]
                if gap:
                    value, grad = value * masks[gap - 1, t], grad * masks[gap - 1, t]
                conv[t] = weight * value if gap == 0 else conv[t] + weight * value
                back[t - gap] = weight * grad if gap == 0 else back[t - gap] + weight * grad
                pair = pair + grads[t] * value
            paired.append(jnp.sum(pair, axis=0, keepdims=True))
        for t in range(STEPS):
            post_ref[tile, slab(CONV, t)] = conv[t]
            post_ref[tile, slab(BACK, t)] = back[t]
        total = jnp.broadcast_to(paired[STEPS - 1], (MODES, LANES))
        for gap in range(STEPS - 2, -1, -1):
            total = total * decay + paired[gap]
        for m in range(MODES):
            arriving = pre_ref[tile, slab(SLOC, m)]
            stage[m : m + 1, :] = jnp.sum(arriving * pre_ref[tile, slab(GSEG, m)], axis=0, keepdims=True)
            scale = row(weight_stage, m, slice(None))
            rate = row(rate_ref, m, lanes) * (-float(STEPS))
            post_ref[tile, slab(SWT, m)] = scale * arriving
            post_ref[tile, slab(RWT, m)] = scale * pre_ref[tile, slab(RLOC, m)]
            post_ref[tile, slab(SCOEF, m)] = scale * reach[0] * jnp.exp(rate * segment)
            post_ref[tile, slab(RCOEF, m)] = scale * reach[1] * jnp.exp(rate * (SEGS - 1 - segment))
        local_ref[tile, 0:MODES] = total + stage[...] * decay
        local_ref[tile, MODES : MODES + 8] = jnp.broadcast_to(paired[0], (8, LANES))

    each_tile(pre_ref.shape[0], tile_body)


def tree_sum(values):
    while len(values) > 1:
        values = [a + b for a, b in zip(values[::2], values[1::2])]
    return values[0]


def tile_slot(tile, spot_ref):
    core, place = spot_ref[0] % 2, spot_ref[1]
    half = jnp.where(tile // 8 == core, 0, 1)
    slot = tile % 8
    high, low = slot // 4, (slot // 2) % 2
    high = jnp.where(high == place // 2, 0, 1)
    low = jnp.where(low == place % 2, 0, 1)
    return half, high * 4 + low * 2 + slot % 2


def gradient_kernel(
    spot_ref, save_ref, post_ref, local_ref, arrived_ref, handed_ref, own_ref, sent_ref, rate_ref, halo_ref,
    out_ref, gfeat_ref, edge_ref, kept_ref, away_ref,
    stage, masks, open_mask, end_mask, parts,
):
    starts, anchor = starts_of(spot_ref), spot_ref[0] * ROWS
    lower = spot_ref[0] % 2 == 0

    store_masks(starts, anchor, masks, STEPS, HALO)
    store_edge_masks(starts, anchor, open_mask, end_mask)

    def tile_body(tile, lanes):
        decay = [jnp.exp(-row(rate_ref, m, lanes)) for m in range(MODES)]
        arrived, handed = arrived_ref[:, lanes], handed_ref[:, lanes]
        entering = jnp.where(lower, arrived, handed)
        parts[0:MODES] = entering
        parts[MODES:] = jnp.where(lower, handed, arrived)
        state = [
            post_ref[tile, slab(SWT, m)] + post_ref[tile, slab(SCOEF, m)] * row(parts, m, slice(None))
            for m in range(MODES)
        ]
        for t in range(STEPS):
            filtered = post_ref[tile, slab(CONV, t)] + open_mask[t] * tree_sum(state)
            stage[pl.ds(t, SEGS, stride=STEPS), :] = save_ref[tile, slab(FEAT, t)] * filtered
            gfeat_ref[tile, slab(0, t)] = save_ref[tile, slab(COT, t)] * filtered
            if t < STEPS - 1:
                state = [d * s for d, s in zip(decay, state)]
        out_ref[:, lanes] = stage[...].astype(out_ref.dtype)
        state = [
            post_ref[tile, slab(RWT, m)] + post_ref[tile, slab(RCOEF, m)] * row(parts, MODES + m, slice(None))
            for m in range(MODES)
        ]
        for t in range(STEPS - 1, -1, -1):
            grad = post_ref[tile, slab(BACK, t)] + end_mask[t] * tree_sum(state)
            gfeat_ref[tile, slab(1, t)] = grad * save_ref[tile, slab(FEAT + 2, t)]
            gfeat_ref[tile, slab(2, t)] = grad * save_ref[tile, slab(FEAT + 1, t)]
            if t:
                state = [d * s for d, s in zip(decay, state)]
        rates = rate_ref[:, lanes]
        begin = jnp.where(lower, sent_ref[:, lanes], own_ref[:, lanes])
        sums = [jnp.sqrt(rates) * (local_ref[tile, 0:MODES] + entering * jnp.exp(-rates) * begin)]
        for branch in range(3):
            totals = [jnp.zeros((SEGS, LANES), F32)] * TAPS
            rows = [save_ref[tile, slab(RAW + branch, t)] for t in range(STEPS)]
            before = rows_before(rows, halo_ref, branch, lanes)
            for t in range(STEPS):
                grad = gfeat_ref[tile, slab(branch, t)]
                if t < HALO:
                    edge_ref[branch * 8 + t : branch * 8 + t + 1, lanes] = grad[:1]
                totals[0] = totals[0] + grad * rows[t]
                for j in range(1, TAPS):
                    earlier = rows[t - j] if t >= j else before[t - j]
                    totals[j] = totals[j] + (grad * masks[j - 1, t]) * earlier
            edge_ref[branch * 8 + HALO : branch * 8 + 8, lanes] = jnp.zeros((8 - HALO, LANES), F32)
            sums += [jnp.sum(total, axis=0, keepdims=True) for total in totals]
        sums.append(local_ref[tile, MODES : MODES + REDUCED - MODES - 3 * TAPS])
        half, slot = tile_slot(tile, spot_ref)
        for which, ref in enumerate((kept_ref, away_ref)):

            @pl.when(half == which)
            def _(ref=ref):
                at = 0
                for piece in sums:
                    ref[slot, at : at + piece.shape[0]] = piece
                    at += piece.shape[0]

    each_tile(save_ref.shape[0], tile_body)


def input_kernel(branch, spot_ref, gfeat_ref, edge_ref, taps_ref, out_ref, stage, masks):
    store_masks(starts_of(spot_ref), spot_ref[0] * ROWS, masks, STEPS + HALO, HALO)

    def tile_body(tile, lanes):
        last = segments() == SEGS - 1
        rows = [gfeat_ref[tile, slab(branch, t)] for t in range(STEPS)]
        for t in range(HALO):
            edge = row(edge_ref, branch * 8 + t, lanes)
            rows.append(jnp.where(last, edge, pltpu.roll(rows[t], SEGS - 1, 0)))
        taps = [jnp.broadcast_to(taps_ref[branch, j : j + 1, lanes], (SEGS, LANES)) for j in range(TAPS)]
        for t in range(STEPS):
            total = taps[0] * rows[t]
            for j in range(1, TAPS):
                total = total + taps[j] * (rows[t + j] * masks[j - 1, t + j])
            stage[pl.ds(t, SEGS, stride=STEPS), :] = total
        out_ref[:, lanes] = stage[...].astype(out_ref.dtype)

    each_tile(gfeat_ref.shape[0], tile_body)


def result_kernel(spot_ref, kept_ref, away_ref, short_ref, residue_ref, skip_ref):
    def tile_body(tile, lanes):
        half, slot = tile_slot(tile, spot_ref)
        block = jnp.where(half == 0, kept_ref[slot], away_ref[slot])
        for branch in range(3):
            at = MODES + branch * TAPS
            short_ref[branch, :, lanes] = block[at : at + TAPS]
        residue_ref[:, lanes] = block[:MODES]
        at = MODES + 3 * TAPS
        skip_ref[:, lanes] = block[at : at + 1]

    each_tile(kept_ref.shape[0] * 2, tile_body)


def combine_kernel(which, first_ref, pass_ref, second_ref, out_ref):
    out_ref[...] = first_ref[...] + pass_ref[which] * second_ref[...]


def arrive_kernel(near_ref, far_ref, own_ref, pass_ref, arrived_ref, handed_ref):
    arrived_ref[...] = near_ref[...] + pass_ref[3] * far_ref[...]
    handed_ref[...] = own_ref[...] + pass_ref[0] * arrived_ref[...]


SMEM, VMEM, HBM = (pl.BlockSpec(memory_space=space) for space in (pltpu.SMEM, pltpu.VMEM, pltpu.HBM))
MASKS = (HALO, STEPS, SEGS, LANES)
EDGE_MASKS = (STEPS, SEGS, LANES)
STAGE = (ROWS, LANES)


def call(body, name, ins, outs, scratch, *args):
    return pl.pallas_call(
        body,
        name=name,
        out_shape=[out if isinstance(out, jax.ShapeDtypeStruct) else pltpu.VMEM(out, F32) for out in outs],
        in_specs=ins,
        out_specs=[VMEM] * len(outs),
        scratch_shapes=[pltpu.VMEM(one, F32) if isinstance(one, tuple) else one for one in scratch],
        compiler_params=pltpu.CompilerParams(vmem_limit_bytes=VMEM_BYTES),
        cost_estimate=pl.CostEstimate(flops=1 << 26, bytes_accessed=8 << 20, transcendentals=0),
    )(*[x if spec is SMEM else pltpu.with_memory_space_constraint(x, spec.memory_space) for x, spec in zip(args, ins)])


def features(spot, query, key, value, upstream, taps, rate, residue, skip, halo):
    channels = query.shape[1]
    tiles, states = channels // LANES, (MODES, channels)
    return call(
        feature_kernel, "features",
        [SMEM] + [HBM] * 8 + [VMEM],
        [(tiles, 7 * ROWS, LANES), (tiles, 5 * ROWS, LANES), states, states, (4, *states),
         taps.shape, rate.shape, residue.shape, skip.shape],
        [(4, *STAGE), MASKS, EDGE_MASKS, EDGE_MASKS, (6, SEGS, LANES),
         pltpu.VMEM((4, ROWS, channels), BF16), pltpu.SemaphoreType.DMA((4, CHUNKS)), pltpu.SemaphoreType.DMA((4,))],
        spot, query, key, value, upstream, taps, rate, residue, skip, halo,
    )


def local_filter(spot, pre, rate, residue, skip):
    tiles = pre.shape[0]
    return call(
        local_kernel, "local_filter",
        [SMEM, VMEM, VMEM, VMEM, VMEM],
        [(tiles, 6 * ROWS, LANES), (tiles, MODES + 8, LANES)],
        [(STEPS - 1, STEPS, SEGS, LANES), (2, SEGS, LANES), (MODES, LANES), (MODES, LANES)],
        spot, pre, rate, residue, skip,
    )


def filter_gradients(spot, save, post, local, arrived, handed, own, sent, rate, halo):
    tiles, channels = save.shape[0], rate.shape[1]
    half = (tiles // 2, REDUCED, LANES)
    return call(
        gradient_kernel, "filter_gradients",
        [SMEM] + [VMEM] * 9,
        [jax.ShapeDtypeStruct((ROWS, channels), BF16), (tiles, 3 * ROWS, LANES), (24, channels), half, half],
        [STAGE, MASKS, EDGE_MASKS, EDGE_MASKS, (2 * MODES, LANES)],
        spot, save, post, local, arrived, handed, own, sent, rate, halo,
    )


def input_gradient(branch, spot, gfeat, edge, taps):
    [made] = call(
        partial(input_kernel, branch), "input_gradient",
        [SMEM, VMEM, VMEM, VMEM],
        [jax.ShapeDtypeStruct((ROWS, taps.shape[2]), BF16)],
        [STAGE, (HALO, STEPS + HALO, SEGS, LANES)],
        spot, gfeat, edge, taps,
    )
    return made


def results(spot, kept, away):
    channels = 2 * kept.shape[0] * LANES
    shapes = (3, TAPS, channels), (MODES, channels), (1, channels)
    return call(
        result_kernel, "parameter_gradients",
        [SMEM, VMEM, VMEM], [jax.ShapeDtypeStruct(shape, F32) for shape in shapes], [], spot, kept, away,
    )


def combine(which, first, through, second):
    [made] = call(
        partial(combine_kernel, which), "combine", [VMEM] * 3, [first.shape], [], first, through, second
    )
    return made


def per_device(query_rows, key_rows, value_rows, cotangent, lengths, short_filter, residue, decay_rate, skip_gain):
    count = lax.axis_size("ctx")
    place = jnp.stack([lax.axis_index("ctx"), lax.axis_index("dp")]).astype(jnp.int32)
    spot = jnp.concatenate([place, lengths[0]])

    stacked = jnp.concatenate([x[0, ROWS - 8 :] for x in (query_rows, key_rows, value_rows)], axis=0)
    halo = lax.ppermute(stacked, "ctx", [(i, i + 1) for i in range(count - 1)]).astype(F32)
    save, pre, own, sent, through, taps, rate, residue, skip = features(
        spot, query_rows[0], key_rows[0], value_rows[0], cotangent[0],
        short_filter, decay_rate.T, residue.T, skip_gain[None], halo,
    )

    pairs = [(i, i ^ 1) for i in range(count)]

    def onward(value, chips):
        moves = [(i, i + 2 * chips * (1 - 2 * (i % 2))) for i in range(count)]
        return lax.ppermute(value, "ctx", [(i, j) for i, j in moves if 0 <= j < count])

    chip_state = combine(1, lax.ppermute(sent, "ctx", pairs), through, own)
    chip_state = combine(2, chip_state, through, onward(chip_state, 1))
    chip_state, pre = lax.optimization_barrier((chip_state, pre))
    near, far = onward(chip_state, 1), onward(chip_state, 3)
    post, local = local_filter(spot, pre, rate, residue, skip)
    far, post = lax.optimization_barrier((far, post))
    arrived, handed = call(
        arrive_kernel, "arrive", [VMEM] * 4, [own.shape, own.shape], [], near, far, own, through
    )
    handed = lax.ppermute(handed, "ctx", pairs)

    block_out, gfeat, edge, kept, away = filter_gradients(
        spot, save, post, local, arrived, handed, own, sent, rate, halo
    )
    next_edge = lax.ppermute(edge, "ctx", [(i, i - 1) for i in range(1, count)])

    def exchange(value, axis, flip):
        return lax.ppermute(value, axis, [(i, i ^ flip) for i in range(lax.axis_size(axis))])

    grad_inputs = []

    def exchange_beside(value, axis, flip):
        value, beside = lax.optimization_barrier((value, next_edge))
        made = input_gradient(len(grad_inputs), spot, gfeat, beside, taps)
        sent, made = lax.optimization_barrier((exchange(value, axis, flip), made))
        grad_inputs.append(made)
        return sent

    received, next_edge = lax.optimization_barrier((exchange(away, "ctx", 1), next_edge))
    total = kept + received
    for flip in (2, 1):
        half = total.shape[0] // 2
        total = total[:half] + exchange(total[half:], "dp", flip)
    for flip in (2, 4, 8):
        total = total + exchange_beside(total, "ctx", flip)
    for flip in (1, 2):
        total = jnp.concatenate([total, exchange(total, "dp", flip)])
    grad_short, grad_residue, grad_skip = results(spot, total, exchange(total, "ctx", 1))
    return (block_out[None], *(g[None] for g in grad_inputs), grad_short, grad_residue.T, grad_skip[0])


def solution(mesh):
    rows = P("dp", "ctx", "ch")
    return jax.shard_map(
        per_device,
        mesh=mesh,
        in_specs=(rows, rows, rows, rows, P("dp", None), P(None, None, "ch"), P("ch", None), P("ch", None), P("ch")),
        out_specs=(rows, rows, rows, rows, P(None, None, "ch"), P("ch", None), P("ch")),
        check_vma=False,
    )
```

time: 134 us -> 102 us (0.76)
  Pallas kernels: 41.2 us -> 30.7 us
  other arithmetic: 11 us -> 0.83 us
  local copies, waits for them, and re-layouts: 9.34 us -> 1.55 us
  starting transfers between devices: 40.5 us -> 35.2 us
  waiting for transfers between devices: 27.6 us -> 32.3 us
  between operations: 3.58 us -> 0.77 us
    pallas_call x4 -> x10, Pallas kernels: 41.2 us -> 30.7 us  [call(): pl.pallas_call(body, name=name, out_shape=[out if isinstance(out, jax.Sha...]
    ppermute x1, starting transfers between devices: 7.84 us -> 2.26 us  [per_device(): next_edge = lax.ppermute(edge, 'ctx', [(i, i - 1) for i in range(1, count)])]
    add x11 -> x6, other arithmetic: 3.11 us -> 0.06 us  [the longest x3 0.02 us: per_device(): total = total + exchange_beside(total, 'ctx', flip)]
    ppermute x2, starting transfers between devices: 3.24 us -> 6.16 us  [the longest x1 6.07 us: per_device(): handed = lax.ppermute(handed, 'ctx', pairs)]
    broadcast_in_dim x4 -> x0, local copies, waits for them, and re-layouts: 2.73 us -> none  [spread(): return jnp.broadcast_to(values[..., None], (*values.shape, LANES))]
    select_n x7 -> x0, other arithmetic: 2.7 us -> none  [the longest x3 1.03 us: per_device(): sent = exchange(jnp.where(bit == 0, high, low), axis, flip)]
    ppermute x9, starting transfers between devices: 20.6 us -> 18 us  [exchange(): lax.ppermute(value, axis, [(i, i ^ flip) for i in range(lax.axis_size(axi...]
    ppermute x9, waiting for transfers between devices: 11.6 us -> 14 us  [exchange(): lax.ppermute(value, axis, [(i, i ^ flip) for i in range(lax.axis_size(axi...]
  transfers between devices with their start and end apart: 16 -> 16, of which waited for: 11 -> 14; matrix products, arithmetic and copies ran while one was open for 6% -> 1% of each run, Pallas kernels for 11% -> 12%
where the time goes in v2:
time: 102 us; the launch traced here: 101 us
  starting transfers between devices  35.2 us (35%)
  waiting for transfers between devices  32.3 us (32%)
  Pallas kernels  30.7 us (30%)
  local copies, waits for them, and re-layouts  1.55 us (2%)
    pallas_call x10, Pallas kernels, call(): pl.pallas_call(body, name=name, out_shape=[out if isinstance(out, jax.Sha...  30.7 us
    ppermute x9, starting transfers between devices, exchange(): lax.ppermute(value, axis, [(i, i ^ flip) for i in range(lax.axis_size(axi...  18 us
    ppermute x9, waiting for transfers between devices, exchange(): lax.ppermute(value, axis, [(i, i ^ flip) for i in range(lax.axis_size(axi...  14 us
    ppermute x3, waiting for transfers between devices, onward(): lax.ppermute(value, 'ctx', [(i, j) for i, j in moves if 0 <= j < count])  11.9 us
    ppermute x1, starting transfers between devices, per_device(): handed = lax.ppermute(handed, 'ctx', pairs)  6.07 us
    ppermute x1, starting transfers between devices, per_device(): lax.ppermute(stacked, 'ctx', [(i, i + 1) for i in range(count - 1)])  4.94 us
    ppermute x3, starting transfers between devices, onward(): lax.ppermute(value, 'ctx', [(i, j) for i, j in moves if 0 <= j < count])  3.88 us
    ppermute x1, waiting for transfers between devices, per_device(): next_edge = lax.ppermute(edge, 'ctx', [(i, i - 1) for i in range(1, count)])  3.23 us
  transfers between devices with their start and end apart: 16, of which 14 were waited for; matrix products, arithmetic and copies ran while one was open for 1% of the time, Pallas kernels for 12%

profile of v2, /device:TPU:1, one launch (start us, length us, event | category | flops | bytes accessed | tf_op | source)
XLA Modules:
  0.0 101.4 jit_solution(7873293576897388812)
XLA Ops:
  0.6 0.8 slice_bitcast_fusion.2
  1.4 0.8 slice_bitcast_fusion
  2.2 4.9 %collective-permute-start = (bf16[24,2048]{1,0:T(8,128)(2,1)S(1)}, bf16[24,2048]{1,0:T(8,128)(2,1)S(1)}, u32[]{:S(2)}, u32[]{:S(2)}) collective-permute-start(bf16[24,2048]{1,0:T(8,128)(2,1)S(1)} %pad_maximum_fusion.1), channel_id=1, source_target_pairs={{0,16},{16,32},{32,48},{48,64},{64,80},{80,96},{96,112},{112,128},... | collective-permute-start | bytes 294920 | tf_op jit(solution)/shard_map/ppermute | solution.py:480
  7.1 0.7 pad_add_fusion.spot_ref
  7.9 0.9 collective-permute-done
  8.8 9.9 %features.1 = (f32[16,896,128]{2,1,0:T(8,128)S(1)}, f32[16,640,128]{2,1,0:T(8,128)S(1)}, f32[16,2048]{1,0:T(8,128)S(1)}, f32[16,2048]{1,0:T(8,128)S(1)}, f32[4,1...) custom-call(s32[10]{0:T(128)S(1)} %pad_add_fusion.spot_ref, ...), custom_call_target="tpu_custom_call" | custom-call | flops 67108864 | bytes 8388608 | tf_op jit(solution)/shard_map/features/pallas_call | solution.py:398
  18.7 0.1 collective-permute-start.1
  18.8 1.3 %collective-permute-done.1.first_ref = f32[16,2048]{1,0:T(8,128)S(1)} collective-permute-done((f32[16,2048]{1,0:T(8,128)S(1)}, f32[16,2048]{1,0:T(8,128)S(1)}, u32[]{:S(2)}, u32[]{:S(2)}) %collective-permute-start.1) | collective-permute-done | bytes 131104 | tf_op jit(solution)/shard_map/ppermute | solution.py:492
  20.2 1.3 %collective-permute-start.2 = (f32[16,2048]{1,0:T(8,128)S(1)}, f32[16,2048]{1,0:T(8,128)S(1)}, u32[]{:S(2)}, u32[]{:S(2)}) collective-permute-start(f32[16,2048]{1,0:T(8,128)S(1)} %combine.2.first_ref), channel_id=1, source_target_pairs={{0,32},{32,64},{48,16},{64,96},{80,48},{96,128},{112,80},{128,160}... | collective-permute-start | bytes 393224 | tf_op jit(solution)/shard_map/ppermute | solution.py:490
  21.5 5.1 %collective-permute-done.2.second_ref = f32[16,2048]{1,0:T(8,128)S(1)} collective-permute-done((f32[16,2048]{1,0:T(8,128)S(1)}, f32[16,2048]{1,0:T(8,128)S(1)}, u32[]{:S(2)}, u32[]{:S(2)}) %collective-permute-start.2) | collective-permute-done | bytes 131104 | tf_op jit(solution)/shard_map/ppermute | solution.py:490
  26.6 1.3 %collective-permute-start.3 = (f32[16,2048]{1,0:T(8,128)S(1)}, f32[16,2048]{1,0:T(8,128)S(1)}, u32[]{:S(2)}, u32[]{:S(2)}) collective-permute-start(f32[16,2048]{1,0:T(8,128)S(1)} %combine.3), channel_id=1, source_target_pairs={{0,96},{32,128},{64,160},{96,192},{112,16},{128,224},{144,48},{176... | collective-permute-start | bytes 393224 | tf_op jit(solution)/shard_map/ppermute | solution.py:490
  27.9 1.3 %collective-permute-start.4 = (f32[16,2048]{1,0:T(8,128)S(1)}, f32[16,2048]{1,0:T(8,128)S(1)}, u32[]{:S(2)}, u32[]{:S(2)}) collective-permute-start(f32[16,2048]{1,0:T(8,128)S(1)} %combine.3), channel_id=1, source_target_pairs={{0,32},{32,64},{48,16},{64,96},{80,48},{96,128},{112,80},{128,160}... | collective-permute-start | bytes 393224 | tf_op jit(solution)/shard_map/ppermute | solution.py:490
  29.2 4.5 %local_filter.1 = (f32[16,768,128]{2,1,0:T(8,128)S(1)}, f32[16,24,128]{2,1,0:T(8,128)S(1)}) custom-call(s32[10]{0:T(128)S(1)} %pad_add_fusion.spot_ref, f32[16,640,128]{2,1,0:T(8,128)S(1)} %get-tuple-element.52.pre_ref, f32[16,2048]{1,0:T(8,128)S(1)} %get-tuple-element.53.rate_ref, f32[16,2048]{1,0:T(8,128)S(1)} %get-tuple-element.54.residue_ref, ...), custom_call_target="tpu_custom_call" | custom-call | flops 67108864 | bytes 8388608 | tf_op jit(solution)/shard_map/local_filter/pallas_call | solution.py:398
  33.7 6.8 %collective-permute-done.3.far_ref = f32[16,2048]{1,0:T(8,128)S(1)} collective-permute-done((f32[16,2048]{1,0:T(8,128)S(1)}, f32[16,2048]{1,0:T(8,128)S(1)}, u32[]{:S(2)}, u32[]{:S(2)}) %collective-permute-start.3) | collective-permute-done | bytes 131104 | tf_op jit(solution)/shard_map/ppermute | solution.py:490
  40.4 0.0 collective-permute-done.4.near_ref
  40.5 6.1 %collective-permute-start.5 = (f32[16,2048]{1,0:T(8,128)S(1)}, f32[16,2048]{1,0:T(8,128)S(1)}, u32[]{:S(2)}, u32[]{:S(2)}) collective-permute-start(f32[16,2048]{1,0:T(8,128)S(1)} %get-tuple-element.61), channel_id=1, source_target_pairs={{0,16},{16,0},{32,48},{48,32},{64,80},{80,64},{96,112},{112,96},{1... | collective-permute-start | bytes 393224 | tf_op jit(solution)/shard_map/ppermute | solution.py:501
  46.5 1.0 collective-permute-done.5.handed_ref
  47.5 7.1 %filter_gradients.1 = (bf16[128,2048]{1,0:T(8,128)(2,1)}, f32[16,384,128]{2,1,0:T(8,128)S(1)}, f32[24,2048]{1,0:T(8,128)S(1)}, f32[8,40,128]{2,1,0:T(8,128)S(1)}, f32[8,40,128]{2,1,0:T(8,128)S(1)}) custom-call(s32[10]{0:T(128)S(1)} %pad_add_fusion.spot_ref, f32[16,896,128]{2,1,0:T(8,128)S(1)} %get-tuple-element.46.save_ref, ...), custom_call_target="tpu_custom_call" | custom-call | flops 67108864 | bytes 8388608 | tf_op jit(solution)/shard_map/filter_gradients/pallas_call | solution.py:398
  54.6 2.3 %collective-permute-start.7 = (f32[24,2048]{1,0:T(8,128)S(1)}, f32[24,2048]{1,0:T(8,128)S(1)}, u32[]{:S(2)}, u32[]{:S(2)}) collective-permute-start(f32[24,2048]{1,0:T(8,128)S(1)} %get-tuple-element.65), channel_id=1, source_target_pairs={{16,0},{32,16},{48,32},{64,48},{80,64},{96,80},{112,96},{128,112},... | collective-permute-start | bytes 589832 | tf_op jit(solution)/shard_map/ppermute | solution.py:506
  56.9 0.1 collective-permute-start.6
  57.0 1.4 %collective-permute-done.6 = f32[8,40,128]{2,1,0:T(8,128)S(1)} collective-permute-done((f32[8,40,128]{2,1,0:T(8,128)S(1)}, f32[8,40,128]{2,1,0:T(8,128)S(1)}, u32[]{:S(2)}, u32[]{:S(2)}) %collective-permute-start.6) | collective-permute-done | bytes 163872 | tf_op jit(solution)/shard_map/ppermute | solution.py:509
  58.3 3.2 %collective-permute-done.7.edge_ref = f32[24,2048]{1,0:T(8,128)S(1)} collective-permute-done((f32[24,2048]{1,0:T(8,128)S(1)}, f32[24,2048]{1,0:T(8,128)S(1)}, u32[]{:S(2)}, u32[]{:S(2)}) %collective-permute-start.7) | collective-permute-done | bytes 196640 | tf_op jit(solution)/shard_map/ppermute | solution.py:506
  61.6 3.0 %collective-permute-start.8 = (f32[4,40,128]{2,1,0:T(8,128)S(1)}, f32[4,40,128]{2,1,0:T(8,128)S(1)}, u32[]{:S(2)}, u32[]{:S(2)}) collective-permute-start(f32[4,40,128]{2,1,0:T(8,128)S(1)} %slice.29), channel_id=1, source_target_pairs={{0,2},{1,3},{2,0},{3,1},{4,6},{5,7},{6,4},{7,5},{8,10},{9,11},{10,... | collective-permute-start | bytes 245768 | tf_op jit(solution)/shard_map/ppermute | solution.py:509
  64.6 1.9 %collective-permute-done.8 = f32[4,40,128]{2,1,0:T(8,128)S(1)} collective-permute-done((f32[4,40,128]{2,1,0:T(8,128)S(1)}, f32[4,40,128]{2,1,0:T(8,128)S(1)}, u32[]{:S(2)}, u32[]{:S(2)}) %collective-permute-start.8) | collective-permute-done | bytes 81952 | tf_op jit(solution)/shard_map/ppermute | solution.py:509
  66.5 1.4 %collective-permute-start.9 = (f32[2,40,128]{2,1,0:T(8,128)S(1)}, f32[2,40,128]{2,1,0:T(8,128)S(1)}, u32[]{:S(2)}, u32[]{:S(2)}) collective-permute-start(f32[2,40,128]{2,1,0:T(8,128)S(1)} %slice.31), channel_id=1, source_target_pairs={{0,1},{1,0},{2,3},{3,2},{4,5},{5,4},{6,7},{7,6},{8,9},{9,8},{10,11... | collective-permute-start | bytes 122888 | tf_op jit(solution)/shard_map/ppermute | solution.py:509
  67.9 1.6 %collective-permute-done.9 = f32[2,40,128]{2,1,0:T(8,128)S(1)} collective-permute-done((f32[2,40,128]{2,1,0:T(8,128)S(1)}, f32[2,40,128]{2,1,0:T(8,128)S(1)}, u32[]{:S(2)}, u32[]{:S(2)}) %collective-permute-start.9) | collective-permute-done | bytes 40992 | tf_op jit(solution)/shard_map/ppermute | solution.py:509
  69.5 1.1 %collective-permute-start.10 = (f32[2,40,128]{2,1,0:T(8,128)S(1)}, f32[2,40,128]{2,1,0:T(8,128)S(1)}, u32[]{:S(2)}, u32[]{:S(2)}) collective-permute-start(f32[2,40,128]{2,1,0:T(8,128)S(1)} %slice_add_fusion.1), channel_id=1, source_target_pairs={{0,32},{16,48},{32,0},{48,16},{64,96},{80,112},{96,64},{112,80},{1... | collective-permute-start | bytes 122888 | tf_op jit(solution)/shard_map/ppermute | solution.py:509
  70.6 2.4 %input_gradient.3 = bf16[128,2048]{1,0:T(8,128)(2,1)} custom-call(s32[10]{0:T(128)S(1)} %pad_add_fusion.spot_ref, f32[16,384,128]{2,1,0:T(8,128)S(1)} %get-tuple-element.69.gfeat_ref, f32[24,2048]{1,0:T(8,128)S(1)} %collective-permute-done.7.edge_ref, f32[3,7,2048]{2,1,0:T(8,128)S(1)} %get-tuple-element.71.taps_ref), custom_call_target="tpu_custom_call" | custom-call | flops 67108864 | bytes 8388608 | tf_op jit(solution)/shard_map/input_gradient/pallas_call | solution.py:398
  73.0 0.0 collective-permute-done.10
  73.0 0.6 collective-permute-start.11
  73.6 2.4 %input_gradient.4 = bf16[128,2048]{1,0:T(8,128)(2,1)} custom-call(s32[10]{0:T(128)S(1)} %pad_add_fusion.spot_ref, f32[16,384,128]{2,1,0:T(8,128)S(1)} %get-tuple-element.69.gfeat_ref, f32[24,2048]{1,0:T(8,128)S(1)} %collective-permute-done.7.edge_ref, f32[3,7,2048]{2,1,0:T(8,128)S(1)} %get-tuple-element.71.taps_ref), custom_call_target="tpu_custom_call" | custom-call | flops 67108864 | bytes 8388608 | tf_op jit(solution)/shard_map/input_gradient/pallas_call | solution.py:398
  76.1 1.2 %collective-permute-done.11 = f32[2,40,128]{2,1,0:T(8,128)S(1)} collective-permute-done((f32[2,40,128]{2,1,0:T(8,128)S(1)}, f32[2,40,128]{2,1,0:T(8,128)S(1)}, u32[]{:S(2)}, u32[]{:S(2)}) %collective-permute-start.11) | collective-permute-done | bytes 40992 | tf_op jit(solution)/shard_map/ppermute | solution.py:509
  77.3 1.5 %collective-permute-start.12 = (f32[2,40,128]{2,1,0:T(8,128)S(1)}, f32[2,40,128]{2,1,0:T(8,128)S(1)}, u32[]{:S(2)}, u32[]{:S(2)}) collective-permute-start(f32[2,40,128]{2,1,0:T(8,128)S(1)} %add.22), channel_id=1, source_target_pairs={{0,128},{16,144},{32,160},{48,176},{64,192},{80,208},{96,224},{112... | collective-permute-start | bytes 122888 | tf_op jit(solution)/shard_map/ppermute | solution.py:509
  78.9 2.4 %input_gradient.5 = bf16[128,2048]{1,0:T(8,128)(2,1)} custom-call(s32[10]{0:T(128)S(1)} %pad_add_fusion.spot_ref, f32[16,384,128]{2,1,0:T(8,128)S(1)} %get-tuple-element.69.gfeat_ref, f32[24,2048]{1,0:T(8,128)S(1)} %collective-permute-done.7.edge_ref, f32[3,7,2048]{2,1,0:T(8,128)S(1)} %get-tuple-element.71.taps_ref), custom_call_target="tpu_custom_call" | custom-call | flops 67108864 | bytes 8388608 | tf_op jit(solution)/shard_map/input_gradient/pallas_call | solution.py:398
  81.3 3.2 %collective-permute-done.12 = f32[2,40,128]{2,1,0:T(8,128)S(1)} collective-permute-done((f32[2,40,128]{2,1,0:T(8,128)S(1)}, f32[2,40,128]{2,1,0:T(8,128)S(1)}, u32[]{:S(2)}, u32[]{:S(2)}) %collective-permute-start.12) | collective-permute-done | bytes 40992 | tf_op jit(solution)/shard_map/ppermute | solution.py:509
  84.5 1.3 %collective-permute-start.13 = (f32[2,40,128]{2,1,0:T(8,128)S(1)}, f32[2,40,128]{2,1,0:T(8,128)S(1)}, u32[]{:S(2)}, u32[]{:S(2)}) collective-permute-start(f32[2,40,128]{2,1,0:T(8,128)S(1)} %add.23), channel_id=1, source_target_pairs={{0,1},{1,0},{2,3},{3,2},{4,5},{5,4},{6,7},{7,6},{8,9},{9,8},{10,11... | collective-permute-start | bytes 122888 | tf_op jit(solution)/shard_map/ppermute | solution.py:509
  85.8 1.9 %collective-permute-done.13 = f32[2,40,128]{2,1,0:T(8,128)S(1)} collective-permute-done((f32[2,40,128]{2,1,0:T(8,128)S(1)}, f32[2,40,128]{2,1,0:T(8,128)S(1)}, u32[]{:S(2)}, u32[]{:S(2)}) %collective-permute-start.13) | collective-permute-done | bytes 40992 | tf_op jit(solution)/shard_map/ppermute | solution.py:509
  87.7 2.9 %collective-permute-start.14 = (f32[4,40,128]{2,1,0:T(8,128)S(1)}, f32[4,40,128]{2,1,0:T(8,128)S(1)}, u32[]{:S(2)}, u32[]{:S(2)}) collective-permute-start(f32[4,40,128]{2,1,0:T(8,128)S(1)} %pad_maximum_fusion.2), channel_id=1, source_target_pairs={{0,2},{1,3},{2,0},{3,1},{4,6},{5,7},{6,4},{7,5},{8,10},{9,11},{10,... | collective-permute-start | bytes 245768 | tf_op jit(solution)/shard_map/ppermute | solution.py:509
  90.6 1.9 %collective-permute-done.14 = f32[4,40,128]{2,1,0:T(8,128)S(1)} collective-permute-done((f32[4,40,128]{2,1,0:T(8,128)S(1)}, f32[4,40,128]{2,1,0:T(8,128)S(1)}, u32[]{:S(2)}, u32[]{:S(2)}) %collective-permute-start.14) | collective-permute-done | bytes 81952 | tf_op jit(solution)/shard_map/ppermute | solution.py:509
  92.5 6.0 %collective-permute-start.15 = (f32[8,40,128]{2,1,0:T(8,128)S(1)}, f32[8,40,128]{2,1,0:T(8,128)S(1)}, u32[]{:S(2)}, u32[]{:S(2)}) collective-permute-start(f32[8,40,128]{2,1,0:T(8,128)S(1)} %pad_maximum_fusion.kept_ref), channel_id=1, source_target_pairs={{0,16},{16,0},{32,48},{48,32},{64,80},{80,64},{96,112},{112,96},{1... | collective-permute-start | bytes 491528 | tf_op jit(solution)/shard_map/ppermute | solution.py:509
  98.5 1.0 %collective-permute-done.15.away_ref = f32[8,40,128]{2,1,0:T(8,128)S(1)} collective-permute-done((f32[8,40,128]{2,1,0:T(8,128)S(1)}, f32[8,40,128]{2,1,0:T(8,128)S(1)}, u32[]{:S(2)}, u32[]{:S(2)}) %collective-permute-start.15) | collective-permute-done | bytes 163872 | tf_op jit(solution)/shard_map/ppermute | solution.py:509
  99.5 1.9 %parameter_gradients.1 = (f32[3,7,2048]{2,1,0:T(8,128)}, f32[16,2048]{1,0:T(8,128)}, f32[1,2048]{1,0:T(1,128)}) custom-call(s32[10]{0:T(128)S(1)} %pad_add_fusion.spot_ref, f32[8,40,128]{2,1,0:T(8,128)S(1)} %pad_maximum_fusion.kept_ref, f32[8,40,128]{2,1,0:T(8,128)S(1)} %collective-permute-done.15.away_ref), custom_call_target="tpu_custom_call" | custom-call | flops 67108864 | bytes 8388608 | tf_op jit(solution)/shard_map/parameter_gradients/pallas_call | solution.py:398
  (15 shorter events, 0.2 us)
Async XLA Ops:
  2.2 6.6 %collective-permute-start = (bf16[24,2048]{1,0:T(8,128)(2,1)S(1)}, bf16[24,2048]{1,0:T(8,128)(2,1)S(1)}, u32[]{:S(2)}, u32[]{:S(2)}) collective-permute-start(bf16[24,2048]{1,0:T(8,128)(2,1)S(1)} %pad_maximum_fusion.1), channel_id=1, source_target_pairs={{0,16},{16,32},{32,48},{48,64},{64,80},{80,96},{96,112},{112,128},... | collective-permute-start | bytes 294920 | tf_op jit(solution)/shard_map/ppermute | solution.py:480
  18.7 1.4 %collective-permute-start.1 = (f32[16,2048]{1,0:T(8,128)S(1)}, f32[16,2048]{1,0:T(8,128)S(1)}, u32[]{:S(2)}, u32[]{:S(2)}) collective-permute-start(f32[16,2048]{1,0:T(8,128)S(1)} %get-tuple-element.47.sent_ref), channel_id=1, source_target_pairs={{0,16},{16,0},{32,48},{48,32},{64,80},{80,64},{96,112},{112,96},{1... | collective-permute-start | bytes 393224 | tf_op jit(solution)/shard_map/ppermute | solution.py:492
  20.2 6.4 %collective-permute-start.2 = (f32[16,2048]{1,0:T(8,128)S(1)}, f32[16,2048]{1,0:T(8,128)S(1)}, u32[]{:S(2)}, u32[]{:S(2)}) collective-permute-start(f32[16,2048]{1,0:T(8,128)S(1)} %combine.2.first_ref), channel_id=1, source_target_pairs={{0,32},{32,64},{48,16},{64,96},{80,48},{96,128},{112,80},{128,160}... | collective-permute-start | bytes 393224 | tf_op jit(solution)/shard_map/ppermute | solution.py:490
  26.6 13.8 %collective-permute-start.3 = (f32[16,2048]{1,0:T(8,128)S(1)}, f32[16,2048]{1,0:T(8,128)S(1)}, u32[]{:S(2)}, u32[]{:S(2)}) collective-permute-start(f32[16,2048]{1,0:T(8,128)S(1)} %combine.3), channel_id=1, source_target_pairs={{0,96},{32,128},{64,160},{96,192},{112,16},{128,224},{144,48},{176... | collective-permute-start | bytes 393224 | tf_op jit(solution)/shard_map/ppermute | solution.py:490
  27.9 12.5 %collective-permute-start.4 = (f32[16,2048]{1,0:T(8,128)S(1)}, f32[16,2048]{1,0:T(8,128)S(1)}, u32[]{:S(2)}, u32[]{:S(2)}) collective-permute-start(f32[16,2048]{1,0:T(8,128)S(1)} %combine.3), channel_id=1, source_target_pairs={{0,32},{32,64},{48,16},{64,96},{80,48},{96,128},{112,80},{128,160}... | collective-permute-start | bytes 393224 | tf_op jit(solution)/shard_map/ppermute | solution.py:490
  40.5 7.1 %collective-permute-start.5 = (f32[16,2048]{1,0:T(8,128)S(1)}, f32[16,2048]{1,0:T(8,128)S(1)}, u32[]{:S(2)}, u32[]{:S(2)}) collective-permute-start(f32[16,2048]{1,0:T(8,128)S(1)} %get-tuple-element.61), channel_id=1, source_target_pairs={{0,16},{16,0},{32,48},{48,32},{64,80},{80,64},{96,112},{112,96},{1... | collective-permute-start | bytes 393224 | tf_op jit(solution)/shard_map/ppermute | solution.py:501
  54.6 7.0 %collective-permute-start.7 = (f32[24,2048]{1,0:T(8,128)S(1)}, f32[24,2048]{1,0:T(8,128)S(1)}, u32[]{:S(2)}, u32[]{:S(2)}) collective-permute-start(f32[24,2048]{1,0:T(8,128)S(1)} %get-tuple-element.65), channel_id=1, source_target_pairs={{16,0},{32,16},{48,32},{64,48},{80,64},{96,80},{112,96},{128,112},... | collective-permute-start | bytes 589832 | tf_op jit(solution)/shard_map/ppermute | solution.py:506
  56.9 1.5 %collective-permute-start.6 = (f32[8,40,128]{2,1,0:T(8,128)S(1)}, f32[8,40,128]{2,1,0:T(8,128)S(1)}, u32[]{:S(2)}, u32[]{:S(2)}) collective-permute-start(f32[8,40,128]{2,1,0:T(8,128)S(1)} %get-tuple-element.64), channel_id=1, source_target_pairs={{0,16},{16,0},{32,48},{48,32},{64,80},{80,64},{96,112},{112,96},{1... | collective-permute-start | bytes 491528 | tf_op jit(solution)/shard_map/ppermute | solution.py:509
  61.6 4.9 %collective-permute-start.8 = (f32[4,40,128]{2,1,0:T(8,128)S(1)}, f32[4,40,128]{2,1,0:T(8,128)S(1)}, u32[]{:S(2)}, u32[]{:S(2)}) collective-permute-start(f32[4,40,128]{2,1,0:T(8,128)S(1)} %slice.29), channel_id=1, source_target_pairs={{0,2},{1,3},{2,0},{3,1},{4,6},{5,7},{6,4},{7,5},{8,10},{9,11},{10,... | collective-permute-start | bytes 245768 | tf_op jit(solution)/shard_map/ppermute | solution.py:509
  66.5 2.9 %collective-permute-start.9 = (f32[2,40,128]{2,1,0:T(8,128)S(1)}, f32[2,40,128]{2,1,0:T(8,128)S(1)}, u32[]{:S(2)}, u32[]{:S(2)}) collective-permute-start(f32[2,40,128]{2,1,0:T(8,128)S(1)} %slice.31), channel_id=1, source_target_pairs={{0,1},{1,0},{2,3},{3,2},{4,5},{5,4},{6,7},{7,6},{8,9},{9,8},{10,11... | collective-permute-start | bytes 122888 | tf_op jit(solution)/shard_map/ppermute | solution.py:509
  69.5 3.6 %collective-permute-start.10 = (f32[2,40,128]{2,1,0:T(8,128)S(1)}, f32[2,40,128]{2,1,0:T(8,128)S(1)}, u32[]{:S(2)}, u32[]{:S(2)}) collective-permute-start(f32[2,40,128]{2,1,0:T(8,128)S(1)} %slice_add_fusion.1), channel_id=1, source_target_pairs={{0,32},{16,48},{32,0},{48,16},{64,96},{80,112},{96,64},{112,80},{1... | collective-permute-start | bytes 122888 | tf_op jit(solution)/shard_map/ppermute | solution.py:509
  73.0 4.3 %collective-permute-start.11 = (f32[2,40,128]{2,1,0:T(8,128)S(1)}, f32[2,40,128]{2,1,0:T(8,128)S(1)}, u32[]{:S(2)}, u32[]{:S(2)}) collective-permute-start(f32[2,40,128]{2,1,0:T(8,128)S(1)} %add.21), channel_id=1, source_target_pairs={{0,64},{16,80},{32,96},{48,112},{64,0},{80,16},{96,32},{112,48},{1... | collective-permute-start | bytes 122888 | tf_op jit(solution)/shard_map/ppermute | solution.py:509
  77.3 7.2 %collective-permute-start.12 = (f32[2,40,128]{2,1,0:T(8,128)S(1)}, f32[2,40,128]{2,1,0:T(8,128)S(1)}, u32[]{:S(2)}, u32[]{:S(2)}) collective-permute-start(f32[2,40,128]{2,1,0:T(8,128)S(1)} %add.22), channel_id=1, source_target_pairs={{0,128},{16,144},{32,160},{48,176},{64,192},{80,208},{96,224},{112... | collective-permute-start | bytes 122888 | tf_op jit(solution)/shard_map/ppermute | solution.py:509
  84.5 3.1 %collective-permute-start.13 = (f32[2,40,128]{2,1,0:T(8,128)S(1)}, f32[2,40,128]{2,1,0:T(8,128)S(1)}, u32[]{:S(2)}, u32[]{:S(2)}) collective-permute-start(f32[2,40,128]{2,1,0:T(8,128)S(1)} %add.23), channel_id=1, source_target_pairs={{0,1},{1,0},{2,3},{3,2},{4,5},{5,4},{6,7},{7,6},{8,9},{9,8},{10,11... | collective-permute-start | bytes 122888 | tf_op jit(solution)/shard_map/ppermute | solution.py:509
  87.7 4.8 %collective-permute-start.14 = (f32[4,40,128]{2,1,0:T(8,128)S(1)}, f32[4,40,128]{2,1,0:T(8,128)S(1)}, u32[]{:S(2)}, u32[]{:S(2)}) collective-permute-start(f32[4,40,128]{2,1,0:T(8,128)S(1)} %pad_maximum_fusion.2), channel_id=1, source_target_pairs={{0,2},{1,3},{2,0},{3,1},{4,6},{5,7},{6,4},{7,5},{8,10},{9,11},{10,... | collective-permute-start | bytes 245768 | tf_op jit(solution)/shard_map/ppermute | solution.py:509
  92.5 7.0 %collective-permute-start.15 = (f32[8,40,128]{2,1,0:T(8,128)S(1)}, f32[8,40,128]{2,1,0:T(8,128)S(1)}, u32[]{:S(2)}, u32[]{:S(2)}) collective-permute-start(f32[8,40,128]{2,1,0:T(8,128)S(1)} %pad_maximum_fusion.kept_ref), channel_id=1, source_target_pairs={{0,16},{16,0},{32,48},{48,32},{64,80},{80,64},{96,112},{112,96},{1... | collective-permute-start | bytes 491528 | tf_op jit(solution)/shard_map/ppermute | solution.py:509

commit v3 on v2

--- a/solution.py
+++ b/solution.py
@@ -19,9 +19,10 @@
 BF16 = jnp.bfloat16
 VMEM_BYTES = 12 << 20
 CHUNKS = 4
-RAW, FEAT, COT = 0, 3, 6
+COT = 3
 SOURCE, GRAD, GSEG, SLOC, RLOC = range(5)
 CONV, BACK, SWT, RWT, SCOEF, RCOEF = range(6)
+NEAR_TERMS, FAR_TERMS, CONV_ROWS, BACK_ROWS, FIRST_ROWS = 0, HALO * MODES, 2 * HALO * MODES, 2 * HALO * MODES + 8, 208
 
 
 def slab(block, index):
@@ -92,16 +93,14 @@
     }
 
 
-def feature_kernel(
-    spot_ref, q_ref, k_ref, v_ref, cot_ref, taps_in, rate_in, residue_in, skip_in, halo_ref,
-    save_ref, pre_ref, own_ref, sent_ref, pass_ref, taps_ref, rate_ref, residue_ref, skip_ref,
-    stage, masks, open_mask, end_mask, chain, columns, arrived, loaded,
+def stage_kernel(
+    spot_ref, q_ref, k_ref, v_ref, cot_ref, taps_in, rate_in, residue_in, skip_in,
+    raw_ref, masks, open_mask, end_mask, chain, taps_ref, rate_ref, residue_ref, skip_ref,
+    stage, columns, arrived, loaded,
 ):
-    starts, here = starts_of(spot_ref), spot_ref[0]
-    anchor, core, chip = here * ROWS, here % 2, here // 2
-
     inputs = (q_ref, k_ref, v_ref, cot_ref)
     chunk = columns.shape[2] // CHUNKS
+    starts, anchor = starts_of(spot_ref), spot_ref[0] * ROWS
 
     def fetch(which, part):
         cols = pl.ds(pl.multiple_of(part * chunk, LANES), chunk)
@@ -113,14 +112,12 @@
             ((taps_in, taps_ref), (rate_in, rate_ref), (residue_in, residue_ref), (skip_in, skip_ref))
         )
     ]
-    for which in range(4):
-        fetch(which, 0).start()
+    for part in range(CHUNKS):
+        for which in range(4):
+            fetch(which, part).start()
     for copy in parameters:
         copy.start()
-    for part in range(1, CHUNKS):
-        for which in range(4):
-            fetch(which, part).start()
-    store_masks(starts, anchor, masks, STEPS, HALO)
+    store_masks(starts, anchor, masks, STEPS + HALO, HALO)
     store_edge_masks(starts, anchor, open_mask, end_mask)
     for k in range(3):
         span = STEPS << k
@@ -130,8 +127,28 @@
         at_end = since_start(starts, anchor + ahead * STEPS - 1)
         chain[3 + k] = flag((at_end >= span) & (segments() + (1 << k) < SEGS))
 
+    def tile_body(tile, lanes):
+        @pl.when(tile % (chunk // LANES) == 0)
+        def _():
+            for which in range(4):
+                fetch(which, tile // (chunk // LANES)).wait()
+
+        for which in range(4):
+            rows = fetch_columns(columns.at[which], stage.at[which], lanes)
+            for t in range(STEPS):
+                raw_ref[tile, slab(which, t)] = rows[t]
+
+    each_tile(raw_ref.shape[0], tile_body)
     for copy in parameters:
         copy.wait()
+
+
+def feature_kernel(
+    spot_ref, raw_ref, masks, open_mask, end_mask, chain, taps_ref, rate_ref, halo_ref,
+    feat_ref, pre_ref, own_ref, sent_ref, pass_ref,
+):
+    starts, here = starts_of(spot_ref), spot_ref[0]
+    anchor, core, chip = here * ROWS, here % 2, here // 2
 
     def passes(position, span):
         return flag(since_start(starts, position) >= span)
@@ -146,28 +163,19 @@
     def tile_body(tile, lanes):
         segment = segments()
         first, last = segment == 0, segment == SEGS - 1
-
-        @pl.when(tile % (chunk // LANES) == 0)
-        def _():
-            for which in range(4):
-                fetch(which, tile // (chunk // LANES)).wait()
-
         for branch in range(3):
-            rows = fetch_columns(columns.at[branch], stage.at[branch], lanes)
+            rows = [raw_ref[tile, slab(branch, t)] for t in range(STEPS)]
             before = rows_before(rows, halo_ref, branch, lanes)
             taps = [jnp.broadcast_to(taps_ref[branch, j : j + 1, lanes], (SEGS, LANES)) for j in range(TAPS)]
             for t in range(STEPS):
-                save_ref[tile, slab(RAW + branch, t)] = rows[t]
                 total = taps[0] * rows[t]
                 for j in range(1, TAPS):
                     earlier = rows[t - j] if t >= j else before[t - j]
                     total = total + taps[j] * (earlier * masks[j - 1, t])
-                save_ref[tile, slab(FEAT + branch, t)] = total
-        upstream = fetch_columns(columns.at[3], stage.at[3], lanes)
+                feat_ref[tile, slab(branch, t)] = total
         for t in range(STEPS):
-            save_ref[tile, slab(COT, t)] = upstream[t]
-            pre_ref[tile, slab(SOURCE, t)] = save_ref[tile, slab(FEAT + 1, t)] * save_ref[tile, slab(FEAT + 2, t)]
-            pre_ref[tile, slab(GRAD, t)] = upstream[t] * save_ref[tile, slab(FEAT, t)]
+            pre_ref[tile, slab(SOURCE, t)] = feat_ref[tile, slab(1, t)] * feat_ref[tile, slab(2, t)]
+            pre_ref[tile, slab(GRAD, t)] = raw_ref[tile, slab(COT, t)] * feat_ref[tile, slab(0, t)]
         for low in range(0, MODES, 8):
             modes = range(low, low + 8)
             decay = [jnp.exp(-row(rate_ref, m, lanes)) for m in modes]
@@ -198,12 +206,12 @@
         pass_ref[2, :, lanes] = chip_pass * power
         pass_ref[3, :, lanes] = far_pass * (power * power)
 
-    each_tile(save_ref.shape[0], tile_body)
+    each_tile(raw_ref.shape[0], tile_body)
 
 
 def local_kernel(
-    spot_ref, pre_ref, rate_ref, residue_ref, skip_ref,
-    post_ref, local_ref,
+    spot_ref, pre_ref, rate_ref, residue_ref, skip_ref, open_mask, end_mask,
+    post_ref, local_ref, first_ref,
     masks, reach, stage, weight_stage,
 ):
     starts, anchor = starts_of(spot_ref), spot_ref[0] * ROWS
@@ -242,6 +250,18 @@
         for t in range(STEPS):
             post_ref[tile, slab(CONV, t)] = conv[t]
             post_ref[tile, slab(BACK, t)] = back[t]
+        scaled = [weight_stage[...]]
+        for t in range(1, STEPS):
+            scaled.append(scaled[-1] * decay)
+        later = pre_ref[tile, pl.ds(RLOC * ROWS, MODES, stride=SEGS), :]
+        beyond = reach[1, :1] * jnp.exp(rates * -float(ROWS - STEPS))
+        for t in range(HALO):
+            far_term = end_mask[t, :1] * scaled[STEPS - 1 - t]
+            first_ref[tile, NEAR_TERMS + t * MODES : NEAR_TERMS + (t + 1) * MODES] = open_mask[t, :1] * scaled[t]
+            first_ref[tile, FAR_TERMS + t * MODES : FAR_TERMS + (t + 1) * MODES] = far_term * beyond
+            back_row = back[t][:1] + jnp.sum(far_term * later, axis=0, keepdims=True)
+            first_ref[tile, CONV_ROWS + t : CONV_ROWS + t + 1] = conv[t][:1]
+            first_ref[tile, BACK_ROWS + t : BACK_ROWS + t + 1] = back_row
         total = jnp.broadcast_to(paired[STEPS - 1], (MODES, LANES))
         for gap in range(STEPS - 2, -1, -1):
             total = total * decay + paired[gap]
@@ -276,60 +296,76 @@
     return half, high * 4 + low * 2 + slot % 2
 
 
+def edge_kernel(
+    spot_ref, raw_ref, feat_ref, first_ref, arrived_ref, handed_ref, enter_ref, return_ref, edge_ref
+):
+    lower = spot_ref[0] % 2 == 0
+
+    def tile_body(tile, lanes):
+        arrived, handed = arrived_ref[:, lanes], handed_ref[:, lanes]
+        entering, returning = jnp.where(lower, arrived, handed), jnp.where(lower, handed, arrived)
+        enter_ref[:, lanes] = entering
+        return_ref[:, lanes] = returning
+        for t in range(HALO):
+            near = first_ref[tile, NEAR_TERMS + t * MODES : NEAR_TERMS + (t + 1) * MODES]
+            far = first_ref[tile, FAR_TERMS + t * MODES : FAR_TERMS + (t + 1) * MODES]
+            filtered = first_ref[tile, CONV_ROWS + t : CONV_ROWS + t + 1]
+            filtered = filtered + jnp.sum(near * entering, axis=0, keepdims=True)
+            grad = first_ref[tile, BACK_ROWS + t : BACK_ROWS + t + 1]
+            grad = grad + jnp.sum(far * returning, axis=0, keepdims=True)
+            edge_ref[t : t + 1, lanes] = raw_ref[tile, slab(COT, t)][:1] * filtered
+            edge_ref[8 + t : 9 + t, lanes] = grad * feat_ref[tile, slab(2, t)][:1]
+            edge_ref[16 + t : 17 + t, lanes] = grad * feat_ref[tile, slab(1, t)][:1]
+        for branch in range(3):
+            edge_ref[branch * 8 + HALO : branch * 8 + 8, lanes] = jnp.zeros((8 - HALO, LANES), F32)
+
+    each_tile(raw_ref.shape[0], tile_body)
+
+
 def gradient_kernel(
-    spot_ref, save_ref, post_ref, local_ref, arrived_ref, handed_ref, own_ref, sent_ref, rate_ref, halo_ref,
-    out_ref, gfeat_ref, edge_ref, kept_ref, away_ref,
-    stage, masks, open_mask, end_mask, parts,
+    spot_ref, raw_ref, feat_ref, post_ref, local_ref, enter_ref, return_ref, own_ref, sent_ref, rate_ref, halo_ref,
+    masks, open_mask, end_mask,
+    out_ref, gfeat_ref, kept_ref, away_ref,
+    stage,
 ):
-    starts, anchor = starts_of(spot_ref), spot_ref[0] * ROWS
     lower = spot_ref[0] % 2 == 0
 
-    store_masks(starts, anchor, masks, STEPS, HALO)
-    store_edge_masks(starts, anchor, open_mask, end_mask)
-
     def tile_body(tile, lanes):
         decay = [jnp.exp(-row(rate_ref, m, lanes)) for m in range(MODES)]
-        arrived, handed = arrived_ref[:, lanes], handed_ref[:, lanes]
-        entering = jnp.where(lower, arrived, handed)
-        parts[0:MODES] = entering
-        parts[MODES:] = jnp.where(lower, handed, arrived)
         state = [
-            post_ref[tile, slab(SWT, m)] + post_ref[tile, slab(SCOEF, m)] * row(parts, m, slice(None))
+            post_ref[tile, slab(SWT, m)] + post_ref[tile, slab(SCOEF, m)] * row(enter_ref, m, lanes)
             for m in range(MODES)
         ]
         for t in range(STEPS):
             filtered = post_ref[tile, slab(CONV, t)] + open_mask[t] * tree_sum(state)
-            stage[pl.ds(t, SEGS, stride=STEPS), :] = save_ref[tile, slab(FEAT, t)] * filtered
-            gfeat_ref[tile, slab(0, t)] = save_ref[tile, slab(COT, t)] * filtered
+            stage[pl.ds(t, SEGS, stride=STEPS), :] = feat_ref[tile, slab(0, t)] * filtered
+            gfeat_ref[tile, slab(0, t)] = raw_ref[tile, slab(COT, t)] * filtered
             if t < STEPS - 1:
                 state = [d * s for d, s in zip(decay, state)]
         out_ref[:, lanes] = stage[...].astype(out_ref.dtype)
         state = [
-            post_ref[tile, slab(RWT, m)] + post_ref[tile, slab(RCOEF, m)] * row(parts, MODES + m, slice(None))
+            post_ref[tile, slab(RWT, m)] + post_ref[tile, slab(RCOEF, m)] * row(return_ref, m, lanes)
             for m in range(MODES)
         ]
         for t in range(STEPS - 1, -1, -1):
             grad = post_ref[tile, slab(BACK, t)] + end_mask[t] * tree_sum(state)
-            gfeat_ref[tile, slab(1, t)] = grad * save_ref[tile, slab(FEAT + 2, t)]
-            gfeat_ref[tile, slab(2, t)] = grad * save_ref[tile, slab(FEAT + 1, t)]
+            gfeat_ref[tile, slab(1, t)] = grad * feat_ref[tile, slab(2, t)]
+            gfeat_ref[tile, slab(2, t)] = grad * feat_ref[tile, slab(1, t)]
             if t:
                 state = [d * s for d, s in zip(decay, state)]
         rates = rate_ref[:, lanes]
         begin = jnp.where(lower, sent_ref[:, lanes], own_ref[:, lanes])
-        sums = [jnp.sqrt(rates) * (local_ref[tile, 0:MODES] + entering * jnp.exp(-rates) * begin)]
+        sums = [jnp.sqrt(rates) * (local_ref[tile, 0:MODES] + enter_ref[:, lanes] * jnp.exp(-rates) * begin)]
         for branch in range(3):
             totals = [jnp.zeros((SEGS, LANES), F32)] * TAPS
-            rows = [save_ref[tile, slab(RAW + branch, t)] for t in range(STEPS)]
+            rows = [raw_ref[tile, slab(branch, t)] for t in range(STEPS)]
             before = rows_before(rows, halo_ref, branch, lanes)
             for t in range(STEPS):
                 grad = gfeat_ref[tile, slab(branch, t)]
-                if t < HALO:
-                    edge_ref[branch * 8 + t : branch * 8 + t + 1, lanes] = grad[:1]
                 totals[0] = totals[0] + grad * rows[t]
                 for j in range(1, TAPS):
                     earlier = rows[t - j] if t >= j else before[t - j]
                     totals[j] = totals[j] + (grad * masks[j - 1, t]) * earlier
-            edge_ref[branch * 8 + HALO : branch * 8 + 8, lanes] = jnp.zeros((8 - HALO, LANES), F32)
             sums += [jnp.sum(total, axis=0, keepdims=True) for total in totals]
         sums.append(local_ref[tile, MODES : MODES + REDUCED - MODES - 3 * TAPS])
         half, slot = tile_slot(tile, spot_ref)
@@ -342,11 +378,10 @@
                     ref[slot, at : at + piece.shape[0]] = piece
                     at += piece.shape[0]
 
-    each_tile(save_ref.shape[0], tile_body)
-
-
-def input_kernel(branch, spot_ref, gfeat_ref, edge_ref, taps_ref, out_ref, stage, masks):
-    store_masks(starts_of(spot_ref), spot_ref[0] * ROWS, masks, STEPS + HALO, HALO)
+    each_tile(raw_ref.shape[0], tile_body)
+
+
+def input_kernel(branch, gfeat_ref, edge_ref, taps_ref, masks, out_ref, stage):
 
     def tile_body(tile, lanes):
         last = segments() == SEGS - 1
@@ -389,7 +424,7 @@
 
 
 SMEM, VMEM, HBM = (pl.BlockSpec(memory_space=space) for space in (pltpu.SMEM, pltpu.VMEM, pltpu.HBM))
-MASKS = (HALO, STEPS, SEGS, LANES)
+MASKS = (HALO, STEPS + HALO, SEGS, LANES)
 EDGE_MASKS = (STEPS, SEGS, LANES)
 STAGE = (ROWS, LANES)
 
@@ -407,50 +442,68 @@
     )(*[x if spec is SMEM else pltpu.with_memory_space_constraint(x, spec.memory_space) for x, spec in zip(args, ins)])
 
 
-def features(spot, query, key, value, upstream, taps, rate, residue, skip, halo):
+def staged(spot, query, key, value, upstream, taps, rate, residue, skip):
     channels = query.shape[1]
-    tiles, states = channels // LANES, (MODES, channels)
+    return call(
+        stage_kernel, "stage",
+        [SMEM] + [HBM] * 8,
+        [(channels // LANES, 4 * ROWS, LANES), MASKS, EDGE_MASKS, EDGE_MASKS, (6, SEGS, LANES),
+         taps.shape, rate.shape, residue.shape, skip.shape],
+        [(4, *STAGE), pltpu.VMEM((4, ROWS, channels), BF16), pltpu.SemaphoreType.DMA((4, CHUNKS)),
+         pltpu.SemaphoreType.DMA((4,))],
+        spot, query, key, value, upstream, taps, rate, residue, skip,
+    )
+
+
+def features(spot, raw, masks, open_mask, end_mask, chain, taps, rate, halo):
+    tiles, states = raw.shape[0], rate.shape
     return call(
         feature_kernel, "features",
-        [SMEM] + [HBM] * 8 + [VMEM],
-        [(tiles, 7 * ROWS, LANES), (tiles, 5 * ROWS, LANES), states, states, (4, *states),
-         taps.shape, rate.shape, residue.shape, skip.shape],
-        [(4, *STAGE), MASKS, EDGE_MASKS, EDGE_MASKS, (6, SEGS, LANES),
-         pltpu.VMEM((4, ROWS, channels), BF16), pltpu.SemaphoreType.DMA((4, CHUNKS)), pltpu.SemaphoreType.DMA((4,))],
-        spot, query, key, value, upstream, taps, rate, residue, skip, halo,
-    )
-
-
-def local_filter(spot, pre, rate, residue, skip):
+        [SMEM] + [VMEM] * 8,
+        [(tiles, 3 * ROWS, LANES), (tiles, 5 * ROWS, LANES), states, states, (4, *states)],
+        [],
+        spot, raw, masks, open_mask, end_mask, chain, taps, rate, halo,
+    )
+
+
+def local_filter(spot, pre, rate, residue, skip, open_mask, end_mask):
     tiles = pre.shape[0]
     return call(
         local_kernel, "local_filter",
-        [SMEM, VMEM, VMEM, VMEM, VMEM],
-        [(tiles, 6 * ROWS, LANES), (tiles, MODES + 8, LANES)],
+        [SMEM] + [VMEM] * 6,
+        [(tiles, 6 * ROWS, LANES), (tiles, MODES + 8, LANES), (tiles, FIRST_ROWS, LANES)],
         [(STEPS - 1, STEPS, SEGS, LANES), (2, SEGS, LANES), (MODES, LANES), (MODES, LANES)],
-        spot, pre, rate, residue, skip,
-    )
-
-
-def filter_gradients(spot, save, post, local, arrived, handed, own, sent, rate, halo):
-    tiles, channels = save.shape[0], rate.shape[1]
+        spot, pre, rate, residue, skip, open_mask, end_mask,
+    )
+
+
+def edge_gradients(spot, raw, feat, first, arrived, handed):
+    states = arrived.shape
+    return call(
+        edge_kernel, "edge_gradients", [SMEM] + [VMEM] * 5, [states, states, (24, states[1])], [],
+        spot, raw, feat, first, arrived, handed,
+    )
+
+
+def filter_gradients(spot, raw, *others):
+    tiles = raw.shape[0]
     half = (tiles // 2, REDUCED, LANES)
     return call(
         gradient_kernel, "filter_gradients",
-        [SMEM] + [VMEM] * 9,
-        [jax.ShapeDtypeStruct((ROWS, channels), BF16), (tiles, 3 * ROWS, LANES), (24, channels), half, half],
-        [STAGE, MASKS, EDGE_MASKS, EDGE_MASKS, (2 * MODES, LANES)],
-        spot, save, post, local, arrived, handed, own, sent, rate, halo,
-    )
-
-
-def input_gradient(branch, spot, gfeat, edge, taps):
+        [SMEM] + [VMEM] * (1 + len(others)),
+        [jax.ShapeDtypeStruct((ROWS, tiles * LANES), BF16), (tiles, 3 * ROWS, LANES), half, half],
+        [STAGE],
+        spot, raw, *others,
+    )
+
+
+def input_gradient(branch, gfeat, edge, taps, masks):
     [made] = call(
         partial(input_kernel, branch), "input_gradient",
-        [SMEM, VMEM, VMEM, VMEM],
+        [VMEM] * 4,
         [jax.ShapeDtypeStruct((ROWS, taps.shape[2]), BF16)],
-        [STAGE, (HALO, STEPS + HALO, SEGS, LANES)],
-        spot, gfeat, edge, taps,
+        [STAGE],
+        gfeat, edge, taps, masks,
     )
     return made
 
@@ -478,10 +531,11 @@
 
     stacked = jnp.concatenate([x[0, ROWS - 8 :] for x in (query_rows, key_rows, value_rows)], axis=0)
     halo = lax.ppermute(stacked, "ctx", [(i, i + 1) for i in range(count - 1)]).astype(F32)
-    save, pre, own, sent, through, taps, rate, residue, skip = features(
+    raw, masks, open_mask, end_mask, chain, taps, rate, residue, skip = staged(
         spot, query_rows[0], key_rows[0], value_rows[0], cotangent[0],
-        short_filter, decay_rate.T, residue.T, skip_gain[None], halo,
-    )
+        short_filter, decay_rate.T, residue.T, skip_gain[None],
+    )
+    feat, pre, own, sent, through = features(spot, raw, masks, open_mask, end_mask, chain, taps, rate, halo)
 
     pairs = [(i, i ^ 1) for i in range(count)]
 
@@ -493,17 +547,19 @@
     chip_state = combine(2, chip_state, through, onward(chip_state, 1))
     chip_state, pre = lax.optimization_barrier((chip_state, pre))
     near, far = onward(chip_state, 1), onward(chip_state, 3)
-    post, local = local_filter(spot, pre, rate, residue, skip)
+    post, local, first = local_filter(spot, pre, rate, residue, skip, open_mask, end_mask)
     far, post = lax.optimization_barrier((far, post))
     arrived, handed = call(
         arrive_kernel, "arrive", [VMEM] * 4, [own.shape, own.shape], [], near, far, own, through
     )
     handed = lax.ppermute(handed, "ctx", pairs)
 
-    block_out, gfeat, edge, kept, away = filter_gradients(
-        spot, save, post, local, arrived, handed, own, sent, rate, halo
-    )
+    entering, returning, edge = edge_gradients(spot, raw, feat, first, arrived, handed)
     next_edge = lax.ppermute(edge, "ctx", [(i, i - 1) for i in range(1, count)])
+    block_out, gfeat, kept, away = filter_gradients(
+        spot, raw, feat, post, local, entering, returning, own, sent, rate, halo, masks, open_mask, end_mask
+    )
+    away, next_edge = lax.optimization_barrier((away, next_edge))
 
     def exchange(value, axis, flip):
         return lax.ppermute(value, axis, [(i, i ^ flip) for i in range(lax.axis_size(axis))])
@@ -512,13 +568,12 @@
 
     def exchange_beside(value, axis, flip):
         value, beside = lax.optimization_barrier((value, next_edge))
-        made = input_gradient(len(grad_inputs), spot, gfeat, beside, taps)
+        made = input_gradient(len(grad_inputs), gfeat, beside, taps, masks)
         sent, made = lax.optimization_barrier((exchange(value, axis, flip), made))
         grad_inputs.append(made)
         return sent
 
-    received, next_edge = lax.optimization_barrier((exchange(away, "ctx", 1), next_edge))
-    total = kept + received
+    total = kept + exchange(away, "ctx", 1)
     for flip in (2, 1):
         half = total.shape[0] // 2
         total = total[:half] + exchange(total[half:], "dp", flip)

time: 102 us -> 96.9 us (0.950)
  waiting for transfers between devices: 32.3 us -> 26 us
  starting transfers between devices: 35.2 us -> 37.1 us
    ppermute x1, waiting for transfers between devices: 3.23 us -> 0.01 us  [per_device(): next_edge = lax.ppermute(edge, 'ctx', [(i, i - 1) for i in range(1, count)])]
    ppermute x9, starting transfers between devices: 18 us -> 20.5 us  [exchange(): lax.ppermute(value, axis, [(i, i ^ flip) for i in range(lax.axis_size(axi...]
    ppermute x3, waiting for transfers between devices: 11.9 us -> 9.75 us  [onward(): lax.ppermute(value, 'ctx', [(i, j) for i, j in moves if 0 <= j < count])]
    pallas_call x10 -> x12, Pallas kernels: 30.7 us -> 30.3 us  [call(): pl.pallas_call(body, name=name, out_shape=[out if isinstance(out, jax.Sha...]
  transfers between devices with their start and end apart: 16 -> 16, of which waited for: 14 -> 13; matrix products, arithmetic and copies ran while one was open for 1% -> 1% of each run, Pallas kernels for 12% -> 22%
where the time goes in v3:
time: 96.9 us; the launch traced here: 96.5 us
  starting transfers between devices  37.1 us (38%)
  Pallas kernels  30.3 us (31%)
  waiting for transfers between devices  26 us (27%)
  local copies, waits for them, and re-layouts  1.55 us (2%)
    pallas_call x12, Pallas kernels, call(): pl.pallas_call(body, name=name, out_shape=[out if isinstance(out, jax.Sha...  30.3 us
    ppermute x9, starting transfers between devices, exchange(): lax.ppermute(value, axis, [(i, i ^ flip) for i in range(lax.axis_size(axi...  20.5 us
    ppermute x9, waiting for transfers between devices, exchange(): lax.ppermute(value, axis, [(i, i ^ flip) for i in range(lax.axis_size(axi...  13.9 us
    ppermute x3, waiting for transfers between devices, onward(): lax.ppermute(value, 'ctx', [(i, j) for i, j in moves if 0 <= j < count])  9.75 us
    ppermute x1, starting transfers between devices, per_device(): handed = lax.ppermute(handed, 'ctx', pairs)  5.37 us
    ppermute x1, starting transfers between devices, per_device(): lax.ppermute(stacked, 'ctx', [(i, i + 1) for i in range(count - 1)])  4.94 us
    ppermute x3, starting transfers between devices, onward(): lax.ppermute(value, 'ctx', [(i, j) for i, j in moves if 0 <= j < count])  3.88 us
    ppermute x1, starting transfers between devices, per_device(): next_edge = lax.ppermute(edge, 'ctx', [(i, i - 1) for i in range(1, count)])  2.27 us
  transfers between devices with their start and end apart: 16, of which 13 were waited for; matrix products, arithmetic and copies ran while one was open for 1% of the time, Pallas kernels for 22%

profile of v3, /device:TPU:1, one launch (start us, length us, event | category | flops | bytes accessed | tf_op | source)
XLA Modules:
  0.0 96.5 jit_solution(9980884556800475307)
XLA Ops:
  0.6 0.8 slice_bitcast_fusion.2
  1.4 0.8 slice_bitcast_fusion
  2.2 4.9 %collective-permute-start = (bf16[24,2048]{1,0:T(8,128)(2,1)S(1)}, bf16[24,2048]{1,0:T(8,128)(2,1)S(1)}, u32[]{:S(2)}, u32[]{:S(2)}) collective-permute-start(bf16[24,2048]{1,0:T(8,128)(2,1)S(1)} %pad_maximum_fusion.1), channel_id=1, source_target_pairs={{0,16},{16,32},{32,48},{48,64},{64,80},{80,96},{96,112},{112,128},... | collective-permute-start | bytes 294920 | tf_op jit(solution)/shard_map/ppermute | solution.py:533
  7.1 0.7 pad_add_fusion.spot_ref
  7.9 3.8 %stage.1 = (f32[16,512,128]{2,1,0:T(8,128)S(1)}, f32[6,22,8,128]{3,2,1,0:T(8,128)S(1)}, f32[16,8,128]{2,1,0:T(8,128)S(1)}, f32[16,8,128]{2,1,0:T(8,128)S(1)}, f3...) custom-call(s32[10]{0:T(128)S(1)} %pad_add_fusion.spot_ref, ...), custom_call_target="tpu_custom_call" | custom-call | flops 67108864 | bytes 8388608 | tf_op jit(solution)/shard_map/stage/pallas_call | solution.py:433
  11.6 0.0 collective-permute-done
  11.7 6.5 %features.1 = (f32[16,384,128]{2,1,0:T(8,128)S(1)}, f32[16,640,128]{2,1,0:T(8,128)S(1)}, f32[16,2048]{1,0:T(8,128)S(1)}, f32[16,2048]{1,0:T(8,128)S(1)}, f32[4,16,2048]{2,1,0:T(8,128)S(1)}) custom-call(s32[10]{0:T(128)S(1)} %pad_add_fusion.spot_ref, f32[16,512,128]{2,1,0:T(8,128)S(1)} %get-tuple-element.54.raw_ref, ...), custom_call_target="tpu_custom_call" | custom-call | flops 67108864 | bytes 8388608 | tf_op jit(solution)/shard_map/features/pallas_call | solution.py:433
  18.2 0.1 collective-permute-start.1
  18.3 1.3 %collective-permute-done.1.first_ref = f32[16,2048]{1,0:T(8,128)S(1)} collective-permute-done((f32[16,2048]{1,0:T(8,128)S(1)}, f32[16,2048]{1,0:T(8,128)S(1)}, u32[]{:S(2)}, u32[]{:S(2)}) %collective-permute-start.1) | collective-permute-done | bytes 131104 | tf_op jit(solution)/shard_map/ppermute | solution.py:546
  19.6 1.3 %collective-permute-start.2 = (f32[16,2048]{1,0:T(8,128)S(1)}, f32[16,2048]{1,0:T(8,128)S(1)}, u32[]{:S(2)}, u32[]{:S(2)}) collective-permute-start(f32[16,2048]{1,0:T(8,128)S(1)} %combine.2.first_ref), channel_id=1, source_target_pairs={{0,32},{32,64},{48,16},{64,96},{80,48},{96,128},{112,80},{128,160}... | collective-permute-start | bytes 393224 | tf_op jit(solution)/shard_map/ppermute | solution.py:544
  20.9 4.6 %collective-permute-done.2.second_ref = f32[16,2048]{1,0:T(8,128)S(1)} collective-permute-done((f32[16,2048]{1,0:T(8,128)S(1)}, f32[16,2048]{1,0:T(8,128)S(1)}, u32[]{:S(2)}, u32[]{:S(2)}) %collective-permute-start.2) | collective-permute-done | bytes 131104 | tf_op jit(solution)/shard_map/ppermute | solution.py:544
  25.5 1.3 %collective-permute-start.3 = (f32[16,2048]{1,0:T(8,128)S(1)}, f32[16,2048]{1,0:T(8,128)S(1)}, u32[]{:S(2)}, u32[]{:S(2)}) collective-permute-start(f32[16,2048]{1,0:T(8,128)S(1)} %combine.3), channel_id=1, source_target_pairs={{0,96},{32,128},{64,160},{96,192},{112,16},{128,224},{144,48},{176... | collective-permute-start | bytes 393224 | tf_op jit(solution)/shard_map/ppermute | solution.py:544
  26.8 1.3 %collective-permute-start.4 = (f32[16,2048]{1,0:T(8,128)S(1)}, f32[16,2048]{1,0:T(8,128)S(1)}, u32[]{:S(2)}, u32[]{:S(2)}) collective-permute-start(f32[16,2048]{1,0:T(8,128)S(1)} %combine.3), channel_id=1, source_target_pairs={{0,32},{32,64},{48,16},{64,96},{80,48},{96,128},{112,80},{128,160}... | collective-permute-start | bytes 393224 | tf_op jit(solution)/shard_map/ppermute | solution.py:544
  28.1 4.8 %local_filter.1 = (f32[16,768,128]{2,1,0:T(8,128)S(1)}, f32[16,24,128]{2,1,0:T(8,128)S(1)}, f32[16,208,128]{2,1,0:T(8,128)S(1)}) custom-call(s32[10]{0:T(128)S(1)} %pad_add_fusion.spot_ref, f32[16,640,128]{2,1,0:T(8,128)S(1)} %get-tuple-element.67.pre_ref, f32[16,2048]{1,0:T(8,128)S(1)} %get-tuple-element.60.rate_ref, ...), custom_call_target="tpu_custom_call" | custom-call | flops 67108864 | bytes 8388608 | tf_op jit(solution)/shard_map/local_filter/pallas_call | solution.py:433
  32.9 5.2 %collective-permute-done.3.far_ref = f32[16,2048]{1,0:T(8,128)S(1)} collective-permute-done((f32[16,2048]{1,0:T(8,128)S(1)}, f32[16,2048]{1,0:T(8,128)S(1)}, u32[]{:S(2)}, u32[]{:S(2)}) %collective-permute-start.3) | collective-permute-done | bytes 131104 | tf_op jit(solution)/shard_map/ppermute | solution.py:544
  38.1 0.0 collective-permute-done.4.near_ref
  38.1 5.4 %collective-permute-start.5 = (f32[16,2048]{1,0:T(8,128)S(1)}, f32[16,2048]{1,0:T(8,128)S(1)}, u32[]{:S(2)}, u32[]{:S(2)}) collective-permute-start(f32[16,2048]{1,0:T(8,128)S(1)} %get-tuple-element.76), channel_id=1, source_target_pairs={{0,16},{16,0},{32,48},{48,32},{64,80},{80,64},{96,112},{112,96},{1... | collective-permute-start | bytes 393224 | tf_op jit(solution)/shard_map/ppermute | solution.py:555
  43.5 1.0 %collective-permute-done.5.handed_ref = f32[16,2048]{1,0:T(8,128)S(1)} collective-permute-done((f32[16,2048]{1,0:T(8,128)S(1)}, f32[16,2048]{1,0:T(8,128)S(1)}, u32[]{:S(2)}, u32[]{:S(2)}) %collective-permute-start.5) | collective-permute-done | bytes 131104 | tf_op jit(solution)/shard_map/ppermute | solution.py:555
  44.5 1.0 %edge_gradients.1 = (f32[16,2048]{1,0:T(8,128)S(1)}, f32[16,2048]{1,0:T(8,128)S(1)}, f32[24,2048]{1,0:T(8,128)S(1)}) custom-call(s32[10]{0:T(128)S(1)} %pad_add_fusion.spot_ref, f32[16,512,128]{2,1,0:T(8,128)S(1)} %get-tuple-element.54.raw_ref, f32[16,384,128]{2,1,0:T(8,128)S(1)} %get-tuple-element.61.feat_ref, ...), custom_call_target="tpu_custom_call" | custom-call | flops 67108864 | bytes 8388608 | tf_op jit(solution)/shard_map/edge_gradients/pallas_call | solution.py:433
  45.5 2.3 %collective-permute-start.6 = (f32[24,2048]{1,0:T(8,128)S(1)}, f32[24,2048]{1,0:T(8,128)S(1)}, u32[]{:S(2)}, u32[]{:S(2)}) collective-permute-start(f32[24,2048]{1,0:T(8,128)S(1)} %get-tuple-element.82), channel_id=1, source_target_pairs={{16,0},{32,16},{48,32},{64,48},{80,64},{96,80},{112,96},{128,112},... | collective-permute-start | bytes 589832 | tf_op jit(solution)/shard_map/ppermute | solution.py:558
  47.8 6.9 %filter_gradients.1 = (bf16[128,2048]{1,0:T(8,128)(2,1)}, f32[16,384,128]{2,1,0:T(8,128)S(1)}, f32[8,40,128]{2,1,0:T(8,128)S(1)}, f32[8,40,128]{2,1,0:T(8,128)S(1)}) custom-call(s32[10]{0:T(128)S(1)} %pad_add_fusion.spot_ref, f32[16,512,128]{2,1,0:T(8,128)S(1)} %get-tuple-element.54.raw_ref, f32[16,384,128]{2,1,0:T(8,128)S(1)} %get-tuple-element.61.feat_ref, ...), custom_call_target="tpu_custom_call" | custom-call | flops 67108864 | bytes 8388608 | tf_op jit(solution)/shard_map/filter_gradients/pallas_call | solution.py:433
  54.7 0.0 collective-permute-done.6.edge_ref
  54.7 0.0 collective-permute-start.7
  54.7 1.4 %collective-permute-done.7 = f32[8,40,128]{2,1,0:T(8,128)S(1)} collective-permute-done((f32[8,40,128]{2,1,0:T(8,128)S(1)}, f32[8,40,128]{2,1,0:T(8,128)S(1)}, u32[]{:S(2)}, u32[]{:S(2)}) %collective-permute-start.7) | collective-permute-done | bytes 163872 | tf_op jit(solution)/shard_map/ppermute | solution.py:565
  56.1 3.0 %collective-permute-start.8 = (f32[4,40,128]{2,1,0:T(8,128)S(1)}, f32[4,40,128]{2,1,0:T(8,128)S(1)}, u32[]{:S(2)}, u32[]{:S(2)}) collective-permute-start(f32[4,40,128]{2,1,0:T(8,128)S(1)} %slice.29), channel_id=1, source_target_pairs={{0,2},{1,3},{2,0},{3,1},{4,6},{5,7},{6,4},{7,5},{8,10},{9,11},{10,... | collective-permute-start | bytes 245768 | tf_op jit(solution)/shard_map/ppermute | solution.py:565
  59.1 2.5 %collective-permute-done.8 = f32[4,40,128]{2,1,0:T(8,128)S(1)} collective-permute-done((f32[4,40,128]{2,1,0:T(8,128)S(1)}, f32[4,40,128]{2,1,0:T(8,128)S(1)}, u32[]{:S(2)}, u32[]{:S(2)}) %collective-permute-start.8) | collective-permute-done | bytes 81952 | tf_op jit(solution)/shard_map/ppermute | solution.py:565
  61.7 1.4 %collective-permute-start.9 = (f32[2,40,128]{2,1,0:T(8,128)S(1)}, f32[2,40,128]{2,1,0:T(8,128)S(1)}, u32[]{:S(2)}, u32[]{:S(2)}) collective-permute-start(f32[2,40,128]{2,1,0:T(8,128)S(1)} %slice.31), channel_id=1, source_target_pairs={{0,1},{1,0},{2,3},{3,2},{4,5},{5,4},{6,7},{7,6},{8,9},{9,8},{10,11... | collective-permute-start | bytes 122888 | tf_op jit(solution)/shard_map/ppermute | solution.py:565
  63.0 1.6 %collective-permute-done.9 = f32[2,40,128]{2,1,0:T(8,128)S(1)} collective-permute-done((f32[2,40,128]{2,1,0:T(8,128)S(1)}, f32[2,40,128]{2,1,0:T(8,128)S(1)}, u32[]{:S(2)}, u32[]{:S(2)}) %collective-permute-start.9) | collective-permute-done | bytes 40992 | tf_op jit(solution)/shard_map/ppermute | solution.py:565
  64.6 0.9 collective-permute-start.10
  65.5 1.8 %input_gradient.3 = bf16[128,2048]{1,0:T(8,128)(2,1)} custom-call(f32[16,384,128]{2,1,0:T(8,128)S(1)} %get-tuple-element.86.gfeat_ref, f32[24,2048]{1,0:T(8,128)S(1)} %collective-permute-done.6.edge_ref, f32[3,7,2048]{2,1,0:T(8,128)S(1)} %get-tuple-element.59.taps_ref, f32[6,22,8,128]{3,2,1,0:T(8,128)S(1)} %get-tuple-element.55.masks), custom_call_target="tpu_custom_call" | custom-call | flops 67108864 | bytes 8388608 | tf_op jit(solution)/shard_map/input_gradient/pallas_call | solution.py:433
  67.3 0.2 collective-permute-done.10
  67.5 0.5 collective-permute-start.11
  68.0 1.8 %input_gradient.4 = bf16[128,2048]{1,0:T(8,128)(2,1)} custom-call(f32[16,384,128]{2,1,0:T(8,128)S(1)} %get-tuple-element.86.gfeat_ref, f32[24,2048]{1,0:T(8,128)S(1)} %collective-permute-done.6.edge_ref, f32[3,7,2048]{2,1,0:T(8,128)S(1)} %get-tuple-element.59.taps_ref, f32[6,22,8,128]{3,2,1,0:T(8,128)S(1)} %get-tuple-element.55.masks), custom_call_target="tpu_custom_call" | custom-call | flops 67108864 | bytes 8388608 | tf_op jit(solution)/shard_map/input_gradient/pallas_call | solution.py:433
  69.7 1.5 %collective-permute-done.11 = f32[2,40,128]{2,1,0:T(8,128)S(1)} collective-permute-done((f32[2,40,128]{2,1,0:T(8,128)S(1)}, f32[2,40,128]{2,1,0:T(8,128)S(1)}, u32[]{:S(2)}, u32[]{:S(2)}) %collective-permute-start.11) | collective-permute-done | bytes 40992 | tf_op jit(solution)/shard_map/ppermute | solution.py:565
  71.3 2.6 %collective-permute-start.12 = (f32[2,40,128]{2,1,0:T(8,128)S(1)}, f32[2,40,128]{2,1,0:T(8,128)S(1)}, u32[]{:S(2)}, u32[]{:S(2)}) collective-permute-start(f32[2,40,128]{2,1,0:T(8,128)S(1)} %add.22), channel_id=1, source_target_pairs={{0,128},{16,144},{32,160},{48,176},{64,192},{80,208},{96,224},{112... | collective-permute-start | bytes 122888 | tf_op jit(solution)/shard_map/ppermute | solution.py:565
  73.9 1.8 %input_gradient.5 = bf16[128,2048]{1,0:T(8,128)(2,1)} custom-call(f32[16,384,128]{2,1,0:T(8,128)S(1)} %get-tuple-element.86.gfeat_ref, f32[24,2048]{1,0:T(8,128)S(1)} %collective-permute-done.6.edge_ref, f32[3,7,2048]{2,1,0:T(8,128)S(1)} %get-tuple-element.59.taps_ref, f32[6,22,8,128]{3,2,1,0:T(8,128)S(1)} %get-tuple-element.55.masks), custom_call_target="tpu_custom_call" | custom-call | flops 67108864 | bytes 8388608 | tf_op jit(solution)/shard_map/input_gradient/pallas_call | solution.py:433
  75.7 2.3 %collective-permute-done.12 = f32[2,40,128]{2,1,0:T(8,128)S(1)} collective-permute-done((f32[2,40,128]{2,1,0:T(8,128)S(1)}, f32[2,40,128]{2,1,0:T(8,128)S(1)}, u32[]{:S(2)}, u32[]{:S(2)}) %collective-permute-start.12) | collective-permute-done | bytes 40992 | tf_op jit(solution)/shard_map/ppermute | solution.py:565
  78.0 1.3 %collective-permute-start.13 = (f32[2,40,128]{2,1,0:T(8,128)S(1)}, f32[2,40,128]{2,1,0:T(8,128)S(1)}, u32[]{:S(2)}, u32[]{:S(2)}) collective-permute-start(f32[2,40,128]{2,1,0:T(8,128)S(1)} %add.23), channel_id=1, source_target_pairs={{0,1},{1,0},{2,3},{3,2},{4,5},{5,4},{6,7},{7,6},{8,9},{9,8},{10,11... | collective-permute-start | bytes 122888 | tf_op jit(solution)/shard_map/ppermute | solution.py:565
  79.3 1.6 %collective-permute-done.13 = f32[2,40,128]{2,1,0:T(8,128)S(1)} collective-permute-done((f32[2,40,128]{2,1,0:T(8,128)S(1)}, f32[2,40,128]{2,1,0:T(8,128)S(1)}, u32[]{:S(2)}, u32[]{:S(2)}) %collective-permute-start.13) | collective-permute-done | bytes 40992 | tf_op jit(solution)/shard_map/ppermute | solution.py:565
  80.9 2.9 %collective-permute-start.14 = (f32[4,40,128]{2,1,0:T(8,128)S(1)}, f32[4,40,128]{2,1,0:T(8,128)S(1)}, u32[]{:S(2)}, u32[]{:S(2)}) collective-permute-start(f32[4,40,128]{2,1,0:T(8,128)S(1)} %pad_maximum_fusion.2), channel_id=1, source_target_pairs={{0,2},{1,3},{2,0},{3,1},{4,6},{5,7},{6,4},{7,5},{8,10},{9,11},{10,... | collective-permute-start | bytes 245768 | tf_op jit(solution)/shard_map/ppermute | solution.py:565
  83.8 1.9 %collective-permute-done.14 = f32[4,40,128]{2,1,0:T(8,128)S(1)} collective-permute-done((f32[4,40,128]{2,1,0:T(8,128)S(1)}, f32[4,40,128]{2,1,0:T(8,128)S(1)}, u32[]{:S(2)}, u32[]{:S(2)}) %collective-permute-start.14) | collective-permute-done | bytes 81952 | tf_op jit(solution)/shard_map/ppermute | solution.py:565
  85.7 7.9 %collective-permute-start.15 = (f32[8,40,128]{2,1,0:T(8,128)S(1)}, f32[8,40,128]{2,1,0:T(8,128)S(1)}, u32[]{:S(2)}, u32[]{:S(2)}) collective-permute-start(f32[8,40,128]{2,1,0:T(8,128)S(1)} %pad_maximum_fusion.kept_ref), channel_id=1, source_target_pairs={{0,16},{16,0},{32,48},{48,32},{64,80},{80,64},{96,112},{112,96},{1... | collective-permute-start | bytes 491528 | tf_op jit(solution)/shard_map/ppermute | solution.py:565
  93.6 1.0 %collective-permute-done.15.away_ref = f32[8,40,128]{2,1,0:T(8,128)S(1)} collective-permute-done((f32[8,40,128]{2,1,0:T(8,128)S(1)}, f32[8,40,128]{2,1,0:T(8,128)S(1)}, u32[]{:S(2)}, u32[]{:S(2)}) %collective-permute-start.15) | collective-permute-done | bytes 163872 | tf_op jit(solution)/shard_map/ppermute | solution.py:565
  94.6 1.9 %parameter_gradients.1 = (f32[3,7,2048]{2,1,0:T(8,128)}, f32[16,2048]{1,0:T(8,128)}, f32[1,2048]{1,0:T(1,128)}) custom-call(s32[10]{0:T(128)S(1)} %pad_add_fusion.spot_ref, f32[8,40,128]{2,1,0:T(8,128)S(1)} %pad_maximum_fusion.kept_ref, f32[8,40,128]{2,1,0:T(8,128)S(1)} %collective-permute-done.15.away_ref), custom_call_target="tpu_custom_call" | custom-call | flops 67108864 | bytes 8388608 | tf_op jit(solution)/shard_map/parameter_gradients/pallas_call | solution.py:433
  (15 shorter events, 0.2 us)
Async XLA Ops:
  2.2 9.4 %collective-permute-start = (bf16[24,2048]{1,0:T(8,128)(2,1)S(1)}, bf16[24,2048]{1,0:T(8,128)(2,1)S(1)}, u32[]{:S(2)}, u32[]{:S(2)}) collective-permute-start(bf16[24,2048]{1,0:T(8,128)(2,1)S(1)} %pad_maximum_fusion.1), channel_id=1, source_target_pairs={{0,16},{16,32},{32,48},{48,64},{64,80},{80,96},{96,112},{112,128},... | collective-permute-start | bytes 294920 | tf_op jit(solution)/shard_map/ppermute | solution.py:533
  18.2 1.4 %collective-permute-start.1 = (f32[16,2048]{1,0:T(8,128)S(1)}, f32[16,2048]{1,0:T(8,128)S(1)}, u32[]{:S(2)}, u32[]{:S(2)}) collective-permute-start(f32[16,2048]{1,0:T(8,128)S(1)} %get-tuple-element.62.sent_ref), channel_id=1, source_target_pairs={{0,16},{16,0},{32,48},{48,32},{64,80},{80,64},{96,112},{112,96},{1... | collective-permute-start | bytes 393224 | tf_op jit(solution)/shard_map/ppermute | solution.py:546
  19.6 5.9 %collective-permute-start.2 = (f32[16,2048]{1,0:T(8,128)S(1)}, f32[16,2048]{1,0:T(8,128)S(1)}, u32[]{:S(2)}, u32[]{:S(2)}) collective-permute-start(f32[16,2048]{1,0:T(8,128)S(1)} %combine.2.first_ref), channel_id=1, source_target_pairs={{0,32},{32,64},{48,16},{64,96},{80,48},{96,128},{112,80},{128,160}... | collective-permute-start | bytes 393224 | tf_op jit(solution)/shard_map/ppermute | solution.py:544
  25.5 12.5 %collective-permute-start.3 = (f32[16,2048]{1,0:T(8,128)S(1)}, f32[16,2048]{1,0:T(8,128)S(1)}, u32[]{:S(2)}, u32[]{:S(2)}) collective-permute-start(f32[16,2048]{1,0:T(8,128)S(1)} %combine.3), channel_id=1, source_target_pairs={{0,96},{32,128},{64,160},{96,192},{112,16},{128,224},{144,48},{176... | collective-permute-start | bytes 393224 | tf_op jit(solution)/shard_map/ppermute | solution.py:544
  26.8 11.2 %collective-permute-start.4 = (f32[16,2048]{1,0:T(8,128)S(1)}, f32[16,2048]{1,0:T(8,128)S(1)}, u32[]{:S(2)}, u32[]{:S(2)}) collective-permute-start(f32[16,2048]{1,0:T(8,128)S(1)} %combine.3), channel_id=1, source_target_pairs={{0,32},{32,64},{48,16},{64,96},{80,48},{96,128},{112,80},{128,160}... | collective-permute-start | bytes 393224 | tf_op jit(solution)/shard_map/ppermute | solution.py:544
  38.1 6.4 %collective-permute-start.5 = (f32[16,2048]{1,0:T(8,128)S(1)}, f32[16,2048]{1,0:T(8,128)S(1)}, u32[]{:S(2)}, u32[]{:S(2)}) collective-permute-start(f32[16,2048]{1,0:T(8,128)S(1)} %get-tuple-element.76), channel_id=1, source_target_pairs={{0,16},{16,0},{32,48},{48,32},{64,80},{80,64},{96,112},{112,96},{1... | collective-permute-start | bytes 393224 | tf_op jit(solution)/shard_map/ppermute | solution.py:555
  45.5 9.2 %collective-permute-start.6 = (f32[24,2048]{1,0:T(8,128)S(1)}, f32[24,2048]{1,0:T(8,128)S(1)}, u32[]{:S(2)}, u32[]{:S(2)}) collective-permute-start(f32[24,2048]{1,0:T(8,128)S(1)} %get-tuple-element.82), channel_id=1, source_target_pairs={{16,0},{32,16},{48,32},{64,48},{80,64},{96,80},{112,96},{128,112},... | collective-permute-start | bytes 589832 | tf_op jit(solution)/shard_map/ppermute | solution.py:558
  54.7 1.4 %collective-permute-start.7 = (f32[8,40,128]{2,1,0:T(8,128)S(1)}, f32[8,40,128]{2,1,0:T(8,128)S(1)}, u32[]{:S(2)}, u32[]{:S(2)}) collective-permute-start(f32[8,40,128]{2,1,0:T(8,128)S(1)} %get-tuple-element.83), channel_id=1, source_target_pairs={{0,16},{16,0},{32,48},{48,32},{64,80},{80,64},{96,112},{112,96},{1... | collective-permute-start | bytes 491528 | tf_op jit(solution)/shard_map/ppermute | solution.py:565
  56.1 5.5 %collective-permute-start.8 = (f32[4,40,128]{2,1,0:T(8,128)S(1)}, f32[4,40,128]{2,1,0:T(8,128)S(1)}, u32[]{:S(2)}, u32[]{:S(2)}) collective-permute-start(f32[4,40,128]{2,1,0:T(8,128)S(1)} %slice.29), channel_id=1, source_target_pairs={{0,2},{1,3},{2,0},{3,1},{4,6},{5,7},{6,4},{7,5},{8,10},{9,11},{10,... | collective-permute-start | bytes 245768 | tf_op jit(solution)/shard_map/ppermute | solution.py:565
  61.7 2.9 %collective-permute-start.9 = (f32[2,40,128]{2,1,0:T(8,128)S(1)}, f32[2,40,128]{2,1,0:T(8,128)S(1)}, u32[]{:S(2)}, u32[]{:S(2)}) collective-permute-start(f32[2,40,128]{2,1,0:T(8,128)S(1)} %slice.31), channel_id=1, source_target_pairs={{0,1},{1,0},{2,3},{3,2},{4,5},{5,4},{6,7},{7,6},{8,9},{9,8},{10,11... | collective-permute-start | bytes 122888 | tf_op jit(solution)/shard_map/ppermute | solution.py:565
  64.6 2.9 %collective-permute-start.10 = (f32[2,40,128]{2,1,0:T(8,128)S(1)}, f32[2,40,128]{2,1,0:T(8,128)S(1)}, u32[]{:S(2)}, u32[]{:S(2)}) collective-permute-start(f32[2,40,128]{2,1,0:T(8,128)S(1)} %slice_add_fusion.1), channel_id=1, source_target_pairs={{0,32},{16,48},{32,0},{48,16},{64,96},{80,112},{96,64},{112,80},{1... | collective-permute-start | bytes 122888 | tf_op jit(solution)/shard_map/ppermute | solution.py:565
  67.5 3.8 %collective-permute-start.11 = (f32[2,40,128]{2,1,0:T(8,128)S(1)}, f32[2,40,128]{2,1,0:T(8,128)S(1)}, u32[]{:S(2)}, u32[]{:S(2)}) collective-permute-start(f32[2,40,128]{2,1,0:T(8,128)S(1)} %add.21), channel_id=1, source_target_pairs={{0,64},{16,80},{32,96},{48,112},{64,0},{80,16},{96,32},{112,48},{1... | collective-permute-start | bytes 122888 | tf_op jit(solution)/shard_map/ppermute | solution.py:565
  71.3 6.8 %collective-permute-start.12 = (f32[2,40,128]{2,1,0:T(8,128)S(1)}, f32[2,40,128]{2,1,0:T(8,128)S(1)}, u32[]{:S(2)}, u32[]{:S(2)}) collective-permute-start(f32[2,40,128]{2,1,0:T(8,128)S(1)} %add.22), channel_id=1, source_target_pairs={{0,128},{16,144},{32,160},{48,176},{64,192},{80,208},{96,224},{112... | collective-permute-start | bytes 122888 | tf_op jit(solution)/shard_map/ppermute | solution.py:565
  78.0 2.9 %collective-permute-start.13 = (f32[2,40,128]{2,1,0:T(8,128)S(1)}, f32[2,40,128]{2,1,0:T(8,128)S(1)}, u32[]{:S(2)}, u32[]{:S(2)}) collective-permute-start(f32[2,40,128]{2,1,0:T(8,128)S(1)} %add.23), channel_id=1, source_target_pairs={{0,1},{1,0},{2,3},{3,2},{4,5},{5,4},{6,7},{7,6},{8,9},{9,8},{10,11... | collective-permute-start | bytes 122888 | tf_op jit(solution)/shard_map/ppermute | solution.py:565
  80.9 4.8 %collective-permute-start.14 = (f32[4,40,128]{2,1,0:T(8,128)S(1)}, f32[4,40,128]{2,1,0:T(8,128)S(1)}, u32[]{:S(2)}, u32[]{:S(2)}) collective-permute-start(f32[4,40,128]{2,1,0:T(8,128)S(1)} %pad_maximum_fusion.2), channel_id=1, source_target_pairs={{0,2},{1,3},{2,0},{3,1},{4,6},{5,7},{6,4},{7,5},{8,10},{9,11},{10,... | collective-permute-start | bytes 245768 | tf_op jit(solution)/shard_map/ppermute | solution.py:565
  85.7 8.9 %collective-permute-start.15 = (f32[8,40,128]{2,1,0:T(8,128)S(1)}, f32[8,40,128]{2,1,0:T(8,128)S(1)}, u32[]{:S(2)}, u32[]{:S(2)}) collective-permute-start(f32[8,40,128]{2,1,0:T(8,128)S(1)} %pad_maximum_fusion.kept_ref), channel_id=1, source_target_pairs={{0,16},{16,0},{32,48},{48,32},{64,80},{80,64},{96,112},{112,96},{1... | collective-permute-start | bytes 491528 | tf_op jit(solution)/shard_map/ppermute | solution.py:565

commit v4 on v3

--- a/solution.py
+++ b/solution.py
@@ -35,10 +35,13 @@
 
 
 def starts_of(spot_ref):
-    found, begun = [], jnp.int32(0)
-    for j in range(2, spot_ref.shape[0]):
-        found.append(begun)
-        begun = begun + spot_ref[j]
+    return sums_before([spot_ref[j] for j in range(2, spot_ref.shape[0])])
+
+
+def sums_before(lengths):
+    found = [jnp.int32(0)]
+    for length in lengths[:-1]:
+        found.append(found[-1] + length)
     return found
 
 
@@ -93,14 +96,34 @@
     }
 
 
+def tail_kernel(q_ref, k_ref, v_ref, out_ref, rows, arrived):
+    copies = [
+        pltpu.make_async_copy(ref.at[ROWS - 16 :], rows.at[which], arrived.at[which])
+        for which, ref in enumerate((q_ref, k_ref, v_ref))
+    ]
+    for copy in copies:
+        copy.start()
+    for copy in copies:
+        copy.wait()
+
+    def tile_body(tile, lanes):
+        q, k, v = (rows[which, :, lanes].astype(F32)[8:] for which in range(3))
+        out_ref[0:16, lanes] = jnp.concatenate([q, k], axis=0).astype(BF16)
+        out_ref[16:32, lanes] = jnp.concatenate([v, jnp.zeros_like(v)], axis=0).astype(BF16)
+
+    each_tile(out_ref.shape[1] // LANES, tile_body)
+
+
 def stage_kernel(
-    spot_ref, q_ref, k_ref, v_ref, cot_ref, taps_in, rate_in, residue_in, skip_in,
-    raw_ref, masks, open_mask, end_mask, chain, taps_ref, rate_ref, residue_ref, skip_ref,
-    stage, columns, arrived, loaded,
+    place_ref, lengths_in, q_ref, k_ref, v_ref, cot_ref, taps_in, rate_in, residue_in, skip_in,
+    raw_ref, masks, open_mask, end_mask, chain, taps_ref, rate_ref, residue_ref, skip_ref, decay_ref,
+    stage, columns, arrived, loaded, lengths_ref, known,
 ):
     inputs = (q_ref, k_ref, v_ref, cot_ref)
     chunk = columns.shape[2] // CHUNKS
-    starts, anchor = starts_of(spot_ref), spot_ref[0] * ROWS
+    anchor = place_ref[0] * ROWS
+    lengths = pltpu.make_async_copy(lengths_in, lengths_ref, known)
+    lengths.start()
 
     def fetch(which, part):
         cols = pl.ds(pl.multiple_of(part * chunk, LANES), chunk)
@@ -117,6 +140,8 @@
             fetch(which, part).start()
     for copy in parameters:
         copy.start()
+    lengths.wait()
+    starts = sums_before([lengths_ref[0, j] for j in range(lengths_ref.shape[1])])
     store_masks(starts, anchor, masks, STEPS + HALO, HALO)
     store_edge_masks(starts, anchor, open_mask, end_mask)
     for k in range(3):
@@ -142,9 +167,14 @@
     for copy in parameters:
         copy.wait()
 
+    def decay_body(tile, lanes):
+        decay_ref[:, lanes] = jnp.exp(-rate_ref[:, lanes])
+
+    each_tile(raw_ref.shape[0], decay_body)
+
 
 def feature_kernel(
-    spot_ref, raw_ref, masks, open_mask, end_mask, chain, taps_ref, rate_ref, halo_ref,
+    spot_ref, raw_ref, masks, open_mask, end_mask, chain, taps_ref, rate_ref, decay_ref, halo_ref,
     feat_ref, pre_ref, own_ref, sent_ref, pass_ref,
 ):
     starts, here = starts_of(spot_ref), spot_ref[0]
@@ -178,7 +208,7 @@
             pre_ref[tile, slab(GRAD, t)] = raw_ref[tile, slab(COT, t)] * feat_ref[tile, slab(0, t)]
         for low in range(0, MODES, 8):
             modes = range(low, low + 8)
-            decay = [jnp.exp(-row(rate_ref, m, lanes)) for m in modes]
+            decay = [row(decay_ref, m, lanes) for m in modes]
             ends = [pre_ref[tile, slab(SOURCE, 0)] * end_mask[0]] * 8
             for t in range(1, STEPS):
                 value = pre_ref[tile, slab(SOURCE, t)] * end_mask[t]
@@ -210,7 +240,7 @@
 
 
 def local_kernel(
-    spot_ref, pre_ref, rate_ref, residue_ref, skip_ref, open_mask, end_mask,
+    spot_ref, pre_ref, rate_ref, decay_ref, residue_ref, skip_ref, open_mask, end_mask,
     post_ref, local_ref, first_ref,
     masks, reach, stage, weight_stage,
 ):
@@ -225,7 +255,7 @@
     def tile_body(tile, lanes):
         segment = segments().astype(F32)
         rates = rate_ref[:, lanes]
-        decay = jnp.exp(-rates)
+        decay = decay_ref[:, lanes]
         power = residue_ref[:, lanes] * jnp.sqrt(rates)
         weight_stage[...] = power * decay
         kernel = []
@@ -323,7 +353,7 @@
 
 
 def gradient_kernel(
-    spot_ref, raw_ref, feat_ref, post_ref, local_ref, enter_ref, return_ref, own_ref, sent_ref, rate_ref, halo_ref,
+    spot_ref, raw_ref, feat_ref, post_ref, local_ref, enter_ref, return_ref, own_ref, sent_ref, rate_ref, decay_ref, halo_ref,
     masks, open_mask, end_mask,
     out_ref, gfeat_ref, kept_ref, away_ref,
     stage,
@@ -331,7 +361,7 @@
     lower = spot_ref[0] % 2 == 0
 
     def tile_body(tile, lanes):
-        decay = [jnp.exp(-row(rate_ref, m, lanes)) for m in range(MODES)]
+        decay = [row(decay_ref, m, lanes) for m in range(MODES)]
         state = [
             post_ref[tile, slab(SWT, m)] + post_ref[tile, slab(SCOEF, m)] * row(enter_ref, m, lanes)
             for m in range(MODES)
@@ -355,7 +385,7 @@
                 state = [d * s for d, s in zip(decay, state)]
         rates = rate_ref[:, lanes]
         begin = jnp.where(lower, sent_ref[:, lanes], own_ref[:, lanes])
-        sums = [jnp.sqrt(rates) * (local_ref[tile, 0:MODES] + enter_ref[:, lanes] * jnp.exp(-rates) * begin)]
+        sums = [jnp.sqrt(rates) * (local_ref[tile, 0:MODES] + enter_ref[:, lanes] * decay_ref[:, lanes] * begin)]
         for branch in range(3):
             totals = [jnp.zeros((SEGS, LANES), F32)] * TAPS
             rows = [raw_ref[tile, slab(branch, t)] for t in range(STEPS)]
@@ -429,11 +459,11 @@
 STAGE = (ROWS, LANES)
 
 
-def call(body, name, ins, outs, scratch, *args):
+def call(body, name, ins, outs, scratch, *args, dtype=F32):
     return pl.pallas_call(
         body,
         name=name,
-        out_shape=[out if isinstance(out, jax.ShapeDtypeStruct) else pltpu.VMEM(out, F32) for out in outs],
+        out_shape=[out if isinstance(out, jax.ShapeDtypeStruct) else pltpu.VMEM(out, dtype) for out in outs],
         in_specs=ins,
         out_specs=[VMEM] * len(outs),
         scratch_shapes=[pltpu.VMEM(one, F32) if isinstance(one, tuple) else one for one in scratch],
@@ -442,38 +472,47 @@
     )(*[x if spec is SMEM else pltpu.with_memory_space_constraint(x, spec.memory_space) for x, spec in zip(args, ins)])
 
 
-def staged(spot, query, key, value, upstream, taps, rate, residue, skip):
+def tails(query, key, value):
+    [made] = call(
+        tail_kernel, "last_rows", [HBM] * 3, [(32, query.shape[1])],
+        [pltpu.VMEM((3, 16, query.shape[1]), BF16), pltpu.SemaphoreType.DMA((3,))],
+        query, key, value, dtype=BF16,
+    )
+    return made
+
+
+def staged(place, lengths, query, key, value, upstream, taps, rate, residue, skip):
     channels = query.shape[1]
     return call(
         stage_kernel, "stage",
-        [SMEM] + [HBM] * 8,
+        [SMEM] + [HBM] * 9,
         [(channels // LANES, 4 * ROWS, LANES), MASKS, EDGE_MASKS, EDGE_MASKS, (6, SEGS, LANES),
-         taps.shape, rate.shape, residue.shape, skip.shape],
+         taps.shape, rate.shape, residue.shape, skip.shape, rate.shape],
         [(4, *STAGE), pltpu.VMEM((4, ROWS, channels), BF16), pltpu.SemaphoreType.DMA((4, CHUNKS)),
-         pltpu.SemaphoreType.DMA((4,))],
-        spot, query, key, value, upstream, taps, rate, residue, skip,
-    )
-
-
-def features(spot, raw, masks, open_mask, end_mask, chain, taps, rate, halo):
+         pltpu.SemaphoreType.DMA((4,)), pltpu.SMEM(lengths.shape, jnp.int32), pltpu.SemaphoreType.DMA],
+        place, lengths, query, key, value, upstream, taps, rate, residue, skip,
+    )
+
+
+def features(spot, raw, masks, open_mask, end_mask, chain, taps, rate, decay, halo):
     tiles, states = raw.shape[0], rate.shape
     return call(
         feature_kernel, "features",
-        [SMEM] + [VMEM] * 8,
+        [SMEM] + [VMEM] * 9,
         [(tiles, 3 * ROWS, LANES), (tiles, 5 * ROWS, LANES), states, states, (4, *states)],
         [],
-        spot, raw, masks, open_mask, end_mask, chain, taps, rate, halo,
-    )
-
-
-def local_filter(spot, pre, rate, residue, skip, open_mask, end_mask):
+        spot, raw, masks, open_mask, end_mask, chain, taps, rate, decay, halo,
+    )
+
+
+def local_filter(spot, pre, rate, decay, residue, skip, open_mask, end_mask):
     tiles = pre.shape[0]
     return call(
         local_kernel, "local_filter",
-        [SMEM] + [VMEM] * 6,
+        [SMEM] + [VMEM] * 7,
         [(tiles, 6 * ROWS, LANES), (tiles, MODES + 8, LANES), (tiles, FIRST_ROWS, LANES)],
         [(STEPS - 1, STEPS, SEGS, LANES), (2, SEGS, LANES), (MODES, LANES), (MODES, LANES)],
-        spot, pre, rate, residue, skip, open_mask, end_mask,
+        spot, pre, rate, decay, residue, skip, open_mask, end_mask,
     )
 
 
@@ -529,13 +568,12 @@
     place = jnp.stack([lax.axis_index("ctx"), lax.axis_index("dp")]).astype(jnp.int32)
     spot = jnp.concatenate([place, lengths[0]])
 
-    stacked = jnp.concatenate([x[0, ROWS - 8 :] for x in (query_rows, key_rows, value_rows)], axis=0)
-    halo = lax.ppermute(stacked, "ctx", [(i, i + 1) for i in range(count - 1)]).astype(F32)
-    raw, masks, open_mask, end_mask, chain, taps, rate, residue, skip = staged(
-        spot, query_rows[0], key_rows[0], value_rows[0], cotangent[0],
+    halo = lax.ppermute(tails(query_rows[0], key_rows[0], value_rows[0]), "ctx", [(i, i + 1) for i in range(count - 1)]).astype(F32)
+    raw, masks, open_mask, end_mask, chain, taps, rate, residue, skip, decay = staged(
+        place, lengths, query_rows[0], key_rows[0], value_rows[0], cotangent[0],
         short_filter, decay_rate.T, residue.T, skip_gain[None],
     )
-    feat, pre, own, sent, through = features(spot, raw, masks, open_mask, end_mask, chain, taps, rate, halo)
+    feat, pre, own, sent, through = features(spot, raw, masks, open_mask, end_mask, chain, taps, rate, decay, halo)
 
     pairs = [(i, i ^ 1) for i in range(count)]
 
@@ -547,7 +585,7 @@
     chip_state = combine(2, chip_state, through, onward(chip_state, 1))
     chip_state, pre = lax.optimization_barrier((chip_state, pre))
     near, far = onward(chip_state, 1), onward(chip_state, 3)
-    post, local, first = local_filter(spot, pre, rate, residue, skip, open_mask, end_mask)
+    post, local, first = local_filter(spot, pre, rate, decay, residue, skip, open_mask, end_mask)
     far, post = lax.optimization_barrier((far, post))
     arrived, handed = call(
         arrive_kernel, "arrive", [VMEM] * 4, [own.shape, own.shape], [], near, far, own, through
@@ -557,7 +595,7 @@
     entering, returning, edge = edge_gradients(spot, raw, feat, first, arrived, handed)
     next_edge = lax.ppermute(edge, "ctx", [(i, i - 1) for i in range(1, count)])
     block_out, gfeat, kept, away = filter_gradients(
-        spot, raw, feat, post, local, entering, returning, own, sent, rate, halo, masks, open_mask, end_mask
+        spot, raw, feat, post, local, entering, returning, own, sent, rate, decay, halo, masks, open_mask, end_mask
     )
     away, next_edge = lax.optimization_barrier((away, next_edge))
 
@@ -566,21 +604,24 @@
 
     grad_inputs = []
 
-    def exchange_beside(value, axis, flip):
-        value, beside = lax.optimization_barrier((value, next_edge))
-        made = input_gradient(len(grad_inputs), gfeat, beside, taps, masks)
-        sent, made = lax.optimization_barrier((exchange(value, axis, flip), made))
+    def exchanges(sent, axis, flips, beside=True):
+        if not beside:
+            return [exchange(value, axis, flip) for value, flip in zip(sent, flips)]
+        *sent, edge_now = lax.optimization_barrier((*sent, next_edge))
+        made = input_gradient(len(grad_inputs), gfeat, edge_now, taps, masks)
+        *received, made = lax.optimization_barrier((*exchanges(sent, axis, flips, False), made))
         grad_inputs.append(made)
-        return sent
+        return received
 
     total = kept + exchange(away, "ctx", 1)
-    for flip in (2, 1):
-        half = total.shape[0] // 2
-        total = total[:half] + exchange(total[half:], "dp", flip)
-    for flip in (2, 4, 8):
-        total = total + exchange_beside(total, "ctx", flip)
-    for flip in (1, 2):
-        total = jnp.concatenate([total, exchange(total, "dp", flip)])
+    quarter = total.shape[0] // 4
+    quarters = [total[quarter * i : quarter * (i + 1)] for i in range(4)]
+    one, two, three = exchanges(quarters[1:], "dp", (1, 2, 3), False)
+    total = (quarters[0] + one) + (two + three)
+    total = total + exchanges([total], "ctx", (2,))[0]
+    one, two, three = exchanges([total] * 3, "ctx", (4, 8, 12))
+    total = (total + one) + (two + three)
+    total = jnp.concatenate([total, *exchanges([total] * 3, "dp", (1, 2, 3))])
     grad_short, grad_residue, grad_skip = results(spot, total, exchange(total, "ctx", 1))
     return (block_out[None], *(g[None] for g in grad_inputs), grad_short, grad_residue.T, grad_skip[0])
 

time: 96.9 us -> 90.1 us (0.930)
  waiting for transfers between devices: 26 us -> 19.6 us
  local copies, waits for them, and re-layouts: 1.55 us -> 0.02 us
  Pallas kernels: 30.3 us -> 31.3 us
    ppermute x9 -> x12, waiting for transfers between devices: 13.9 us -> 7.05 us  [exchange(): lax.ppermute(value, axis, [(i, i ^ flip) for i in range(lax.axis_size(axi...]
    squeeze x2 -> x0, local copies, waits for them, and re-layouts: 1.54 us -> none  [per_device(): x[0, ROWS - 8:]]
    pallas_call x12 -> x13, Pallas kernels: 30.3 us -> 31.3 us  [call(): pl.pallas_call(body, name=name, out_shape=[out if isinstance(out, jax.Sha...]
    ppermute x9 -> x12, starting transfers between devices: 20.5 us -> 21.2 us  [exchange(): lax.ppermute(value, axis, [(i, i ^ flip) for i in range(lax.axis_size(axi...]
  transfers between devices with their start and end apart: 16 -> 19, of which waited for: 13 -> 13; matrix products, arithmetic and copies ran while one was open for 1% -> 0% of each run, Pallas kernels for 22% -> 23%
where the time goes in v4:
time: 90.1 us; the launch traced here: 89.9 us
  starting transfers between devices  37.9 us (42%)
  Pallas kernels  31.3 us (35%)
  waiting for transfers between devices  19.6 us (22%)
    pallas_call x13, Pallas kernels, call(): pl.pallas_call(body, name=name, out_shape=[out if isinstance(out, jax.Sha...  31.3 us
    ppermute x12, starting transfers between devices, exchange(): lax.ppermute(value, axis, [(i, i ^ flip) for i in range(lax.axis_size(axi...  21.2 us
    ppermute x3, waiting for transfers between devices, onward(): lax.ppermute(value, 'ctx', [(i, j) for i, j in moves if 0 <= j < count])  10.3 us
    ppermute x12, waiting for transfers between devices, exchange(): lax.ppermute(value, axis, [(i, i ^ flip) for i in range(lax.axis_size(axi...  7.05 us
    ppermute x1, starting transfers between devices, per_device(): handed = lax.ppermute(handed, 'ctx', pairs)  5.57 us
    ppermute x1, starting transfers between devices, per_device(): lax.ppermute(tails(query_rows[0], key_rows[0], value_rows[0]), 'ctx', [(i...  4.94 us
    ppermute x3, starting transfers between devices, onward(): lax.ppermute(value, 'ctx', [(i, j) for i, j in moves if 0 <= j < count])  3.88 us
    ppermute x1, starting transfers between devices, per_device(): next_edge = lax.ppermute(edge, 'ctx', [(i, i - 1) for i in range(1, count)])  2.27 us
  transfers between devices with their start and end apart: 19, of which 13 were waited for; matrix products, arithmetic and copies ran while one was open for 0% of the time, Pallas kernels for 23%

profile of v4, /device:TPU:1, one launch (start us, length us, event | category | flops | bytes accessed | tf_op | source)
XLA Modules:
  0.0 89.9 jit_solution(5854375016245888575)
XLA Ops:
  0.6 0.0 copy-start
  0.6 1.0 %last_rows.1 = bf16[32,2048]{1,0:T(8,128)(2,1)S(1)} custom-call(bf16[128,2048]{1,0:T(8,128)(2,1)} %bitcast.16, bf16[128,2048]{1,0:T(8,128)(2,1)} %bitcast.18, bf16[128,2048]{1,0:T(8,128)(2,1)} %bitcast.20), custom_call_target="tpu_custom_call" | custom-call | flops 67108864 | bytes 8388608 | tf_op jit(solution)/shard_map/last_rows/pallas_call | solution.py:463
  1.7 4.9 %collective-permute-start = (bf16[32,2048]{1,0:T(8,128)(2,1)S(1)}, bf16[32,2048]{1,0:T(8,128)(2,1)S(1)}, u32[]{:S(2)}, u32[]{:S(2)}) collective-permute-start(bf16[32,2048]{1,0:T(8,128)(2,1)S(1)} %last_rows.1), channel_id=1, source_target_pairs={{0,16},{16,32},{32,48},{48,64},{64,80},{80,96},{96,112},{112,128},... | collective-permute-start | bytes 393224 | tf_op jit(solution)/shard_map/ppermute | solution.py:571
  6.6 0.1 pad_add_fusion.1.place_ref
  6.7 3.9 %stage.1 = (f32[16,512,128]{2,1,0:T(8,128)S(1)}, f32[6,22,8,128]{3,2,1,0:T(8,128)S(1)}, f32[16,8,128]{2,1,0:T(8,128)S(1)}, f32[16,8,128]{2,1,0:T(8,128)S(1)}, f3...) custom-call(s32[2]{0:T(128)S(1)} %pad_add_fusion.1.place_ref, ...), custom_call_target="tpu_custom_call" | custom-call | flops 67108864 | bytes 8388608 | tf_op jit(solution)/shard_map/stage/pallas_call | solution.py:463
  10.6 0.0 copy-done
  10.6 0.1 pad_add_fusion.spot_ref
  10.7 0.0 collective-permute-done
  10.7 6.4 %features.1 = (f32[16,384,128]{2,1,0:T(8,128)S(1)}, f32[16,640,128]{2,1,0:T(8,128)S(1)}, f32[16,2048]{1,0:T(8,128)S(1)}, f32[16,2048]{1,0:T(8,128)S(1)}, f32[4,16,2048]{2,1,0:T(8,128)S(1)}) custom-call(s32[10]{0:T(128)S(1)} %pad_add_fusion.spot_ref, f32[16,512,128]{2,1,0:T(8,128)S(1)} %get-tuple-element.63.raw_ref, ...), custom_call_target="tpu_custom_call" | custom-call | flops 67108864 | bytes 8388608 | tf_op jit(solution)/shard_map/features/pallas_call | solution.py:463
  17.1 0.1 collective-permute-start.1
  17.2 1.3 %collective-permute-done.1.first_ref = f32[16,2048]{1,0:T(8,128)S(1)} collective-permute-done((f32[16,2048]{1,0:T(8,128)S(1)}, f32[16,2048]{1,0:T(8,128)S(1)}, u32[]{:S(2)}, u32[]{:S(2)}) %collective-permute-start.1) | collective-permute-done | bytes 131104 | tf_op jit(solution)/shard_map/ppermute | solution.py:584
  18.6 1.3 %collective-permute-start.2 = (f32[16,2048]{1,0:T(8,128)S(1)}, f32[16,2048]{1,0:T(8,128)S(1)}, u32[]{:S(2)}, u32[]{:S(2)}) collective-permute-start(f32[16,2048]{1,0:T(8,128)S(1)} %combine.2.first_ref), channel_id=1, source_target_pairs={{0,32},{32,64},{48,16},{64,96},{80,48},{96,128},{112,80},{128,160}... | collective-permute-start | bytes 393224 | tf_op jit(solution)/shard_map/ppermute | solution.py:582
  19.9 4.6 %collective-permute-done.2.second_ref = f32[16,2048]{1,0:T(8,128)S(1)} collective-permute-done((f32[16,2048]{1,0:T(8,128)S(1)}, f32[16,2048]{1,0:T(8,128)S(1)}, u32[]{:S(2)}, u32[]{:S(2)}) %collective-permute-start.2) | collective-permute-done | bytes 131104 | tf_op jit(solution)/shard_map/ppermute | solution.py:582
  24.5 1.3 %collective-permute-start.3 = (f32[16,2048]{1,0:T(8,128)S(1)}, f32[16,2048]{1,0:T(8,128)S(1)}, u32[]{:S(2)}, u32[]{:S(2)}) collective-permute-start(f32[16,2048]{1,0:T(8,128)S(1)} %combine.3), channel_id=1, source_target_pairs={{0,96},{32,128},{64,160},{96,192},{112,16},{128,224},{144,48},{176... | collective-permute-start | bytes 393224 | tf_op jit(solution)/shard_map/ppermute | solution.py:582
  25.8 1.3 %collective-permute-start.4 = (f32[16,2048]{1,0:T(8,128)S(1)}, f32[16,2048]{1,0:T(8,128)S(1)}, u32[]{:S(2)}, u32[]{:S(2)}) collective-permute-start(f32[16,2048]{1,0:T(8,128)S(1)} %combine.3), channel_id=1, source_target_pairs={{0,32},{32,64},{48,16},{64,96},{80,48},{96,128},{112,80},{128,160}... | collective-permute-start | bytes 393224 | tf_op jit(solution)/shard_map/ppermute | solution.py:582
  27.1 4.8 %local_filter.1 = (f32[16,768,128]{2,1,0:T(8,128)S(1)}, f32[16,24,128]{2,1,0:T(8,128)S(1)}, f32[16,208,128]{2,1,0:T(8,128)S(1)}) custom-call(s32[10]{0:T(128)S(1)} %pad_add_fusion.spot_ref, f32[16,640,128]{2,1,0:T(8,128)S(1)} %get-tuple-element.77.pre_ref, f32[16,2048]{1,0:T(8,128)S(1)} %get-tuple-element.69.rate_ref, ...), custom_call_target="tpu_custom_call" | custom-call | flops 67108864 | bytes 8388608 | tf_op jit(solution)/shard_map/local_filter/pallas_call | solution.py:463
  31.9 5.7 %collective-permute-done.3.far_ref = f32[16,2048]{1,0:T(8,128)S(1)} collective-permute-done((f32[16,2048]{1,0:T(8,128)S(1)}, f32[16,2048]{1,0:T(8,128)S(1)}, u32[]{:S(2)}, u32[]{:S(2)}) %collective-permute-start.3) | collective-permute-done | bytes 131104 | tf_op jit(solution)/shard_map/ppermute | solution.py:582
  37.5 0.0 collective-permute-done.4.near_ref
  37.6 5.6 %collective-permute-start.5 = (f32[16,2048]{1,0:T(8,128)S(1)}, f32[16,2048]{1,0:T(8,128)S(1)}, u32[]{:S(2)}, u32[]{:S(2)}) collective-permute-start(f32[16,2048]{1,0:T(8,128)S(1)} %get-tuple-element.86), channel_id=1, source_target_pairs={{0,16},{16,0},{32,48},{48,32},{64,80},{80,64},{96,112},{112,96},{1... | collective-permute-start | bytes 393224 | tf_op jit(solution)/shard_map/ppermute | solution.py:593
  43.2 1.0 %collective-permute-done.5.handed_ref = f32[16,2048]{1,0:T(8,128)S(1)} collective-permute-done((f32[16,2048]{1,0:T(8,128)S(1)}, f32[16,2048]{1,0:T(8,128)S(1)}, u32[]{:S(2)}, u32[]{:S(2)}) %collective-permute-start.5) | collective-permute-done | bytes 131104 | tf_op jit(solution)/shard_map/ppermute | solution.py:593
  44.1 1.0 %edge_gradients.1 = (f32[16,2048]{1,0:T(8,128)S(1)}, f32[16,2048]{1,0:T(8,128)S(1)}, f32[24,2048]{1,0:T(8,128)S(1)}) custom-call(s32[10]{0:T(128)S(1)} %pad_add_fusion.spot_ref, f32[16,512,128]{2,1,0:T(8,128)S(1)} %get-tuple-element.63.raw_ref, f32[16,384,128]{2,1,0:T(8,128)S(1)} %get-tuple-element.71.feat_ref, ...), custom_call_target="tpu_custom_call" | custom-call | flops 67108864 | bytes 8388608 | tf_op jit(solution)/shard_map/edge_gradients/pallas_call | solution.py:463
  45.2 2.3 %collective-permute-start.6 = (f32[24,2048]{1,0:T(8,128)S(1)}, f32[24,2048]{1,0:T(8,128)S(1)}, u32[]{:S(2)}, u32[]{:S(2)}) collective-permute-start(f32[24,2048]{1,0:T(8,128)S(1)} %get-tuple-element.92), channel_id=1, source_target_pairs={{16,0},{32,16},{48,32},{64,48},{80,64},{96,80},{112,96},{128,112},... | collective-permute-start | bytes 589832 | tf_op jit(solution)/shard_map/ppermute | solution.py:596
  47.5 6.9 %filter_gradients.1 = (bf16[128,2048]{1,0:T(8,128)(2,1)}, f32[16,384,128]{2,1,0:T(8,128)S(1)}, f32[8,40,128]{2,1,0:T(8,128)S(1)}, f32[8,40,128]{2,1,0:T(8,128)S(1)}) custom-call(s32[10]{0:T(128)S(1)} %pad_add_fusion.spot_ref, f32[16,512,128]{2,1,0:T(8,128)S(1)} %get-tuple-element.63.raw_ref, f32[16,384,128]{2,1,0:T(8,128)S(1)} %get-tuple-element.71.feat_ref, ...), custom_call_target="tpu_custom_call" | custom-call | flops 67108864 | bytes 8388608 | tf_op jit(solution)/shard_map/filter_gradients/pallas_call | solution.py:463
  54.3 0.0 collective-permute-done.6.edge_ref
  54.3 0.0 collective-permute-start.7
  54.3 1.4 %collective-permute-done.7 = f32[8,40,128]{2,1,0:T(8,128)S(1)} collective-permute-done((f32[8,40,128]{2,1,0:T(8,128)S(1)}, f32[8,40,128]{2,1,0:T(8,128)S(1)}, u32[]{:S(2)}, u32[]{:S(2)}) %collective-permute-start.7) | collective-permute-done | bytes 163872 | tf_op jit(solution)/shard_map/ppermute | solution.py:603
  55.8 2.8 %collective-permute-start.10 = (f32[2,40,128]{2,1,0:T(8,128)S(1)}, f32[2,40,128]{2,1,0:T(8,128)S(1)}, u32[]{:S(2)}, u32[]{:S(2)}) collective-permute-start(f32[2,40,128]{2,1,0:T(8,128)S(1)} %get-tuple-element.119), channel_id=1, source_target_pairs={{0,3},{1,2},{2,1},{3,0},{4,7},{5,6},{6,5},{7,4},{8,11},{9,10},{10,... | collective-permute-start | bytes 122888 | tf_op jit(solution)/shard_map/ppermute | solution.py:603
  58.6 0.0 collective-permute-start.8
  58.6 1.3 %collective-permute-start.9 = (f32[2,40,128]{2,1,0:T(8,128)S(1)}, f32[2,40,128]{2,1,0:T(8,128)S(1)}, u32[]{:S(2)}, u32[]{:S(2)}) collective-permute-start(f32[2,40,128]{2,1,0:T(8,128)S(1)} %get-tuple-element.120), channel_id=1, source_target_pairs={{0,2},{1,3},{2,0},{3,1},{4,6},{5,7},{6,4},{7,5},{8,10},{9,11},{10,... | collective-permute-start | bytes 122888 | tf_op jit(solution)/shard_map/ppermute | solution.py:603
  59.9 0.1 collective-permute-done.10
  60.0 1.5 %collective-permute-done.8 = f32[2,40,128]{2,1,0:T(8,128)S(1)} collective-permute-done((f32[2,40,128]{2,1,0:T(8,128)S(1)}, f32[2,40,128]{2,1,0:T(8,128)S(1)}, u32[]{:S(2)}, u32[]{:S(2)}) %collective-permute-start.8) | collective-permute-done | bytes 40992 | tf_op jit(solution)/shard_map/ppermute | solution.py:603
  61.4 1.5 %collective-permute-done.9 = f32[2,40,128]{2,1,0:T(8,128)S(1)} collective-permute-done((f32[2,40,128]{2,1,0:T(8,128)S(1)}, f32[2,40,128]{2,1,0:T(8,128)S(1)}, u32[]{:S(2)}, u32[]{:S(2)}) %collective-permute-start.9) | collective-permute-done | bytes 40992 | tf_op jit(solution)/shard_map/ppermute | solution.py:603
  63.0 1.2 %collective-permute-start.11 = (f32[2,40,128]{2,1,0:T(8,128)S(1)}, f32[2,40,128]{2,1,0:T(8,128)S(1)}, u32[]{:S(2)}, u32[]{:S(2)}) collective-permute-start(f32[2,40,128]{2,1,0:T(8,128)S(1)} %fusion), channel_id=1, source_target_pairs={{0,32},{16,48},{32,0},{48,16},{64,96},{80,112},{96,64},{112,80},{1... | collective-permute-start | bytes 122888 | tf_op jit(solution)/shard_map/ppermute | solution.py:603
  64.2 1.8 %input_gradient.3 = bf16[128,2048]{1,0:T(8,128)(2,1)} custom-call(f32[16,384,128]{2,1,0:T(8,128)S(1)} %get-tuple-element.96.gfeat_ref, f32[24,2048]{1,0:T(8,128)S(1)} %collective-permute-done.6.edge_ref, f32[3,7,2048]{2,1,0:T(8,128)S(1)} %get-tuple-element.68.taps_ref, f32[6,22,8,128]{3,2,1,0:T(8,128)S(1)} %get-tuple-element.64.masks), custom_call_target="tpu_custom_call" | custom-call | flops 67108864 | bytes 8388608 | tf_op jit(solution)/shard_map/input_gradient/pallas_call | solution.py:463
  66.0 0.0 collective-permute-done.11
  66.0 0.6 collective-permute-start.12
  66.6 2.3 %collective-permute-start.13 = (f32[2,40,128]{2,1,0:T(8,128)S(1)}, f32[2,40,128]{2,1,0:T(8,128)S(1)}, u32[]{:S(2)}, u32[]{:S(2)}) collective-permute-start(f32[2,40,128]{2,1,0:T(8,128)S(1)} %add.28), channel_id=1, source_target_pairs={{0,128},{16,144},{32,160},{48,176},{64,192},{80,208},{96,224},{112... | collective-permute-start | bytes 122888 | tf_op jit(solution)/shard_map/ppermute | solution.py:603
  68.9 2.9 %collective-permute-start.14 = (f32[2,40,128]{2,1,0:T(8,128)S(1)}, f32[2,40,128]{2,1,0:T(8,128)S(1)}, u32[]{:S(2)}, u32[]{:S(2)}) collective-permute-start(f32[2,40,128]{2,1,0:T(8,128)S(1)} %add.28), channel_id=1, source_target_pairs={{0,192},{16,208},{32,224},{48,240},{64,128},{80,144},{96,160},{112... | collective-permute-start | bytes 122888 | tf_op jit(solution)/shard_map/ppermute | solution.py:603
  71.7 1.8 %input_gradient.4 = bf16[128,2048]{1,0:T(8,128)(2,1)} custom-call(f32[16,384,128]{2,1,0:T(8,128)S(1)} %get-tuple-element.96.gfeat_ref, f32[24,2048]{1,0:T(8,128)S(1)} %collective-permute-done.6.edge_ref, f32[3,7,2048]{2,1,0:T(8,128)S(1)} %get-tuple-element.68.taps_ref, f32[6,22,8,128]{3,2,1,0:T(8,128)S(1)} %get-tuple-element.64.masks), custom_call_target="tpu_custom_call" | custom-call | flops 67108864 | bytes 8388608 | tf_op jit(solution)/shard_map/input_gradient/pallas_call | solution.py:463
  73.5 0.0 collective-permute-done.12
  73.5 0.1 collective-permute-done.13
  73.6 0.8 collective-permute-done.14
  74.4 1.6 %collective-permute-start.15 = (f32[2,40,128]{2,1,0:T(8,128)S(1)}, f32[2,40,128]{2,1,0:T(8,128)S(1)}, u32[]{:S(2)}, u32[]{:S(2)}) collective-permute-start(f32[2,40,128]{2,1,0:T(8,128)S(1)} %add_add_fusion), channel_id=1, source_target_pairs={{0,1},{1,0},{2,3},{3,2},{4,5},{5,4},{6,7},{7,6},{8,9},{9,8},{10,11... | collective-permute-start | bytes 122888 | tf_op jit(solution)/shard_map/ppermute | solution.py:603
  76.0 0.9 collective-permute-start.16
  76.9 1.6 %collective-permute-start.17 = (f32[2,40,128]{2,1,0:T(8,128)S(1)}, f32[2,40,128]{2,1,0:T(8,128)S(1)}, u32[]{:S(2)}, u32[]{:S(2)}) collective-permute-start(f32[2,40,128]{2,1,0:T(8,128)S(1)} %add_add_fusion), channel_id=1, source_target_pairs={{0,3},{1,2},{2,1},{3,0},{4,7},{5,6},{6,5},{7,4},{8,11},{9,10},{10,... | collective-permute-start | bytes 122888 | tf_op jit(solution)/shard_map/ppermute | solution.py:603
  78.5 1.8 %input_gradient.5 = bf16[128,2048]{1,0:T(8,128)(2,1)} custom-call(f32[16,384,128]{2,1,0:T(8,128)S(1)} %get-tuple-element.96.gfeat_ref, f32[24,2048]{1,0:T(8,128)S(1)} %collective-permute-done.6.edge_ref, f32[3,7,2048]{2,1,0:T(8,128)S(1)} %get-tuple-element.68.taps_ref, f32[6,22,8,128]{3,2,1,0:T(8,128)S(1)} %get-tuple-element.64.masks), custom_call_target="tpu_custom_call" | custom-call | flops 67108864 | bytes 8388608 | tf_op jit(solution)/shard_map/input_gradient/pallas_call | solution.py:463
  80.3 0.0 collective-permute-done.15
  80.3 0.1 collective-permute-done.16
  80.4 0.6 collective-permute-done.17
  80.9 6.0 %collective-permute-start.18 = (f32[8,40,128]{2,1,0:T(8,128)S(1)}, f32[8,40,128]{2,1,0:T(8,128)S(1)}, u32[]{:S(2)}, u32[]{:S(2)}) collective-permute-start(f32[8,40,128]{2,1,0:T(8,128)S(1)} %pad_maximum_fusion.kept_ref), channel_id=1, source_target_pairs={{0,16},{16,0},{32,48},{48,32},{64,80},{80,64},{96,112},{112,96},{1... | collective-permute-start | bytes 491528 | tf_op jit(solution)/shard_map/ppermute | solution.py:603
  87.0 1.0 %collective-permute-done.18.away_ref = f32[8,40,128]{2,1,0:T(8,128)S(1)} collective-permute-done((f32[8,40,128]{2,1,0:T(8,128)S(1)}, f32[8,40,128]{2,1,0:T(8,128)S(1)}, u32[]{:S(2)}, u32[]{:S(2)}) %collective-permute-start.18) | collective-permute-done | bytes 163872 | tf_op jit(solution)/shard_map/ppermute | solution.py:603
  88.0 1.9 %parameter_gradients.1 = (f32[3,7,2048]{2,1,0:T(8,128)}, f32[16,2048]{1,0:T(8,128)}, f32[1,2048]{1,0:T(1,128)}) custom-call(s32[10]{0:T(128)S(1)} %pad_add_fusion.spot_ref, f32[8,40,128]{2,1,0:T(8,128)S(1)} %pad_maximum_fusion.kept_ref, f32[8,40,128]{2,1,0:T(8,128)S(1)} %collective-permute-done.18.away_ref), custom_call_target="tpu_custom_call" | custom-call | flops 67108864 | bytes 8388608 | tf_op jit(solution)/shard_map/parameter_gradients/pallas_call | solution.py:463
  (10 shorter events, 0.2 us)
Async XLA Ops:
  0.6 10.0 %copy-start = (s32[1,8]{1,0:T(1,128)S(1)}, s32[1,8]{1,0:T(1,128)}, u32[]{:S(2)}) copy-start(s32[1,8]{1,0:T(1,128)} %lengths_in.1) | copy-start | bytes 100
  1.7 9.0 %collective-permute-start = (bf16[32,2048]{1,0:T(8,128)(2,1)S(1)}, bf16[32,2048]{1,0:T(8,128)(2,1)S(1)}, u32[]{:S(2)}, u32[]{:S(2)}) collective-permute-start(bf16[32,2048]{1,0:T(8,128)(2,1)S(1)} %last_rows.1), channel_id=1, source_target_pairs={{0,16},{16,32},{32,48},{48,64},{64,80},{80,96},{96,112},{112,128},... | collective-permute-start | bytes 393224 | tf_op jit(solution)/shard_map/ppermute | solution.py:571
  17.1 1.4 %collective-permute-start.1 = (f32[16,2048]{1,0:T(8,128)S(1)}, f32[16,2048]{1,0:T(8,128)S(1)}, u32[]{:S(2)}, u32[]{:S(2)}) collective-permute-start(f32[16,2048]{1,0:T(8,128)S(1)} %get-tuple-element.72.sent_ref), channel_id=1, source_target_pairs={{0,16},{16,0},{32,48},{48,32},{64,80},{80,64},{96,112},{112,96},{1... | collective-permute-start | bytes 393224 | tf_op jit(solution)/shard_map/ppermute | solution.py:584
  18.6 5.9 %collective-permute-start.2 = (f32[16,2048]{1,0:T(8,128)S(1)}, f32[16,2048]{1,0:T(8,128)S(1)}, u32[]{:S(2)}, u32[]{:S(2)}) collective-permute-start(f32[16,2048]{1,0:T(8,128)S(1)} %combine.2.first_ref), channel_id=1, source_target_pairs={{0,32},{32,64},{48,16},{64,96},{80,48},{96,128},{112,80},{128,160}... | collective-permute-start | bytes 393224 | tf_op jit(solution)/shard_map/ppermute | solution.py:582
  24.5 13.1 %collective-permute-start.3 = (f32[16,2048]{1,0:T(8,128)S(1)}, f32[16,2048]{1,0:T(8,128)S(1)}, u32[]{:S(2)}, u32[]{:S(2)}) collective-permute-start(f32[16,2048]{1,0:T(8,128)S(1)} %combine.3), channel_id=1, source_target_pairs={{0,96},{32,128},{64,160},{96,192},{112,16},{128,224},{144,48},{176... | collective-permute-start | bytes 393224 | tf_op jit(solution)/shard_map/ppermute | solution.py:582
  25.8 11.8 %collective-permute-start.4 = (f32[16,2048]{1,0:T(8,128)S(1)}, f32[16,2048]{1,0:T(8,128)S(1)}, u32[]{:S(2)}, u32[]{:S(2)}) collective-permute-start(f32[16,2048]{1,0:T(8,128)S(1)} %combine.3), channel_id=1, source_target_pairs={{0,32},{32,64},{48,16},{64,96},{80,48},{96,128},{112,80},{128,160}... | collective-permute-start | bytes 393224 | tf_op jit(solution)/shard_map/ppermute | solution.py:582
  37.6 6.6 %collective-permute-start.5 = (f32[16,2048]{1,0:T(8,128)S(1)}, f32[16,2048]{1,0:T(8,128)S(1)}, u32[]{:S(2)}, u32[]{:S(2)}) collective-permute-start(f32[16,2048]{1,0:T(8,128)S(1)} %get-tuple-element.86), channel_id=1, source_target_pairs={{0,16},{16,0},{32,48},{48,32},{64,80},{80,64},{96,112},{112,96},{1... | collective-permute-start | bytes 393224 | tf_op jit(solution)/shard_map/ppermute | solution.py:593
  45.2 9.1 %collective-permute-start.6 = (f32[24,2048]{1,0:T(8,128)S(1)}, f32[24,2048]{1,0:T(8,128)S(1)}, u32[]{:S(2)}, u32[]{:S(2)}) collective-permute-start(f32[24,2048]{1,0:T(8,128)S(1)} %get-tuple-element.92), channel_id=1, source_target_pairs={{16,0},{32,16},{48,32},{64,48},{80,64},{96,80},{112,96},{128,112},... | collective-permute-start | bytes 589832 | tf_op jit(solution)/shard_map/ppermute | solution.py:596
  54.3 1.4 %collective-permute-start.7 = (f32[8,40,128]{2,1,0:T(8,128)S(1)}, f32[8,40,128]{2,1,0:T(8,128)S(1)}, u32[]{:S(2)}, u32[]{:S(2)}) collective-permute-start(f32[8,40,128]{2,1,0:T(8,128)S(1)} %get-tuple-element.93), channel_id=1, source_target_pairs={{0,16},{16,0},{32,48},{48,32},{64,80},{80,64},{96,112},{112,96},{1... | collective-permute-start | bytes 491528 | tf_op jit(solution)/shard_map/ppermute | solution.py:603
  55.8 4.2 %collective-permute-start.10 = (f32[2,40,128]{2,1,0:T(8,128)S(1)}, f32[2,40,128]{2,1,0:T(8,128)S(1)}, u32[]{:S(2)}, u32[]{:S(2)}) collective-permute-start(f32[2,40,128]{2,1,0:T(8,128)S(1)} %get-tuple-element.119), channel_id=1, source_target_pairs={{0,3},{1,2},{2,1},{3,0},{4,7},{5,6},{6,5},{7,4},{8,11},{9,10},{10,... | collective-permute-start | bytes 122888 | tf_op jit(solution)/shard_map/ppermute | solution.py:603
  58.6 2.9 %collective-permute-start.8 = (f32[2,40,128]{2,1,0:T(8,128)S(1)}, f32[2,40,128]{2,1,0:T(8,128)S(1)}, u32[]{:S(2)}, u32[]{:S(2)}) collective-permute-start(f32[2,40,128]{2,1,0:T(8,128)S(1)} %get-tuple-element.121), channel_id=1, source_target_pairs={{0,1},{1,0},{2,3},{3,2},{4,5},{5,4},{6,7},{7,6},{8,9},{9,8},{10,11... | collective-permute-start | bytes 122888 | tf_op jit(solution)/shard_map/ppermute | solution.py:603
  58.6 4.4 %collective-permute-start.9 = (f32[2,40,128]{2,1,0:T(8,128)S(1)}, f32[2,40,128]{2,1,0:T(8,128)S(1)}, u32[]{:S(2)}, u32[]{:S(2)}) collective-permute-start(f32[2,40,128]{2,1,0:T(8,128)S(1)} %get-tuple-element.120), channel_id=1, source_target_pairs={{0,2},{1,3},{2,0},{3,1},{4,6},{5,7},{6,4},{7,5},{8,10},{9,11},{10,... | collective-permute-start | bytes 122888 | tf_op jit(solution)/shard_map/ppermute | solution.py:603
  63.0 3.0 %collective-permute-start.11 = (f32[2,40,128]{2,1,0:T(8,128)S(1)}, f32[2,40,128]{2,1,0:T(8,128)S(1)}, u32[]{:S(2)}, u32[]{:S(2)}) collective-permute-start(f32[2,40,128]{2,1,0:T(8,128)S(1)} %fusion), channel_id=1, source_target_pairs={{0,32},{16,48},{32,0},{48,16},{64,96},{80,112},{96,64},{112,80},{1... | collective-permute-start | bytes 122888 | tf_op jit(solution)/shard_map/ppermute | solution.py:603
  66.0 7.5 %collective-permute-start.12 = (f32[2,40,128]{2,1,0:T(8,128)S(1)}, f32[2,40,128]{2,1,0:T(8,128)S(1)}, u32[]{:S(2)}, u32[]{:S(2)}) collective-permute-start(f32[2,40,128]{2,1,0:T(8,128)S(1)} %add.28), channel_id=1, source_target_pairs={{0,64},{16,80},{32,96},{48,112},{64,0},{80,16},{96,32},{112,48},{1... | collective-permute-start | bytes 122888 | tf_op jit(solution)/shard_map/ppermute | solution.py:603
  66.6 7.0 %collective-permute-start.13 = (f32[2,40,128]{2,1,0:T(8,128)S(1)}, f32[2,40,128]{2,1,0:T(8,128)S(1)}, u32[]{:S(2)}, u32[]{:S(2)}) collective-permute-start(f32[2,40,128]{2,1,0:T(8,128)S(1)} %add.28), channel_id=1, source_target_pairs={{0,128},{16,144},{32,160},{48,176},{64,192},{80,208},{96,224},{112... | collective-permute-start | bytes 122888 | tf_op jit(solution)/shard_map/ppermute | solution.py:603
  68.9 5.6 %collective-permute-start.14 = (f32[2,40,128]{2,1,0:T(8,128)S(1)}, f32[2,40,128]{2,1,0:T(8,128)S(1)}, u32[]{:S(2)}, u32[]{:S(2)}) collective-permute-start(f32[2,40,128]{2,1,0:T(8,128)S(1)} %add.28), channel_id=1, source_target_pairs={{0,192},{16,208},{32,224},{48,240},{64,128},{80,144},{96,160},{112... | collective-permute-start | bytes 122888 | tf_op jit(solution)/shard_map/ppermute | solution.py:603
  74.4 5.8 %collective-permute-start.15 = (f32[2,40,128]{2,1,0:T(8,128)S(1)}, f32[2,40,128]{2,1,0:T(8,128)S(1)}, u32[]{:S(2)}, u32[]{:S(2)}) collective-permute-start(f32[2,40,128]{2,1,0:T(8,128)S(1)} %add_add_fusion), channel_id=1, source_target_pairs={{0,1},{1,0},{2,3},{3,2},{4,5},{5,4},{6,7},{7,6},{8,9},{9,8},{10,11... | collective-permute-start | bytes 122888 | tf_op jit(solution)/shard_map/ppermute | solution.py:603
  76.0 4.4 %collective-permute-start.16 = (f32[2,40,128]{2,1,0:T(8,128)S(1)}, f32[2,40,128]{2,1,0:T(8,128)S(1)}, u32[]{:S(2)}, u32[]{:S(2)}) collective-permute-start(f32[2,40,128]{2,1,0:T(8,128)S(1)} %add_add_fusion), channel_id=1, source_target_pairs={{0,2},{1,3},{2,0},{3,1},{4,6},{5,7},{6,4},{7,5},{8,10},{9,11},{10,... | collective-permute-start | bytes 122888 | tf_op jit(solution)/shard_map/ppermute | solution.py:603
  76.9 4.1 %collective-permute-start.17 = (f32[2,40,128]{2,1,0:T(8,128)S(1)}, f32[2,40,128]{2,1,0:T(8,128)S(1)}, u32[]{:S(2)}, u32[]{:S(2)}) collective-permute-start(f32[2,40,128]{2,1,0:T(8,128)S(1)} %add_add_fusion), channel_id=1, source_target_pairs={{0,3},{1,2},{2,1},{3,0},{4,7},{5,6},{6,5},{7,4},{8,11},{9,10},{10,... | collective-permute-start | bytes 122888 | tf_op jit(solution)/shard_map/ppermute | solution.py:603
  80.9 7.1 %collective-permute-start.18 = (f32[8,40,128]{2,1,0:T(8,128)S(1)}, f32[8,40,128]{2,1,0:T(8,128)S(1)}, u32[]{:S(2)}, u32[]{:S(2)}) collective-permute-start(f32[8,40,128]{2,1,0:T(8,128)S(1)} %pad_maximum_fusion.kept_ref), channel_id=1, source_target_pairs={{0,16},{16,0},{32,48},{48,32},{64,80},{80,64},{96,112},{112,96},{1... | collective-permute-start | bytes 491528 | tf_op jit(solution)/shard_map/ppermute | solution.py:603

commit v5 on v4

--- a/solution.py
+++ b/solution.py
@@ -21,8 +21,8 @@
 CHUNKS = 4
 COT = 3
 SOURCE, GRAD, GSEG, SLOC, RLOC = range(5)
-CONV, BACK, SWT, RWT, SCOEF, RCOEF = range(6)
-NEAR_TERMS, FAR_TERMS, CONV_ROWS, BACK_ROWS, FIRST_ROWS = 0, HALO * MODES, 2 * HALO * MODES, 2 * HALO * MODES + 8, 208
+CONV, BACK = range(2)
+SWT, RWT, SCOEF, RCOEF = range(4)
 
 
 def slab(block, index):
@@ -239,25 +239,16 @@
     each_tile(raw_ref.shape[0], tile_body)
 
 
-def local_kernel(
-    spot_ref, pre_ref, rate_ref, decay_ref, residue_ref, skip_ref, open_mask, end_mask,
-    post_ref, local_ref, first_ref,
-    masks, reach, stage, weight_stage,
+def segment_kernel(
+    spot_ref, pre_ref, rate_ref, decay_ref, residue_ref, skip_ref,
+    near_ref, pair_ref,
+    masks,
 ):
-    starts, anchor = starts_of(spot_ref), spot_ref[0] * ROWS
-
-    store_masks(starts, anchor, masks, STEPS, STEPS - 1)
-    before = since_start(starts, anchor + segments() * STEPS - 1)
-    reach[0] = flag((before >= segments() * STEPS) | (segments() == 0))
-    at_end = since_start(starts, anchor + segments() * 0 + ROWS - 1)
-    reach[1] = flag(at_end >= (SEGS - 1 - segments()) * STEPS)
-
-    def tile_body(tile, lanes):
-        segment = segments().astype(F32)
-        rates = rate_ref[:, lanes]
+    store_masks(starts_of(spot_ref), spot_ref[0] * ROWS, masks, STEPS, STEPS - 1)
+
+    def tile_body(tile, lanes):
         decay = decay_ref[:, lanes]
-        power = residue_ref[:, lanes] * jnp.sqrt(rates)
-        weight_stage[...] = power * decay
+        power = residue_ref[:, lanes] * jnp.sqrt(rate_ref[:, lanes])
         kernel = []
         for gap in range(STEPS):
             kernel.append(jnp.sum(power, axis=0, keepdims=True))
@@ -265,7 +256,7 @@
         kernel[0] = kernel[0] + skip_ref[:, lanes]
         source = [pre_ref[tile, slab(SOURCE, t)] for t in range(STEPS)]
         grads = [pre_ref[tile, slab(GRAD, t)] for t in range(STEPS)]
-        conv, back, paired = [None] * STEPS, [None] * STEPS, []
+        conv, back = [None] * STEPS, [None] * STEPS
         for gap in range(STEPS):
             weight = jnp.broadcast_to(kernel[gap], (SEGS, LANES))
             pair = jnp.zeros((SEGS, LANES), F32)
@@ -276,25 +267,33 @@
                 conv[t] = weight * value if gap == 0 else conv[t] + weight * value
                 back[t - gap] = weight * grad if gap == 0 else back[t - gap] + weight * grad
                 pair = pair + grads[t] * value
-            paired.append(jnp.sum(pair, axis=0, keepdims=True))
+            pair_ref[tile, gap : gap + 1] = jnp.sum(pair, axis=0, keepdims=True)
         for t in range(STEPS):
-            post_ref[tile, slab(CONV, t)] = conv[t]
-            post_ref[tile, slab(BACK, t)] = back[t]
-        scaled = [weight_stage[...]]
-        for t in range(1, STEPS):
-            scaled.append(scaled[-1] * decay)
-        later = pre_ref[tile, pl.ds(RLOC * ROWS, MODES, stride=SEGS), :]
-        beyond = reach[1, :1] * jnp.exp(rates * -float(ROWS - STEPS))
-        for t in range(HALO):
-            far_term = end_mask[t, :1] * scaled[STEPS - 1 - t]
-            first_ref[tile, NEAR_TERMS + t * MODES : NEAR_TERMS + (t + 1) * MODES] = open_mask[t, :1] * scaled[t]
-            first_ref[tile, FAR_TERMS + t * MODES : FAR_TERMS + (t + 1) * MODES] = far_term * beyond
-            back_row = back[t][:1] + jnp.sum(far_term * later, axis=0, keepdims=True)
-            first_ref[tile, CONV_ROWS + t : CONV_ROWS + t + 1] = conv[t][:1]
-            first_ref[tile, BACK_ROWS + t : BACK_ROWS + t + 1] = back_row
-        total = jnp.broadcast_to(paired[STEPS - 1], (MODES, LANES))
+            near_ref[tile, slab(CONV, t)] = conv[t]
+            near_ref[tile, slab(BACK, t)] = back[t]
+
+    each_tile(pre_ref.shape[0], tile_body)
+
+
+def local_kernel(
+    spot_ref, pre_ref, pair_ref, rate_ref, decay_ref, residue_ref,
+    post_ref, local_ref,
+    reach, stage, weight_stage,
+):
+    starts, anchor = starts_of(spot_ref), spot_ref[0] * ROWS
+    before = since_start(starts, anchor + segments() * STEPS - 1)
+    reach[0] = flag((before >= segments() * STEPS) | (segments() == 0))
+    at_end = since_start(starts, anchor + segments() * 0 + ROWS - 1)
+    reach[1] = flag(at_end >= (SEGS - 1 - segments()) * STEPS)
+
+    def tile_body(tile, lanes):
+        segment = segments().astype(F32)
+        rates = rate_ref[:, lanes]
+        decay = decay_ref[:, lanes]
+        weight_stage[...] = residue_ref[:, lanes] * jnp.sqrt(rates) * decay
+        total = jnp.broadcast_to(pair_ref[tile, STEPS - 1 : STEPS], (MODES, LANES))
         for gap in range(STEPS - 2, -1, -1):
-            total = total * decay + paired[gap]
+            total = total * decay + pair_ref[tile, gap : gap + 1]
         for m in range(MODES):
             arriving = pre_ref[tile, slab(SLOC, m)]
             stage[m : m + 1, :] = jnp.sum(arriving * pre_ref[tile, slab(GSEG, m)], axis=0, keepdims=True)
@@ -305,7 +304,7 @@
             post_ref[tile, slab(SCOEF, m)] = scale * reach[0] * jnp.exp(rate * segment)
             post_ref[tile, slab(RCOEF, m)] = scale * reach[1] * jnp.exp(rate * (SEGS - 1 - segment))
         local_ref[tile, 0:MODES] = total + stage[...] * decay
-        local_ref[tile, MODES : MODES + 8] = jnp.broadcast_to(paired[0], (8, LANES))
+        local_ref[tile, MODES : MODES + 8] = jnp.broadcast_to(pair_ref[tile, 0:1], (8, LANES))
 
     each_tile(pre_ref.shape[0], tile_body)
 
@@ -326,76 +325,68 @@
     return half, high * 4 + low * 2 + slot % 2
 
 
-def edge_kernel(
-    spot_ref, raw_ref, feat_ref, first_ref, arrived_ref, handed_ref, enter_ref, return_ref, edge_ref
+def gradient_kernel(
+    spot_ref, raw_ref, feat_ref, near_ref, post_ref, local_ref, arrived_ref, handed_ref, own_ref, sent_ref, rate_ref, decay_ref, halo_ref,
+    masks, open_mask, end_mask,
+    out_ref, gfeat_ref, edge_ref, kept_ref, away_ref,
+    stage, rounded, written, states,
 ):
     lower = spot_ref[0] % 2 == 0
 
-    def tile_body(tile, lanes):
+    chunk = rounded.shape[1] // CHUNKS
+
+    def write(part):
+        cols = pl.ds(pl.multiple_of(part * chunk, LANES), chunk)
+        return pltpu.make_async_copy(rounded.at[:, cols], out_ref.at[:, cols], written.at[part])
+
+    def tile_body(tile, lanes):
+        decay = [row(decay_ref, m, lanes) for m in range(MODES)]
         arrived, handed = arrived_ref[:, lanes], handed_ref[:, lanes]
-        entering, returning = jnp.where(lower, arrived, handed), jnp.where(lower, handed, arrived)
-        enter_ref[:, lanes] = entering
-        return_ref[:, lanes] = returning
-        for t in range(HALO):
-            near = first_ref[tile, NEAR_TERMS + t * MODES : NEAR_TERMS + (t + 1) * MODES]
-            far = first_ref[tile, FAR_TERMS + t * MODES : FAR_TERMS + (t + 1) * MODES]
-            filtered = first_ref[tile, CONV_ROWS + t : CONV_ROWS + t + 1]
-            filtered = filtered + jnp.sum(near * entering, axis=0, keepdims=True)
-            grad = first_ref[tile, BACK_ROWS + t : BACK_ROWS + t + 1]
-            grad = grad + jnp.sum(far * returning, axis=0, keepdims=True)
-            edge_ref[t : t + 1, lanes] = raw_ref[tile, slab(COT, t)][:1] * filtered
-            edge_ref[8 + t : 9 + t, lanes] = grad * feat_ref[tile, slab(2, t)][:1]
-            edge_ref[16 + t : 17 + t, lanes] = grad * feat_ref[tile, slab(1, t)][:1]
-        for branch in range(3):
-            edge_ref[branch * 8 + HALO : branch * 8 + 8, lanes] = jnp.zeros((8 - HALO, LANES), F32)
-
-    each_tile(raw_ref.shape[0], tile_body)
-
-
-def gradient_kernel(
-    spot_ref, raw_ref, feat_ref, post_ref, local_ref, enter_ref, return_ref, own_ref, sent_ref, rate_ref, decay_ref, halo_ref,
-    masks, open_mask, end_mask,
-    out_ref, gfeat_ref, kept_ref, away_ref,
-    stage,
-):
-    lower = spot_ref[0] % 2 == 0
-
-    def tile_body(tile, lanes):
-        decay = [row(decay_ref, m, lanes) for m in range(MODES)]
+        entering = jnp.where(lower, arrived, handed)
+        states[0:MODES] = entering
+        states[MODES:] = jnp.where(lower, handed, arrived)
         state = [
-            post_ref[tile, slab(SWT, m)] + post_ref[tile, slab(SCOEF, m)] * row(enter_ref, m, lanes)
+            post_ref[tile, slab(SWT, m)] + post_ref[tile, slab(SCOEF, m)] * row(states, m, slice(None))
             for m in range(MODES)
         ]
         for t in range(STEPS):
-            filtered = post_ref[tile, slab(CONV, t)] + open_mask[t] * tree_sum(state)
+            filtered = near_ref[tile, slab(CONV, t)] + open_mask[t] * tree_sum(state)
             stage[pl.ds(t, SEGS, stride=STEPS), :] = feat_ref[tile, slab(0, t)] * filtered
             gfeat_ref[tile, slab(0, t)] = raw_ref[tile, slab(COT, t)] * filtered
             if t < STEPS - 1:
                 state = [d * s for d, s in zip(decay, state)]
-        out_ref[:, lanes] = stage[...].astype(out_ref.dtype)
+        rounded[:, lanes] = stage[...].astype(rounded.dtype)
+
+        @pl.when(tile % (chunk // LANES) == chunk // LANES - 1)
+        def _():
+            write(tile // (chunk // LANES)).start()
+
         state = [
-            post_ref[tile, slab(RWT, m)] + post_ref[tile, slab(RCOEF, m)] * row(return_ref, m, lanes)
+            post_ref[tile, slab(RWT, m)] + post_ref[tile, slab(RCOEF, m)] * row(states, MODES + m, slice(None))
             for m in range(MODES)
         ]
         for t in range(STEPS - 1, -1, -1):
-            grad = post_ref[tile, slab(BACK, t)] + end_mask[t] * tree_sum(state)
+            grad = near_ref[tile, slab(BACK, t)] + end_mask[t] * tree_sum(state)
             gfeat_ref[tile, slab(1, t)] = grad * feat_ref[tile, slab(2, t)]
             gfeat_ref[tile, slab(2, t)] = grad * feat_ref[tile, slab(1, t)]
             if t:
                 state = [d * s for d, s in zip(decay, state)]
         rates = rate_ref[:, lanes]
         begin = jnp.where(lower, sent_ref[:, lanes], own_ref[:, lanes])
-        sums = [jnp.sqrt(rates) * (local_ref[tile, 0:MODES] + enter_ref[:, lanes] * decay_ref[:, lanes] * begin)]
+        sums = [jnp.sqrt(rates) * (local_ref[tile, 0:MODES] + entering * decay_ref[:, lanes] * begin)]
         for branch in range(3):
             totals = [jnp.zeros((SEGS, LANES), F32)] * TAPS
             rows = [raw_ref[tile, slab(branch, t)] for t in range(STEPS)]
             before = rows_before(rows, halo_ref, branch, lanes)
             for t in range(STEPS):
                 grad = gfeat_ref[tile, slab(branch, t)]
+                if t < HALO:
+                    edge_ref[branch * 8 + t : branch * 8 + t + 1, lanes] = grad[:1]
                 totals[0] = totals[0] + grad * rows[t]
                 for j in range(1, TAPS):
                     earlier = rows[t - j] if t >= j else before[t - j]
                     totals[j] = totals[j] + (grad * masks[j - 1, t]) * earlier
+            edge_ref[branch * 8 + HALO : branch * 8 + 8, lanes] = jnp.zeros((8 - HALO, LANES), F32)
             sums += [jnp.sum(total, axis=0, keepdims=True) for total in totals]
         sums.append(local_ref[tile, MODES : MODES + REDUCED - MODES - 3 * TAPS])
         half, slot = tile_slot(tile, spot_ref)
@@ -409,6 +400,8 @@
                     at += piece.shape[0]
 
     each_tile(raw_ref.shape[0], tile_body)
+    for part in range(CHUNKS):
+        write(part).wait()
 
 
 def input_kernel(branch, gfeat_ref, edge_ref, taps_ref, masks, out_ref, stage):
@@ -459,13 +452,13 @@
 STAGE = (ROWS, LANES)
 
 
-def call(body, name, ins, outs, scratch, *args, dtype=F32):
+def call(body, name, ins, outs, scratch, *args, dtype=F32, specs=None):
     return pl.pallas_call(
         body,
         name=name,
         out_shape=[out if isinstance(out, jax.ShapeDtypeStruct) else pltpu.VMEM(out, dtype) for out in outs],
         in_specs=ins,
-        out_specs=[VMEM] * len(outs),
+        out_specs=specs or [VMEM] * len(outs),
         scratch_shapes=[pltpu.VMEM(one, F32) if isinstance(one, tuple) else one for one in scratch],
         compiler_params=pltpu.CompilerParams(vmem_limit_bytes=VMEM_BYTES),
         cost_estimate=pl.CostEstimate(flops=1 << 26, bytes_accessed=8 << 20, transcendentals=0),
@@ -505,22 +498,25 @@
     )
 
 
-def local_filter(spot, pre, rate, decay, residue, skip, open_mask, end_mask):
+def segment_filter(spot, pre, *others):
+    tiles = pre.shape[0]
+    return call(
+        segment_kernel, "segment_filter",
+        [SMEM] + [VMEM] * (1 + len(others)),
+        [(tiles, 2 * ROWS, LANES), (tiles, STEPS, LANES)],
+        [(STEPS - 1, STEPS, SEGS, LANES)],
+        spot, pre, *others,
+    )
+
+
+def local_filter(spot, pre, *others):
     tiles = pre.shape[0]
     return call(
         local_kernel, "local_filter",
-        [SMEM] + [VMEM] * 7,
-        [(tiles, 6 * ROWS, LANES), (tiles, MODES + 8, LANES), (tiles, FIRST_ROWS, LANES)],
-        [(STEPS - 1, STEPS, SEGS, LANES), (2, SEGS, LANES), (MODES, LANES), (MODES, LANES)],
-        spot, pre, rate, decay, residue, skip, open_mask, end_mask,
-    )
-
-
-def edge_gradients(spot, raw, feat, first, arrived, handed):
-    states = arrived.shape
-    return call(
-        edge_kernel, "edge_gradients", [SMEM] + [VMEM] * 5, [states, states, (24, states[1])], [],
-        spot, raw, feat, first, arrived, handed,
+        [SMEM] + [VMEM] * (1 + len(others)),
+        [(tiles, 4 * ROWS, LANES), (tiles, MODES + 8, LANES)],
+        [(2, SEGS, LANES), (MODES, LANES), (MODES, LANES)],
+        spot, pre, *others,
     )
 
 
@@ -530,9 +526,9 @@
     return call(
         gradient_kernel, "filter_gradients",
         [SMEM] + [VMEM] * (1 + len(others)),
-        [jax.ShapeDtypeStruct((ROWS, tiles * LANES), BF16), (tiles, 3 * ROWS, LANES), half, half],
-        [STAGE],
-        spot, raw, *others,
+        [jax.ShapeDtypeStruct((ROWS, tiles * LANES), BF16), (tiles, 3 * ROWS, LANES), (24, tiles * LANES), half, half],
+        [STAGE, pltpu.VMEM((ROWS, tiles * LANES), BF16), pltpu.SemaphoreType.DMA((CHUNKS,)), (2 * MODES, LANES)],
+        spot, raw, *others, specs=[HBM] + [VMEM] * 4,
     )
 
 
@@ -582,46 +578,51 @@
         return lax.ppermute(value, "ctx", [(i, j) for i, j in moves if 0 <= j < count])
 
     chip_state = combine(1, lax.ppermute(sent, "ctx", pairs), through, own)
-    chip_state = combine(2, chip_state, through, onward(chip_state, 1))
+    chip_state, pre = lax.optimization_barrier((chip_state, pre))
+    near_rows, paired = segment_filter(spot, pre, rate, decay, residue, skip)
+    received, near_rows = lax.optimization_barrier((onward(chip_state, 1), near_rows))
+    chip_state = combine(2, chip_state, through, received)
     chip_state, pre = lax.optimization_barrier((chip_state, pre))
     near, far = onward(chip_state, 1), onward(chip_state, 3)
-    post, local, first = local_filter(spot, pre, rate, decay, residue, skip, open_mask, end_mask)
+    post, local = local_filter(spot, pre, paired, rate, decay, residue)
     far, post = lax.optimization_barrier((far, post))
     arrived, handed = call(
         arrive_kernel, "arrive", [VMEM] * 4, [own.shape, own.shape], [], near, far, own, through
     )
     handed = lax.ppermute(handed, "ctx", pairs)
 
-    entering, returning, edge = edge_gradients(spot, raw, feat, first, arrived, handed)
-    next_edge = lax.ppermute(edge, "ctx", [(i, i - 1) for i in range(1, count)])
-    block_out, gfeat, kept, away = filter_gradients(
-        spot, raw, feat, post, local, entering, returning, own, sent, rate, decay, halo, masks, open_mask, end_mask
-    )
-    away, next_edge = lax.optimization_barrier((away, next_edge))
+    block_out, gfeat, edge, kept, away = filter_gradients(
+        spot, raw, feat, near_rows, post, local, arrived, handed, own, sent, rate, decay, halo,
+        masks, open_mask, end_mask,
+    )
 
     def exchange(value, axis, flip):
         return lax.ppermute(value, axis, [(i, i ^ flip) for i in range(lax.axis_size(axis))])
 
     grad_inputs = []
 
-    def exchanges(sent, axis, flips, beside=True):
-        if not beside:
+    def exchanges(sent, axis, flips, beside):
+        if beside == 0:
             return [exchange(value, axis, flip) for value, flip in zip(sent, flips)]
         *sent, edge_now = lax.optimization_barrier((*sent, next_edge))
-        made = input_gradient(len(grad_inputs), gfeat, edge_now, taps, masks)
-        *received, made = lax.optimization_barrier((*exchanges(sent, axis, flips, False), made))
-        grad_inputs.append(made)
-        return received
+        made = [input_gradient(len(grad_inputs) + i, gfeat, edge_now, taps, masks) for i in range(beside)]
+        done = lax.optimization_barrier((*exchanges(sent, axis, flips, 0), *made))
+        grad_inputs.extend(done[len(sent) :])
+        return done[: len(sent)]
 
     total = kept + exchange(away, "ctx", 1)
     quarter = total.shape[0] // 4
     quarters = [total[quarter * i : quarter * (i + 1)] for i in range(4)]
-    one, two, three = exchanges(quarters[1:], "dp", (1, 2, 3), False)
+    quarters[1], edge = lax.optimization_barrier((quarters[1], edge))
+    next_edge = lax.ppermute(edge, "ctx", [(i, i - 1) for i in range(1, count)])
+    one, two, three, next_edge = lax.optimization_barrier(
+        (*exchanges(quarters[1:], "dp", (1, 2, 3), 0), next_edge)
+    )
     total = (quarters[0] + one) + (two + three)
-    total = total + exchanges([total], "ctx", (2,))[0]
-    one, two, three = exchanges([total] * 3, "ctx", (4, 8, 12))
+    total = total + exchange(total, "ctx", 2)
+    one, two, three = exchanges([total] * 3, "ctx", (4, 8, 12), 2)
     total = (total + one) + (two + three)
-    total = jnp.concatenate([total, *exchanges([total] * 3, "dp", (1, 2, 3))])
+    total = jnp.concatenate([total, *exchanges([total] * 3, "dp", (1, 2, 3), 1)])
     grad_short, grad_residue, grad_skip = results(spot, total, exchange(total, "ctx", 1))
     return (block_out[None], *(g[None] for g in grad_inputs), grad_short, grad_residue.T, grad_skip[0])
 

time: 90.1 us -> 89.6 us (level)
  starting transfers between devices: 37.9 us -> 36.7 us
  waiting for transfers between devices: 19.6 us -> 20.6 us
    ppermute x1, starting transfers between devices: 5.57 us -> 2.62 us  [per_device(): handed = lax.ppermute(handed, 'ctx', pairs)]
    ppermute x12, starting transfers between devices: 21.2 us -> 22.9 us  [exchange(): lax.ppermute(value, axis, [(i, i ^ flip) for i in range(lax.axis_size(axi...]
    ppermute x12, waiting for transfers between devices: 7.05 us -> 7.96 us  [exchange(): lax.ppermute(value, axis, [(i, i ^ flip) for i in range(lax.axis_size(axi...]
  transfers between devices with their start and end apart: 19 -> 19, of which waited for: 13 -> 10; matrix products, arithmetic and copies ran while one was open for 0% -> 0% of each run, Pallas kernels for 23% -> 16%
where the time goes in v5:
time: 89.6 us; the launch traced here: 89.3 us
  starting transfers between devices  36.7 us (41%)
  Pallas kernels  30.9 us (34%)
  waiting for transfers between devices  20.6 us (23%)
    pallas_call x13, Pallas kernels, call(): pl.pallas_call(body, name=name, out_shape=[out if isinstance(out, jax.Sha...  30.9 us
    ppermute x12, starting transfers between devices, exchange(): lax.ppermute(value, axis, [(i, i ^ flip) for i in range(lax.axis_size(axi...  22.9 us
    ppermute x3, waiting for transfers between devices, onward(): lax.ppermute(value, 'ctx', [(i, j) for i, j in moves if 0 <= j < count])  10.4 us
    ppermute x12, waiting for transfers between devices, exchange(): lax.ppermute(value, axis, [(i, i ^ flip) for i in range(lax.axis_size(axi...  7.96 us
    ppermute x1, starting transfers between devices, per_device(): lax.ppermute(tails(query_rows[0], key_rows[0], value_rows[0]), 'ctx', [(i...  4.94 us
    ppermute x3, starting transfers between devices, onward(): lax.ppermute(value, 'ctx', [(i, j) for i, j in moves if 0 <= j < count])  3.88 us
    ppermute x1, starting transfers between devices, per_device(): handed = lax.ppermute(handed, 'ctx', pairs)  2.62 us
    ppermute x1, starting transfers between devices, per_device(): next_edge = lax.ppermute(edge, 'ctx', [(i, i - 1) for i in range(1, count)])  2.27 us
  transfers between devices with their start and end apart: 19, of which 10 were waited for; matrix products, arithmetic and copies ran while one was open for 0% of the time, Pallas kernels for 16%

profile of v5, /device:TPU:1, one launch (start us, length us, event | category | flops | bytes accessed | tf_op | source)
XLA Modules:
  0.0 89.3 jit_solution(2008521390688319676)
XLA Ops:
  0.6 0.0 copy-start
  0.6 1.0 %last_rows.1 = bf16[32,2048]{1,0:T(8,128)(2,1)S(1)} custom-call(bf16[128,2048]{1,0:T(8,128)(2,1)} %bitcast.16, bf16[128,2048]{1,0:T(8,128)(2,1)} %bitcast.18, bf16[128,2048]{1,0:T(8,128)(2,1)} %bitcast.20), custom_call_target="tpu_custom_call" | custom-call | flops 67108864 | bytes 8388608 | tf_op jit(solution)/shard_map/last_rows/pallas_call | solution.py:456
  1.7 4.9 %collective-permute-start = (bf16[32,2048]{1,0:T(8,128)(2,1)S(1)}, bf16[32,2048]{1,0:T(8,128)(2,1)S(1)}, u32[]{:S(2)}, u32[]{:S(2)}) collective-permute-start(bf16[32,2048]{1,0:T(8,128)(2,1)S(1)} %last_rows.1), channel_id=1, source_target_pairs={{0,16},{16,32},{32,48},{48,64},{64,80},{80,96},{96,112},{112,128},... | collective-permute-start | bytes 393224 | tf_op jit(solution)/shard_map/ppermute | solution.py:567
  6.6 0.1 pad_add_fusion.1.place_ref
  6.7 3.9 %stage.1 = (f32[16,512,128]{2,1,0:T(8,128)S(1)}, f32[6,22,8,128]{3,2,1,0:T(8,128)S(1)}, f32[16,8,128]{2,1,0:T(8,128)S(1)}, f32[16,8,128]{2,1,0:T(8,128)S(1)}, f3...) custom-call(s32[2]{0:T(128)S(1)} %pad_add_fusion.1.place_ref, ...), custom_call_target="tpu_custom_call" | custom-call | flops 67108864 | bytes 8388608 | tf_op jit(solution)/shard_map/stage/pallas_call | solution.py:456
  10.6 0.0 copy-done
  10.6 0.1 pad_add_fusion.spot_ref
  10.7 0.0 collective-permute-done
  10.7 6.4 %features.1 = (f32[16,384,128]{2,1,0:T(8,128)S(1)}, f32[16,640,128]{2,1,0:T(8,128)S(1)}, f32[16,2048]{1,0:T(8,128)S(1)}, f32[16,2048]{1,0:T(8,128)S(1)}, f32[4,16,2048]{2,1,0:T(8,128)S(1)}) custom-call(s32[10]{0:T(128)S(1)} %pad_add_fusion.spot_ref, f32[16,512,128]{2,1,0:T(8,128)S(1)} %get-tuple-element.67.raw_ref, ...), custom_call_target="tpu_custom_call" | custom-call | flops 67108864 | bytes 8388608 | tf_op jit(solution)/shard_map/features/pallas_call | solution.py:456
  17.2 0.1 collective-permute-start.1
  17.3 1.3 %collective-permute-done.1.first_ref = f32[16,2048]{1,0:T(8,128)S(1)} collective-permute-done((f32[16,2048]{1,0:T(8,128)S(1)}, f32[16,2048]{1,0:T(8,128)S(1)}, u32[]{:S(2)}, u32[]{:S(2)}) %collective-permute-start.1) | collective-permute-done | bytes 131104 | tf_op jit(solution)/shard_map/ppermute | solution.py:580
  18.6 1.3 %collective-permute-start.2 = (f32[16,2048]{1,0:T(8,128)S(1)}, f32[16,2048]{1,0:T(8,128)S(1)}, u32[]{:S(2)}, u32[]{:S(2)}) collective-permute-start(f32[16,2048]{1,0:T(8,128)S(1)} %combine.2.first_ref), channel_id=1, source_target_pairs={{0,32},{32,64},{48,16},{64,96},{80,48},{96,128},{112,80},{128,160}... | collective-permute-start | bytes 393224 | tf_op jit(solution)/shard_map/ppermute | solution.py:578
  19.9 3.6 %segment_filter.1 = (f32[16,256,128]{2,1,0:T(8,128)S(1)}, f32[16,16,128]{2,1,0:T(8,128)S(1)}) custom-call(s32[10]{0:T(128)S(1)} %pad_add_fusion.spot_ref, f32[16,640,128]{2,1,0:T(8,128)S(1)} %get-tuple-element.88.pre_ref, f32[16,2048]{1,0:T(8,128)S(1)} %get-tuple-element.73.rate_ref, f32[16,2048]{1,0:T(8,128)S(1)} %get-tuple-element.74.decay_ref, ...), custom_call_target="tpu_custom_call" | custom-call | flops 67108864 | bytes 8388608 | tf_op jit(solution)/shard_map/segment_filter/pallas_call | solution.py:456
  23.5 1.0 %collective-permute-done.2.second_ref = f32[16,2048]{1,0:T(8,128)S(1)} collective-permute-done((f32[16,2048]{1,0:T(8,128)S(1)}, f32[16,2048]{1,0:T(8,128)S(1)}, u32[]{:S(2)}, u32[]{:S(2)}) %collective-permute-start.2) | collective-permute-done | bytes 131104 | tf_op jit(solution)/shard_map/ppermute | solution.py:578
  24.6 1.3 %collective-permute-start.3 = (f32[16,2048]{1,0:T(8,128)S(1)}, f32[16,2048]{1,0:T(8,128)S(1)}, u32[]{:S(2)}, u32[]{:S(2)}) collective-permute-start(f32[16,2048]{1,0:T(8,128)S(1)} %combine.3), channel_id=1, source_target_pairs={{0,96},{32,128},{64,160},{96,192},{112,16},{128,224},{144,48},{176... | collective-permute-start | bytes 393224 | tf_op jit(solution)/shard_map/ppermute | solution.py:578
  25.9 1.3 %collective-permute-start.4 = (f32[16,2048]{1,0:T(8,128)S(1)}, f32[16,2048]{1,0:T(8,128)S(1)}, u32[]{:S(2)}, u32[]{:S(2)}) collective-permute-start(f32[16,2048]{1,0:T(8,128)S(1)} %combine.3), channel_id=1, source_target_pairs={{0,32},{32,64},{48,16},{64,96},{80,48},{96,128},{112,80},{128,160}... | collective-permute-start | bytes 393224 | tf_op jit(solution)/shard_map/ppermute | solution.py:578
  27.2 1.7 %local_filter.1 = (f32[16,512,128]{2,1,0:T(8,128)S(1)}, f32[16,24,128]{2,1,0:T(8,128)S(1)}) custom-call(s32[10]{0:T(128)S(1)} %pad_add_fusion.spot_ref, f32[16,640,128]{2,1,0:T(8,128)S(1)} %get-tuple-element.88.pre_ref, f32[16,16,128]{2,1,0:T(8,128)S(1)} %get-tuple-element.89.pair_ref, f32[16,2048]{1,0:T(8,128)S(1)} %get-tuple-element.73.rate_ref, ...), custom_call_target="tpu_custom_call" | custom-call | flops 67108864 | bytes 8388608 | tf_op jit(solution)/shard_map/local_filter/pallas_call | solution.py:456
  28.9 9.4 %collective-permute-done.3.far_ref = f32[16,2048]{1,0:T(8,128)S(1)} collective-permute-done((f32[16,2048]{1,0:T(8,128)S(1)}, f32[16,2048]{1,0:T(8,128)S(1)}, u32[]{:S(2)}, u32[]{:S(2)}) %collective-permute-start.3) | collective-permute-done | bytes 131104 | tf_op jit(solution)/shard_map/ppermute | solution.py:578
  38.3 0.0 collective-permute-done.4.near_ref
  38.3 2.6 %collective-permute-start.5 = (f32[16,2048]{1,0:T(8,128)S(1)}, f32[16,2048]{1,0:T(8,128)S(1)}, u32[]{:S(2)}, u32[]{:S(2)}) collective-permute-start(f32[16,2048]{1,0:T(8,128)S(1)} %get-tuple-element.95), channel_id=1, source_target_pairs={{0,16},{16,0},{32,48},{48,32},{64,80},{80,64},{96,112},{112,96},{1... | collective-permute-start | bytes 393224 | tf_op jit(solution)/shard_map/ppermute | solution.py:592
  40.9 1.0 %collective-permute-done.5.handed_ref = f32[16,2048]{1,0:T(8,128)S(1)} collective-permute-done((f32[16,2048]{1,0:T(8,128)S(1)}, f32[16,2048]{1,0:T(8,128)S(1)}, u32[]{:S(2)}, u32[]{:S(2)}) %collective-permute-start.5) | collective-permute-done | bytes 131104 | tf_op jit(solution)/shard_map/ppermute | solution.py:592
  41.9 6.8 %filter_gradients.1 = (bf16[128,2048]{1,0:T(8,128)(2,1)}, f32[16,384,128]{2,1,0:T(8,128)S(1)}, f32[24,2048]{1,0:T(8,128)S(1)}, f32[8,40,128]{2,1,0:T(8,128)S(1)}, f32[8,40,128]{2,1,0:T(8,128)S(1)}) custom-call(s32[10]{0:T(128)S(1)} %pad_add_fusion.spot_ref, f32[16,512,128]{2,1,0:T(8,128)S(1)} %get-tuple-element.67.raw_ref, ...), custom_call_target="tpu_custom_call" | custom-call | flops 67108864 | bytes 8388608 | tf_op jit(solution)/shard_map/filter_gradients/pallas_call | solution.py:456
  48.7 0.4 collective-permute-start.6
  49.2 1.0 %collective-permute-done.6 = f32[8,40,128]{2,1,0:T(8,128)S(1)} collective-permute-done((f32[8,40,128]{2,1,0:T(8,128)S(1)}, f32[8,40,128]{2,1,0:T(8,128)S(1)}, u32[]{:S(2)}, u32[]{:S(2)}) %collective-permute-start.6) | collective-permute-done | bytes 163872 | tf_op jit(solution)/shard_map/ppermute | solution.py:600
  50.3 2.3 %collective-permute-start.10 = (f32[24,2048]{1,0:T(8,128)S(1)}, f32[24,2048]{1,0:T(8,128)S(1)}, u32[]{:S(2)}, u32[]{:S(2)}) collective-permute-start(f32[24,2048]{1,0:T(8,128)S(1)} %get-tuple-element.101), channel_id=1, source_target_pairs={{16,0},{32,16},{48,32},{64,48},{80,64},{96,80},{112,96},{128,112},... | collective-permute-start | bytes 589832 | tf_op jit(solution)/shard_map/ppermute | solution.py:617
  52.5 1.4 %collective-permute-start.7 = (f32[2,40,128]{2,1,0:T(8,128)S(1)}, f32[2,40,128]{2,1,0:T(8,128)S(1)}, u32[]{:S(2)}, u32[]{:S(2)}) collective-permute-start(f32[2,40,128]{2,1,0:T(8,128)S(1)} %get-tuple-element.100), channel_id=1, source_target_pairs={{0,1},{1,0},{2,3},{3,2},{4,5},{5,4},{6,7},{7,6},{8,9},{9,8},{10,11... | collective-permute-start | bytes 122888 | tf_op jit(solution)/shard_map/ppermute | solution.py:600
  53.9 1.9 %collective-permute-start.9 = (f32[2,40,128]{2,1,0:T(8,128)S(1)}, f32[2,40,128]{2,1,0:T(8,128)S(1)}, u32[]{:S(2)}, u32[]{:S(2)}) collective-permute-start(f32[2,40,128]{2,1,0:T(8,128)S(1)} %get-tuple-element.127), channel_id=1, source_target_pairs={{0,3},{1,2},{2,1},{3,0},{4,7},{5,6},{6,5},{7,4},{8,11},{9,10},{10,... | collective-permute-start | bytes 122888 | tf_op jit(solution)/shard_map/ppermute | solution.py:600
  55.8 0.7 collective-permute-start.8
  56.5 0.0 collective-permute-done.7
  56.5 2.0 %collective-permute-done.9 = f32[2,40,128]{2,1,0:T(8,128)S(1)} collective-permute-done((f32[2,40,128]{2,1,0:T(8,128)S(1)}, f32[2,40,128]{2,1,0:T(8,128)S(1)}, u32[]{:S(2)}, u32[]{:S(2)}) %collective-permute-start.9) | collective-permute-done | bytes 40992 | tf_op jit(solution)/shard_map/ppermute | solution.py:600
  58.6 2.0 %collective-permute-done.8 = f32[2,40,128]{2,1,0:T(8,128)S(1)} collective-permute-done((f32[2,40,128]{2,1,0:T(8,128)S(1)}, f32[2,40,128]{2,1,0:T(8,128)S(1)}, u32[]{:S(2)}, u32[]{:S(2)}) %collective-permute-start.8) | collective-permute-done | bytes 40992 | tf_op jit(solution)/shard_map/ppermute | solution.py:600
  60.6 0.0 collective-permute-done.10.edge_ref
  60.6 1.8 %collective-permute-start.11 = (f32[2,40,128]{2,1,0:T(8,128)S(1)}, f32[2,40,128]{2,1,0:T(8,128)S(1)}, u32[]{:S(2)}, u32[]{:S(2)}) collective-permute-start(f32[2,40,128]{2,1,0:T(8,128)S(1)} %fusion), channel_id=1, source_target_pairs={{0,32},{16,48},{32,0},{48,16},{64,96},{80,112},{96,64},{112,80},{1... | collective-permute-start | bytes 122888 | tf_op jit(solution)/shard_map/ppermute | solution.py:600
  62.4 1.4 %collective-permute-done.11 = f32[2,40,128]{2,1,0:T(8,128)S(1)} collective-permute-done((f32[2,40,128]{2,1,0:T(8,128)S(1)}, f32[2,40,128]{2,1,0:T(8,128)S(1)}, u32[]{:S(2)}, u32[]{:S(2)}) %collective-permute-start.11) | collective-permute-done | bytes 40992 | tf_op jit(solution)/shard_map/ppermute | solution.py:600
  63.8 1.4 %collective-permute-start.12 = (f32[2,40,128]{2,1,0:T(8,128)S(1)}, f32[2,40,128]{2,1,0:T(8,128)S(1)}, u32[]{:S(2)}, u32[]{:S(2)}) collective-permute-start(f32[2,40,128]{2,1,0:T(8,128)S(1)} %add.28), channel_id=1, source_target_pairs={{0,64},{16,80},{32,96},{48,112},{64,0},{80,16},{96,32},{112,48},{1... | collective-permute-start | bytes 122888 | tf_op jit(solution)/shard_map/ppermute | solution.py:600
  65.3 2.2 %collective-permute-start.13 = (f32[2,40,128]{2,1,0:T(8,128)S(1)}, f32[2,40,128]{2,1,0:T(8,128)S(1)}, u32[]{:S(2)}, u32[]{:S(2)}) collective-permute-start(f32[2,40,128]{2,1,0:T(8,128)S(1)} %add.28), channel_id=1, source_target_pairs={{0,128},{16,144},{32,160},{48,176},{64,192},{80,208},{96,224},{112... | collective-permute-start | bytes 122888 | tf_op jit(solution)/shard_map/ppermute | solution.py:600
  67.5 2.0 %collective-permute-start.14 = (f32[2,40,128]{2,1,0:T(8,128)S(1)}, f32[2,40,128]{2,1,0:T(8,128)S(1)}, u32[]{:S(2)}, u32[]{:S(2)}) collective-permute-start(f32[2,40,128]{2,1,0:T(8,128)S(1)} %add.28), channel_id=1, source_target_pairs={{0,192},{16,208},{32,224},{48,240},{64,128},{80,144},{96,160},{112... | collective-permute-start | bytes 122888 | tf_op jit(solution)/shard_map/ppermute | solution.py:600
  69.5 1.8 %input_gradient.4 = bf16[128,2048]{1,0:T(8,128)(2,1)} custom-call(f32[16,384,128]{2,1,0:T(8,128)S(1)} %get-tuple-element.109.gfeat_ref, f32[24,2048]{1,0:T(8,128)S(1)} %collective-permute-done.10.edge_ref, f32[3,7,2048]{2,1,0:T(8,128)S(1)} %get-tuple-element.72.taps_ref, f32[6,22,8,128]{3,2,1,0:T(8,128)S(1)} %get-tuple-element.68.masks), custom_call_target="tpu_custom_call" | custom-call | flops 67108864 | bytes 8388608 | tf_op jit(solution)/shard_map/input_gradient/pallas_call | solution.py:456
  71.3 1.8 %input_gradient.3 = bf16[128,2048]{1,0:T(8,128)(2,1)} custom-call(f32[16,384,128]{2,1,0:T(8,128)S(1)} %get-tuple-element.109.gfeat_ref, f32[24,2048]{1,0:T(8,128)S(1)} %collective-permute-done.10.edge_ref, f32[3,7,2048]{2,1,0:T(8,128)S(1)} %get-tuple-element.72.taps_ref, f32[6,22,8,128]{3,2,1,0:T(8,128)S(1)} %get-tuple-element.68.masks), custom_call_target="tpu_custom_call" | custom-call | flops 67108864 | bytes 8388608 | tf_op jit(solution)/shard_map/input_gradient/pallas_call | solution.py:456
  73.1 0.0 collective-permute-done.12
  73.2 0.0 collective-permute-done.13
  73.2 0.0 collective-permute-done.14
  73.2 0.5 collective-permute-start.15
  73.7 1.7 %collective-permute-start.16 = (f32[2,40,128]{2,1,0:T(8,128)S(1)}, f32[2,40,128]{2,1,0:T(8,128)S(1)}, u32[]{:S(2)}, u32[]{:S(2)}) collective-permute-start(f32[2,40,128]{2,1,0:T(8,128)S(1)} %add_add_fusion), channel_id=1, source_target_pairs={{0,2},{1,3},{2,0},{3,1},{4,6},{5,7},{6,4},{7,5},{8,10},{9,11},{10,... | collective-permute-start | bytes 122888 | tf_op jit(solution)/shard_map/ppermute | solution.py:600
  75.3 1.8 %collective-permute-start.17 = (f32[2,40,128]{2,1,0:T(8,128)S(1)}, f32[2,40,128]{2,1,0:T(8,128)S(1)}, u32[]{:S(2)}, u32[]{:S(2)}) collective-permute-start(f32[2,40,128]{2,1,0:T(8,128)S(1)} %add_add_fusion), channel_id=1, source_target_pairs={{0,3},{1,2},{2,1},{3,0},{4,7},{5,6},{6,5},{7,4},{8,11},{9,10},{10,... | collective-permute-start | bytes 122888 | tf_op jit(solution)/shard_map/ppermute | solution.py:600
  77.1 1.8 %input_gradient.5 = bf16[128,2048]{1,0:T(8,128)(2,1)} custom-call(f32[16,384,128]{2,1,0:T(8,128)S(1)} %get-tuple-element.109.gfeat_ref, f32[24,2048]{1,0:T(8,128)S(1)} %collective-permute-done.10.edge_ref, f32[3,7,2048]{2,1,0:T(8,128)S(1)} %get-tuple-element.72.taps_ref, f32[6,22,8,128]{3,2,1,0:T(8,128)S(1)} %get-tuple-element.68.masks), custom_call_target="tpu_custom_call" | custom-call | flops 67108864 | bytes 8388608 | tf_op jit(solution)/shard_map/input_gradient/pallas_call | solution.py:456
  78.9 0.0 collective-permute-done.15
  79.0 0.0 collective-permute-done.16
  79.0 0.4 collective-permute-done.17
  79.4 7.0 %collective-permute-start.18 = (f32[8,40,128]{2,1,0:T(8,128)S(1)}, f32[8,40,128]{2,1,0:T(8,128)S(1)}, u32[]{:S(2)}, u32[]{:S(2)}) collective-permute-start(f32[8,40,128]{2,1,0:T(8,128)S(1)} %pad_maximum_fusion.kept_ref), channel_id=1, source_target_pairs={{0,16},{16,0},{32,48},{48,32},{64,80},{80,64},{96,112},{112,96},{1... | collective-permute-start | bytes 491528 | tf_op jit(solution)/shard_map/ppermute | solution.py:600
  86.4 1.0 %collective-permute-done.18.away_ref = f32[8,40,128]{2,1,0:T(8,128)S(1)} collective-permute-done((f32[8,40,128]{2,1,0:T(8,128)S(1)}, f32[8,40,128]{2,1,0:T(8,128)S(1)}, u32[]{:S(2)}, u32[]{:S(2)}) %collective-permute-start.18) | collective-permute-done | bytes 163872 | tf_op jit(solution)/shard_map/ppermute | solution.py:600
  87.4 1.9 %parameter_gradients.1 = (f32[3,7,2048]{2,1,0:T(8,128)}, f32[16,2048]{1,0:T(8,128)}, f32[1,2048]{1,0:T(1,128)}) custom-call(s32[10]{0:T(128)S(1)} %pad_add_fusion.spot_ref, f32[8,40,128]{2,1,0:T(8,128)S(1)} %pad_maximum_fusion.kept_ref, f32[8,40,128]{2,1,0:T(8,128)S(1)} %collective-permute-done.18.away_ref), custom_call_target="tpu_custom_call" | custom-call | flops 67108864 | bytes 8388608 | tf_op jit(solution)/shard_map/parameter_gradients/pallas_call | solution.py:456
  (10 shorter events, 0.2 us)
Async XLA Ops:
  0.6 10.0 %copy-start = (s32[1,8]{1,0:T(1,128)S(1)}, s32[1,8]{1,0:T(1,128)}, u32[]{:S(2)}) copy-start(s32[1,8]{1,0:T(1,128)} %lengths_in.1) | copy-start | bytes 100
  1.7 9.0 %collective-permute-start = (bf16[32,2048]{1,0:T(8,128)(2,1)S(1)}, bf16[32,2048]{1,0:T(8,128)(2,1)S(1)}, u32[]{:S(2)}, u32[]{:S(2)}) collective-permute-start(bf16[32,2048]{1,0:T(8,128)(2,1)S(1)} %last_rows.1), channel_id=1, source_target_pairs={{0,16},{16,32},{32,48},{48,64},{64,80},{80,96},{96,112},{112,128},... | collective-permute-start | bytes 393224 | tf_op jit(solution)/shard_map/ppermute | solution.py:567
  17.2 1.4 %collective-permute-start.1 = (f32[16,2048]{1,0:T(8,128)S(1)}, f32[16,2048]{1,0:T(8,128)S(1)}, u32[]{:S(2)}, u32[]{:S(2)}) collective-permute-start(f32[16,2048]{1,0:T(8,128)S(1)} %get-tuple-element.76.sent_ref), channel_id=1, source_target_pairs={{0,16},{16,0},{32,48},{48,32},{64,80},{80,64},{96,112},{112,96},{1... | collective-permute-start | bytes 393224 | tf_op jit(solution)/shard_map/ppermute | solution.py:580
  18.6 5.9 %collective-permute-start.2 = (f32[16,2048]{1,0:T(8,128)S(1)}, f32[16,2048]{1,0:T(8,128)S(1)}, u32[]{:S(2)}, u32[]{:S(2)}) collective-permute-start(f32[16,2048]{1,0:T(8,128)S(1)} %combine.2.first_ref), channel_id=1, source_target_pairs={{0,32},{32,64},{48,16},{64,96},{80,48},{96,128},{112,80},{128,160}... | collective-permute-start | bytes 393224 | tf_op jit(solution)/shard_map/ppermute | solution.py:578
  24.6 13.7 %collective-permute-start.3 = (f32[16,2048]{1,0:T(8,128)S(1)}, f32[16,2048]{1,0:T(8,128)S(1)}, u32[]{:S(2)}, u32[]{:S(2)}) collective-permute-start(f32[16,2048]{1,0:T(8,128)S(1)} %combine.3), channel_id=1, source_target_pairs={{0,96},{32,128},{64,160},{96,192},{112,16},{128,224},{144,48},{176... | collective-permute-start | bytes 393224 | tf_op jit(solution)/shard_map/ppermute | solution.py:578
  25.9 12.4 %collective-permute-start.4 = (f32[16,2048]{1,0:T(8,128)S(1)}, f32[16,2048]{1,0:T(8,128)S(1)}, u32[]{:S(2)}, u32[]{:S(2)}) collective-permute-start(f32[16,2048]{1,0:T(8,128)S(1)} %combine.3), channel_id=1, source_target_pairs={{0,32},{32,64},{48,16},{64,96},{80,48},{96,128},{112,80},{128,160}... | collective-permute-start | bytes 393224 | tf_op jit(solution)/shard_map/ppermute | solution.py:578
  38.3 3.6 %collective-permute-start.5 = (f32[16,2048]{1,0:T(8,128)S(1)}, f32[16,2048]{1,0:T(8,128)S(1)}, u32[]{:S(2)}, u32[]{:S(2)}) collective-permute-start(f32[16,2048]{1,0:T(8,128)S(1)} %get-tuple-element.95), channel_id=1, source_target_pairs={{0,16},{16,0},{32,48},{48,32},{64,80},{80,64},{96,112},{112,96},{1... | collective-permute-start | bytes 393224 | tf_op jit(solution)/shard_map/ppermute | solution.py:592
  48.7 1.5 %collective-permute-start.6 = (f32[8,40,128]{2,1,0:T(8,128)S(1)}, f32[8,40,128]{2,1,0:T(8,128)S(1)}, u32[]{:S(2)}, u32[]{:S(2)}) collective-permute-start(f32[8,40,128]{2,1,0:T(8,128)S(1)} %get-tuple-element.98), channel_id=1, source_target_pairs={{0,16},{16,0},{32,48},{48,32},{64,80},{80,64},{96,112},{112,96},{1... | collective-permute-start | bytes 491528 | tf_op jit(solution)/shard_map/ppermute | solution.py:600
  50.3 10.3 %collective-permute-start.10 = (f32[24,2048]{1,0:T(8,128)S(1)}, f32[24,2048]{1,0:T(8,128)S(1)}, u32[]{:S(2)}, u32[]{:S(2)}) collective-permute-start(f32[24,2048]{1,0:T(8,128)S(1)} %get-tuple-element.101), channel_id=1, source_target_pairs={{16,0},{32,16},{48,32},{64,48},{80,64},{96,80},{112,96},{128,112},... | collective-permute-start | bytes 589832 | tf_op jit(solution)/shard_map/ppermute | solution.py:617
  52.5 4.0 %collective-permute-start.7 = (f32[2,40,128]{2,1,0:T(8,128)S(1)}, f32[2,40,128]{2,1,0:T(8,128)S(1)}, u32[]{:S(2)}, u32[]{:S(2)}) collective-permute-start(f32[2,40,128]{2,1,0:T(8,128)S(1)} %get-tuple-element.100), channel_id=1, source_target_pairs={{0,1},{1,0},{2,3},{3,2},{4,5},{5,4},{6,7},{7,6},{8,9},{9,8},{10,11... | collective-permute-start | bytes 122888 | tf_op jit(solution)/shard_map/ppermute | solution.py:600
  53.9 4.7 %collective-permute-start.9 = (f32[2,40,128]{2,1,0:T(8,128)S(1)}, f32[2,40,128]{2,1,0:T(8,128)S(1)}, u32[]{:S(2)}, u32[]{:S(2)}) collective-permute-start(f32[2,40,128]{2,1,0:T(8,128)S(1)} %get-tuple-element.127), channel_id=1, source_target_pairs={{0,3},{1,2},{2,1},{3,0},{4,7},{5,6},{6,5},{7,4},{8,11},{9,10},{10,... | collective-permute-start | bytes 122888 | tf_op jit(solution)/shard_map/ppermute | solution.py:600
  55.8 4.8 %collective-permute-start.8 = (f32[2,40,128]{2,1,0:T(8,128)S(1)}, f32[2,40,128]{2,1,0:T(8,128)S(1)}, u32[]{:S(2)}, u32[]{:S(2)}) collective-permute-start(f32[2,40,128]{2,1,0:T(8,128)S(1)} %get-tuple-element.128), channel_id=1, source_target_pairs={{0,2},{1,3},{2,0},{3,1},{4,6},{5,7},{6,4},{7,5},{8,10},{9,11},{10,... | collective-permute-start | bytes 122888 | tf_op jit(solution)/shard_map/ppermute | solution.py:600
  60.6 3.2 %collective-permute-start.11 = (f32[2,40,128]{2,1,0:T(8,128)S(1)}, f32[2,40,128]{2,1,0:T(8,128)S(1)}, u32[]{:S(2)}, u32[]{:S(2)}) collective-permute-start(f32[2,40,128]{2,1,0:T(8,128)S(1)} %fusion), channel_id=1, source_target_pairs={{0,32},{16,48},{32,0},{48,16},{64,96},{80,112},{96,64},{112,80},{1... | collective-permute-start | bytes 122888 | tf_op jit(solution)/shard_map/ppermute | solution.py:600
  63.8 9.3 %collective-permute-start.12 = (f32[2,40,128]{2,1,0:T(8,128)S(1)}, f32[2,40,128]{2,1,0:T(8,128)S(1)}, u32[]{:S(2)}, u32[]{:S(2)}) collective-permute-start(f32[2,40,128]{2,1,0:T(8,128)S(1)} %add.28), channel_id=1, source_target_pairs={{0,64},{16,80},{32,96},{48,112},{64,0},{80,16},{96,32},{112,48},{1... | collective-permute-start | bytes 122888 | tf_op jit(solution)/shard_map/ppermute | solution.py:600
  65.3 7.9 %collective-permute-start.13 = (f32[2,40,128]{2,1,0:T(8,128)S(1)}, f32[2,40,128]{2,1,0:T(8,128)S(1)}, u32[]{:S(2)}, u32[]{:S(2)}) collective-permute-start(f32[2,40,128]{2,1,0:T(8,128)S(1)} %add.28), channel_id=1, source_target_pairs={{0,128},{16,144},{32,160},{48,176},{64,192},{80,208},{96,224},{112... | collective-permute-start | bytes 122888 | tf_op jit(solution)/shard_map/ppermute | solution.py:600
  67.5 5.6 %collective-permute-start.14 = (f32[2,40,128]{2,1,0:T(8,128)S(1)}, f32[2,40,128]{2,1,0:T(8,128)S(1)}, u32[]{:S(2)}, u32[]{:S(2)}) collective-permute-start(f32[2,40,128]{2,1,0:T(8,128)S(1)} %add.28), channel_id=1, source_target_pairs={{0,192},{16,208},{32,224},{48,240},{64,128},{80,144},{96,160},{112... | collective-permute-start | bytes 122888 | tf_op jit(solution)/shard_map/ppermute | solution.py:600
  73.2 5.8 %collective-permute-start.15 = (f32[2,40,128]{2,1,0:T(8,128)S(1)}, f32[2,40,128]{2,1,0:T(8,128)S(1)}, u32[]{:S(2)}, u32[]{:S(2)}) collective-permute-start(f32[2,40,128]{2,1,0:T(8,128)S(1)} %add_add_fusion), channel_id=1, source_target_pairs={{0,1},{1,0},{2,3},{3,2},{4,5},{5,4},{6,7},{7,6},{8,9},{9,8},{10,11... | collective-permute-start | bytes 122888 | tf_op jit(solution)/shard_map/ppermute | solution.py:600
  73.7 5.3 %collective-permute-start.16 = (f32[2,40,128]{2,1,0:T(8,128)S(1)}, f32[2,40,128]{2,1,0:T(8,128)S(1)}, u32[]{:S(2)}, u32[]{:S(2)}) collective-permute-start(f32[2,40,128]{2,1,0:T(8,128)S(1)} %add_add_fusion), channel_id=1, source_target_pairs={{0,2},{1,3},{2,0},{3,1},{4,6},{5,7},{6,4},{7,5},{8,10},{9,11},{10,... | collective-permute-start | bytes 122888 | tf_op jit(solution)/shard_map/ppermute | solution.py:600
  75.3 4.1 %collective-permute-start.17 = (f32[2,40,128]{2,1,0:T(8,128)S(1)}, f32[2,40,128]{2,1,0:T(8,128)S(1)}, u32[]{:S(2)}, u32[]{:S(2)}) collective-permute-start(f32[2,40,128]{2,1,0:T(8,128)S(1)} %add_add_fusion), channel_id=1, source_target_pairs={{0,3},{1,2},{2,1},{3,0},{4,7},{5,6},{6,5},{7,4},{8,11},{9,10},{10,... | collective-permute-start | bytes 122888 | tf_op jit(solution)/shard_map/ppermute | solution.py:600
  79.4 8.0 %collective-permute-start.18 = (f32[8,40,128]{2,1,0:T(8,128)S(1)}, f32[8,40,128]{2,1,0:T(8,128)S(1)}, u32[]{:S(2)}, u32[]{:S(2)}) collective-permute-start(f32[8,40,128]{2,1,0:T(8,128)S(1)} %pad_maximum_fusion.kept_ref), channel_id=1, source_target_pairs={{0,16},{16,0},{32,48},{48,32},{64,80},{80,64},{96,112},{112,96},{1... | collective-permute-start | bytes 491528 | tf_op jit(solution)/shard_map/ppermute | solution.py:600
